TPU v7x, 32 devices: a whole 2x2x4 slice. The times are simulated.
32 devices in a mesh: slab: 8 (over y, x, core), orb: 4 (over z).
Axes of the slice: x: 2, y: 2, z: 4, core: 2. Of those that a mesh axis runs over, the one named last changes fastest.
Arguments:
- orbitals: float32 [256, 64, 4096], P('orb', 'slab'), may hold values from -6 to 6
- pair_list: int32 [32, 2], P(('slab', 'orb')), may hold values from 0 to 255, as said below
- box_start: int32 [32, 3], P(('slab', 'orb')), may hold values from 0 to 63
Outputs:
- exchange_action: float32 [256, 64, 4096], P('orb', 'slab')
Inputs may be any that keep to these rules, and one draw needn't show every extreme that they name: `pair_list`: the two orbitals of a row differ.
All inputs are finite; a program needn't handle non-finite values.
Results may differ from a plain program's by a relative error of at most 0.0003.
Values sent between devices are 32-bit elements; how exact they have to be, the bound alone decides.
No kernel may reach another device: no remote copies, remote signals or barrier semaphores. Data moves between devices by JAX's collectives and lax.ppermute only.
A program may use at most 192 MiB of HBM per device.

v0:
```python
import jax
import jax.numpy as jnp
from jax import lax
from jax.sharding import PartitionSpec as P

NX = 64
NY = 64
NZ = 64
ITERS = 16


screening = 0.02
center_eig = 6.0 + screening
half_width = 6.0
sigma_one = center_eig / half_width


def operate(field):
    cells = field.shape[2]
    z_index = jnp.arange(cells, dtype=jnp.int32) % NZ
    beside = jnp.roll(field, 1, 1) + jnp.roll(field, -1, 1)
    beside = beside + jnp.roll(field, NZ, 2) + jnp.roll(field, -NZ, 2)
    upper = jnp.where(z_index == NZ - 1, jnp.roll(field, NZ - 1, 2), jnp.roll(field, -1, 2))
    lower = jnp.where(z_index == 0, jnp.roll(field, 1 - NZ, 2), jnp.roll(field, 1, 2))
    return center_eig * field - (beside + upper + lower)


def solve_screened(density):

    def sweep(step_index, state_now):
        solution, residue, update, ratio = state_now
        solution = solution + update
        residue = residue - operate(update)
        ratio_next = 1.0 / (2.0 * sigma_one - ratio)
        update = ratio_next * ratio * update + 2.0 * ratio_next / half_width * residue
        return (solution, residue, update, ratio_next)

    start_state = (
        jnp.zeros_like(density),
        density,
        density / center_eig,
        jnp.asarray(1.0 / sigma_one, jnp.float32),
    )
    return lax.fori_loop(0, ITERS, sweep, start_state)[0]


def pair_work(received):
    left = received[:, 0]
    right = received[:, 1]
    potential = solve_screened(left * right)
    return jnp.stack([-potential * right, -potential * left], axis=1)


def roll_cells(rows, shift_y, shift_z):
    grid = rows.reshape(rows.shape[0], NY, NZ)
    grid = jnp.roll(grid, shift_y, 1)
    grid = jnp.roll(grid, shift_z, 2)
    return grid.reshape(rows.shape[0], NY * NZ)


def cut_box(rows, shift_y, shift_z):
    moved = roll_cells(rows, -shift_y, -shift_z).reshape(rows.shape[0], NY, NZ)
    return moved[:, : NY // 2, : NZ // 2].reshape(rows.shape[0], NY // 2 * (NZ // 2))


def place_box(rows, shift_y, shift_z):
    grid = rows.reshape(rows.shape[0], NY // 2, NZ // 2)
    grid = jnp.pad(grid, ((0, 0), (0, NY - NY // 2), (0, NZ - NZ // 2)))
    return roll_cells(grid.reshape(rows.shape[0], NY * NZ), shift_y, shift_z)


def box_mask(starts, slab_at, slab_rows, cells):
    x_cells = slab_at * slab_rows + jnp.arange(slab_rows, dtype=jnp.int32)
    cell_index = jnp.arange(cells, dtype=jnp.int32)
    y_index = cell_index // NZ
    z_index = cell_index % NZ
    inside_x = (x_cells[None, None, :] - starts[:, :, 0:1]) % NX < NX // 2
    inside_y = (y_index[None, None, :] - starts[:, :, 1:2]) % NY < NY // 2
    inside_z = (z_index[None, None, :] - starts[:, :, 2:3]) % NZ < NZ // 2
    inside = inside_x[:, :, :, None] & (inside_y & inside_z)[:, :, None, :]
    return inside[:, None]


def body(orbitals, pair_list, box_start):
    n_slab = lax.axis_size("slab")
    n_orb = lax.axis_size("orb")
    slab_at = lax.axis_index("slab")
    orb_at = lax.axis_index("orb")
    orb_dev, slab_rows, cells = orbitals.shape
    pair_dev = pair_list.shape[0]
    devices = n_slab * n_orb
    all_pairs, all_boxes = (
        lax.all_gather(pair_list, ("slab", "orb"), axis=0, tiled=True),
        lax.all_gather(box_start, ("slab", "orb"), axis=0, tiled=True),
    )
    pair_grid = all_pairs.reshape(n_slab, n_orb, pair_dev, 2)
    box_grid = all_boxes.reshape(n_slab, n_orb, pair_dev, 3)
    own_y = jnp.broadcast_to(box_start[:, None, 1:2], (pair_dev, 2, 1)).reshape(-1)
    own_z = jnp.broadcast_to(box_start[:, None, 2:3], (pair_dev, 2, 1)).reshape(-1)
    wanted = all_pairs.reshape(devices, pair_dev, 2).transpose(1, 2, 0)
    starts = all_boxes.reshape(devices, pair_dev, 3).transpose(1, 0, 2)
    local_index = wanted - orb_at * orb_dev
    inside = (local_index >= 0) & (local_index < orb_dev)
    pieces = jnp.take(orbitals, jnp.clip(local_index, 0, orb_dev - 1), axis=0)
    keep = inside[:, :, :, None, None] & box_mask(starts, slab_at, slab_rows, cells)
    pieces = jnp.where(keep, pieces, 0.0)
    outgoing = pieces.reshape(pair_dev, 2, devices * slab_rows, cells)
    received = lax.all_to_all(outgoing, ("slab", "orb"), split_axis=2, concat_axis=2, tiled=True)
    count_now = received.shape[0]
    whole_grid = received.reshape(count_now, 2, n_slab, n_orb, slab_rows, cells).sum(axis=3)
    terms = pair_work(whole_grid.reshape(count_now, 2, n_slab * slab_rows, cells))
    full_rows = n_slab * slab_rows
    owners_all = pair_grid.transpose(1, 2, 3, 0).reshape(-1) - orb_at * orb_dev
    cut = jax.vmap(cut_box)(terms.reshape(pair_dev * 2, full_rows, cells), own_y, own_z)
    cut = cut.reshape(pair_dev, 2, full_rows, cut.shape[2])
    returned = lax.all_to_all(cut, "slab", split_axis=2, concat_axis=2, tiled=True)
    collected = lax.all_gather(returned, "orb", axis=0, tiled=True)
    count_all = n_orb * pair_dev * 2 * n_slab
    corners = jnp.broadcast_to(
        box_grid.transpose(1, 2, 0, 3)[:, :, None], (n_orb, pair_dev, 2, n_slab, 3)
    )
    corners = corners.reshape(count_all, 3)
    rows_small = collected.reshape(count_all, slab_rows, collected.shape[3])
    placed = jax.vmap(place_box)(rows_small, corners[:, 1], corners[:, 2])
    one_hot = (jnp.arange(orb_dev, dtype=jnp.int32)[:, None] == owners_all[None, :]).astype(
        jnp.float32
    )
    action = jnp.dot(
        one_hot,
        placed.reshape(count_all, slab_rows * cells),
        precision=lax.Precision.HIGHEST,
        preferred_element_type=jnp.float32,
    )
    return action.reshape(orb_dev, slab_rows, cells)


def solution(mesh):
    return jax.shard_map(
        body,
        mesh=mesh,
        in_specs=(P("orb", "slab", None), P(("slab", "orb"), None), P(("slab", "orb"), None)),
        out_specs=P("orb", "slab", None),
        check_vma=False,
    )
```

profile of v0, /device:TPU:0, one launch (start us, length us, event | category | flops | bytes accessed | tf_op | source)
XLA Modules:
  0.0 713.9 jit_solution(8477646325260732136)
XLA Ops:
  6.5 69.5 %all-gather = s32[32,1,2]{2,1,0:T(1,128)S(1)} all-gather(s32[1,1,2]{2,1,0:T(1,128)} %bitcast.81), channel_id=1, replica_groups=mesh['slab'=8,'orb'=4] {'slab','orb'}, dimensions={0}, use_global_device_ids=true | all-gather | bytes 264 | tf_op jit(solution)/shard_map/all_gather | solution.py:93
  76.1 63.2 %all-gather.1 = s32[32,1,3]{2,1,0:T(1,128)S(1)} all-gather(s32[1,1,3]{2,1,0:T(1,128)} %bitcast.80), channel_id=1, replica_groups=mesh['slab'=8,'orb'=4] {'slab','orb'}, dimensions={0}, use_global_device_ids=true | all-gather | bytes 396 | tf_op jit(solution)/shard_map/all_gather | solution.py:94
  140.1 0.6 fusion.21
  140.6 0.7 bitcast_and_fusion
  141.4 7.9 %gather_fusion = f32[64,8,4096]{2,1,0:T(8,128)} fusion(f32[64,8,4096]{2,1,0:T(8,128)} %param.5, s32[1024]{0:T(1024)S(1)} %pad_clamp_fusion), kind=kCustom, calls=%fused_computation | custom fusion | bytes 16777472 | tf_op jit(solution)/shard_map/jit(_take)/gather | solution.py:104
  149.2 4.3 select_select_fusion
  153.5 9.8 %copy.99 = f32[1,2,256,4096]{3,1,0,2:T(2,128)} copy(f32[1,2,256,4096]{3,2,1,0:T(8,128)S(1)} %select_select_fusion) | data formatting | bytes 16777216 | tf_op jit(solution)/shard_map/jit(_where)/select_n | solution.py:106
  163.4 3.8 all-to-all-start
  167.2 0.5 all-gather.4.cloned.1.call-start
  167.7 0.7 fusion.49
  171.1 177.6 %all-to-all-done = f32[1,2,256,4096]{3,1,0,2:T(2,128)} async-done(((f32[1,2,256,4096]{3,1,0,2:T(2,128)}), f32[1,2,256,4096]{3,1,0,2:T(2,128)}, u32[]{:S(2)}, u32[]{:S(2)}) %all-to-all-start) | async-done | bytes 8388640 | tf_op jit(solution)/shard_map/all_to_all | solution.py:108
  348.7 9.5 %reduce_sum.9 = f32[2,8,8,4096]{3,0,2,1:T(2,128)S(1)} reduce(f32[2,8,4,8,4096]{4,0,3,2,1:T(2,128)} %bitcast.14, f32[]{:T(128)} %constant.192.clone.1), dimensions={2}, to_apply=%region_0.1 | reduce | flops 1572864 | bytes 10485764 | tf_op jit(solution)/shard_map/reduce_sum | solution.py:110
  358.2 2.4 fusion.48
  360.6 1.0 copy-done
  361.5 1.7 broadcast_multiply_fusion
  363.2 54.5 %while.17 = (s32[]{:T(128)}, f32[1,64,4096]{2,1,0:T(8,128)S(1)}, f32[1,64,4096]{2,1,0:T(8,128)S(1)}, f32[1,64,4096]{2,1,0:T(8,128)S(1)}, f32[]{:T(128)}, /*index...) while((s32[]{:T(128)}, f32[1,64,4096]{2,1,0:T(8,128)S(1)}, ...), condition=%wide.region_2.3_spmd.clone, body=%wide.region_1.2_spmd.clone.sunk | while | flops 6062087 | bytes 32522416 | solution.py:44
  365.3 1.5 multiply_add_fusion.2
  367.8 0.4 fusion.62
  368.7 1.5 multiply_add_fusion.2
  372.1 1.5 multiply_add_fusion.2
  374.6 0.4 fusion.62
  375.5 1.5 multiply_add_fusion.2
  378.4 0.4 fusion.59
  378.9 1.5 multiply_add_fusion.2
  382.3 1.5 multiply_add_fusion.2
  385.1 0.4 fusion.59
  385.7 1.5 multiply_add_fusion.2
  389.1 1.5 multiply_add_fusion.2
  392.5 1.5 multiply_add_fusion.2
  395.9 1.5 multiply_add_fusion.2
  399.2 1.5 multiply_add_fusion.2
  402.6 1.5 multiply_add_fusion.2
  406.0 1.5 multiply_add_fusion.2
  409.4 1.5 multiply_add_fusion.2
  412.8 1.5 multiply_add_fusion.2
  416.2 1.5 multiply_add_fusion.2
  417.7 4.6 fusion.16
  422.3 2.0 stack.9
  424.3 2.6 copy.102
  426.9 2.0 stack.10
  428.9 1.2 copy.103
  430.1 5.6 maximum_maximum_fusion
  435.7 6.1 gather_fusion.1
  441.8 6.8 pad_maximum_fusion.2
  448.6 9.6 %copy.104 = f32[2,64,64,128]{2,1,0,3:T(8,128)} copy(f32[2,64,64,128]{3,1,2,0:T(8,128)} %pad_maximum_fusion.2) | data formatting | bytes 8388608 | tf_op jit(solution)/shard_map/vmap(jit(_roll_dynamic))/concatenate | solution.py:57
  458.2 6.1 gather_fusion.2
  464.3 1.7 slice.152
  466.0 0.9 copy.105
  467.0 0.4 copy.106
  467.4 13.6 %all_to_all.10 = f32[1,2,64,1024]{3,1,0,2:T(2,128)S(1)} all-to-all(f32[1,2,64,1024]{3,1,0,2:T(2,128)S(1)} %copy.106), channel_id=1, replica_groups=mesh['slab'=8,'orb'=4] {'slab'}, dimensions={2} | all-to-all | bytes 1048576 | tf_op jit(solution)/shard_map/all_to_all | solution.py:116
  480.9 1.0 copy.107
  482.5 47.0 %all-gather.4.cloned.1.call-done = f32[4,2,64,1024]{3,2,1,0:T(8,128)} async-done(((f32[1,2,64,1024]{3,2,1,0:T(8,128)}), f32[4,2,64,1024]{3,2,1,0:T(8,128)}) %all-gather.4.cloned.1.call-update) | async-done | bytes 2097168 | tf_op jit(solution)/shard_map/all_gather | solution.py:117
  529.6 6.5 reshape_reshape.4
  536.0 11.5 %copy.108 = f32[64,8,32,32]{3,1,0,2:T(8,128)} copy(f32[64,8,32,32]{3,2,1,0:T(8,128)} %reshape_reshape.4) | data formatting | bytes 4194304 | tf_op jit(solution)/shard_map/vmap()/reshape;reshape | solution.py:67
  547.5 11.3 %pad.6 = f32[64,8,64,64]{3,1,0,2:T(8,128)} pad(f32[64,8,32,32]{3,1,0,2:T(8,128)} %copy.108, f32[]{:T(128)} %constant.192.clone.1), padding=0_0x0_0x0_32x0_32 | pad | bytes 10485764 | tf_op jit(solution)/shard_map/vmap(jit(_pad))/pad | solution.py:68
  558.8 24.5 %pad_maximum_fusion = f32[64,8,128,64]{3,1,0,2:T(8,128)} fusion(f32[64,8,64,64]{3,1,0,2:T(8,128)} %pad.6), kind=kLoop, calls=%fused_computation.23 | loop fusion | flops 4194304 | bytes 25165824 | tf_op jit(solution)/shard_map/vmap(jit(_roll_dynamic))/concatenate | solution.py:56
  583.3 13.5 %gather_fusion.3 = f32[64,8,64,64]{3,1,2,0:T(8,128)} fusion(f32[64,8,128,64]{3,1,0,2:T(8,128)} %pad_maximum_fusion, s32[64]{0:T(128)S(1)} %get-tuple-element.90), kind=kCustom, calls=%fused_computation.3 | custom fusion | bytes 16778240 | tf_op jit(solution)/shard_map/vmap(jit(_roll_dynamic))/gather | solution.py:56
  596.8 19.5 %pad_maximum_fusion.1 = f32[64,8,64,128]{3,1,2,0:T(8,128)} fusion(f32[64,8,64,64]{3,1,2,0:T(8,128)} %gather_fusion.3), kind=kLoop, calls=%fused_computation.24 | loop fusion | flops 4194304 | bytes 25165824 | tf_op jit(solution)/shard_map/vmap(jit(_roll_dynamic))/concatenate | solution.py:57
  616.3 31.3 %copy.111 = f32[64,8,64,128]{2,1,0,3:T(8,128)} copy(f32[64,8,64,128]{3,1,2,0:T(8,128)} %pad_maximum_fusion.1) | data formatting | bytes 33554432 | tf_op jit(solution)/shard_map/vmap(jit(_roll_dynamic))/concatenate | solution.py:57
  647.6 13.5 %gather_fusion.4 = f32[64,8,64,64]{2,1,3,0:T(8,128)} fusion(f32[64,8,64,128]{2,1,0,3:T(8,128)} %copy.111, s32[64]{0:T(128)S(1)} %get-tuple-element.89), kind=kCustom, calls=%fused_computation.4 | custom fusion | bytes 16778240 | tf_op jit(solution)/shard_map/vmap(jit(_roll_dynamic))/gather | solution.py:57
  661.1 17.4 %copy.112 = f32[64,8,64,64]{3,2,1,0:T(8,128)} copy(f32[64,8,64,64]{2,1,3,0:T(8,128)} %gather_fusion.4) | data formatting | bytes 16777216 | tf_op jit(solution)/shard_map/vmap(jit(_roll_dynamic))/gather | solution.py:57
  678.6 12.9 %reshape.601 = f32[64,32768]{1,0:T(8,128)} reshape(f32[64,8,64,64]{3,2,1,0:T(8,128)} %copy.112) | data formatting | bytes 16777216 | tf_op jit(solution)/shard_map/reshape;vmap()/reshape | solution.py:130
  691.4 7.2 %fusion.11 = f32[64,8,4096]{2,0,1:T(8,128)S(1)} fusion(f32[8,8,8,4096]{3,2,1,0:T(8,128)} %bitcast.71, s32[64]{0:T(128)S(1)} %sub.137), kind=kOutput, calls=%fused_computation.25 | convolution fusion | flops 1610616832 | bytes 16777472 | tf_op jit(solution)/shard_map/dot_general | solution.py:128
  698.6 8.3 %copy.114 = f32[64,8,4096]{2,1,0:T(8,128)} copy(f32[64,8,4096]{2,0,1:T(8,128)S(1)} %fusion.11) | data formatting | bytes 16777216 | tf_op jit(solution)/shard_map/dot_general | solution.py:128
  (190 shorter events, 29.0 us)
Async XLA Ops:
  163.3 4.4 copy-start.2
  163.4 185.3 %all-to-all-start = ((f32[1,2,256,4096]{3,1,0,2:T(2,128)}), f32[1,2,256,4096]{3,1,0,2:T(2,128)}, u32[]{:S(2)}, u32[]{:S(2)}) async-start(f32[1,2,256,4096]{3,1,0,2:T(2,128)} %copy.99), calls=%async_computation | async-start | bytes 16777216 | tf_op jit(solution)/shard_map/all_to_all | solution.py:108
  167.2 362.4 %all-gather.4.cloned.1.call-start = ((), (), s32[]{:S(2)}) async-start(), calls=%async_computation.2 | async-start | bytes 2621440 | tf_op jit(solution)/shard_map/all_gather | solution.py:117
  360.6 1.0 copy-start
  360.6 2.6 copy-start.1
Sparse Core Ops, SparseCore 0:
  482.0 47.4 all-gather.3
where the time goes:
time: 720 us; the launch traced here: 714 us
  waiting for transfers between devices  225 us (31%)
  local copies, waits for them, and re-layouts  206 us (29%)
  blocking collectives  146 us (20%)
  other arithmetic  107 us (15%)
  between operations  16.5 us (2%)
    all_to_all x1, waiting for transfers between devices, body(): lax.all_to_all(outgoing, ('slab', 'orb'), split_axis=2, concat_axis=2, ti...  178 us
    all_gather x1, blocking collectives, body(): lax.all_gather(pair_list, ('slab', 'orb'), axis=0, tiled=True)  69.5 us
    all_gather x1, blocking collectives, body(): lax.all_gather(box_start, ('slab', 'orb'), axis=0, tiled=True)  63.2 us
    all_gather x1, waiting for transfers between devices, body(): collected = lax.all_gather(returned, 'orb', axis=0, tiled=True)  47 us
    concatenate x2, local copies, waits for them, and re-layouts, roll_cells(): grid = jnp.roll(grid, shift_z, 2)  40.9 us
    gather x3, local copies, waits for them, and re-layouts, roll_cells(): grid = jnp.roll(grid, shift_z, 2)  37.1 us
    concatenate x2, other arithmetic, roll_cells(): grid = jnp.roll(grid, shift_y, 1)  30.1 us
    concatenate x2, other arithmetic, roll_cells(): grid = jnp.roll(grid, shift_z, 2)  26.2 us
  transfers between devices with their start and end apart: 2, of which 2 were waited for; matrix products, arithmetic and copies ran while one was open for 0% of the time, Pallas kernels for 0%

commit v1 on v0

v1 whole, which is shorter than its diff:
```python
import functools

import jax
import jax.numpy as jnp
import numpy as np
from jax import lax
from jax.experimental import pallas as pl
from jax.experimental.pallas import tpu as pltpu
from jax.sharding import PartitionSpec as P

NY = 64
NZ = 64
ITERS = 16
HALF = 32
FULL = 64
PACKED = HALF * HALF
MODES = 48
MARGIN = (MODES - HALF) // 2
PERIOD = 2 * (MODES + 1)
LANES = 128
FIELDS = 8
VMEM_LIMIT = 56 * 1024 * 1024

screening = 0.02
center_eig = 6.0 + screening
half_width = 6.0
sigma_one = center_eig / half_width


def spectrum():
    cosine = np.cos(np.pi * (np.arange(MODES) + 1) / (MODES + 1))
    lam = center_eig - 2.0 * (
        cosine[:, None, None] + cosine[None, :, None] + cosine[None, None, :]
    )
    solution_now, residue, ratio = np.zeros_like(lam), np.ones_like(lam), 1.0 / sigma_one
    update = residue / center_eig
    for _ in range(ITERS):
        solution_now = solution_now + update
        residue = residue - lam * update
        ratio_next = 1.0 / (2.0 * sigma_one - ratio)
        update = ratio_next * ratio * update + 2.0 * ratio_next / half_width * residue
        ratio = ratio_next
    table = -solution_now * (2.0 / (MODES + 1)) ** 3
    table = np.pad(table, ((0, 0), (0, 0), (0, LANES // 2 - MODES)))
    table = table.reshape(MODES // 16, 2, 8, MODES, LANES // 2).transpose(3, 2, 0, 1, 4)
    return table.reshape(MODES * 8, MODES // 16 * LANES).astype(np.float32)


def sine(mode, cell, start):
    place = (cell - start) & (HALF - 1)
    phase = ((mode + 1) * (place + MARGIN + 1)) % PERIOD
    return jnp.sin(phase.astype(jnp.float32) * np.float32(np.pi / (MODES + 1)))


def split(full):
    high = full.astype(jnp.bfloat16)
    return high, (full - high.astype(jnp.float32)).astype(jnp.bfloat16)


def halves(full):
    high = lax.reduce_precision(full, 8, 7)
    return high.astype(jnp.bfloat16), (full - high).astype(jnp.bfloat16)


def iotas(shape):
    return [lax.broadcasted_iota(jnp.int32, shape, d) for d in range(len(shape))]


def cell_y(q, g):
    return 2 * q + (g >> 1) + HALF // 2 * (g & 1)


def matrices(box_start):
    count = box_start.shape[0]
    bx, by, bz = (box_start[:, d][:, None, None] for d in range(3))

    def x_of(k, r):
        return sine(k, r, bx)

    def y_of(row, col):
        g, q = col >> 6, (col >> 3) & 7
        return jnp.where((row & 7) == (col & 7), sine(row >> 3, cell_y(q, g), by), 0.0)

    def z_of(row, col):
        same = ((row >> 7) == ((col >> 6) & 1)) & (((row >> 5) & 3) == (col >> 7))
        kz = col & 63
        return jnp.where(same & (kz < MODES), sine(kz, row & 31, bz), 0.0)

    out = []
    for of, rows, cols in ((x_of, MODES, HALF), (z_of, 256, 512), (y_of, MODES * 8, 256)):
        _, row, col = iotas((count, rows, cols))
        out += halves(of(row, col))
        _, row, col = iotas((count, cols, rows))
        out += halves(of(col, row))
    return out


def lane(shape):
    return lax.broadcasted_iota(jnp.int32, shape, len(shape) - 1)


def in_box(cell, start):
    return ((cell - start) & (FULL - 1)) < HALF


def fold(full, start_y, start_z):
    rows = full.shape[0]
    at = lane((rows, LANES))
    upper = (at >> 6) & 1
    in_z = in_box(at & 31, start_z)
    first = (at & 63) < 32
    picked = []
    for v in range(HALF // 2):
        low = full[:, v * LANES : (v + 1) * LANES]
        high = full[:, (v + HALF // 2) * LANES : (v + HALF // 2 + 1) * LANES]
        picked.append(jnp.where(in_box(2 * v + upper, start_y), low, high))
    out = []
    for q in range(8):
        a, b = picked[q], picked[q + 8]
        a = jnp.where(in_z, a, pltpu.roll(a, 96, 1))
        b = jnp.where(in_z, pltpu.roll(b, 32, 1), b)
        out.append(jnp.where(first, a, b))
    return out


def unfold(packed, start_y, start_z, row_mask):
    rows = packed.shape[0]
    at = lane((rows, LANES))
    upper = (at >> 6) & 1
    inside = in_box(at & 63, start_z) & row_mask
    first = (at & 63) < 32
    out = [None] * 32
    for v in range(16):
        piece = packed[:, (v % 8) * LANES : (v % 8 + 1) * LANES]
        if v < 8:
            wide = jnp.where(first, piece, pltpu.roll(piece, 32, 1))
        else:
            wide = jnp.where(first, pltpu.roll(piece, 96, 1), piece)
        wide = jnp.where(inside, wide, 0.0)
        in_y = in_box(2 * v + upper, start_y)
        out[v] = jnp.where(in_y, wide, 0.0)
        out[v + 16] = jnp.where(in_y, 0.0, wide)
    return out


class Task:
    def __init__(self, table, place, g, pair_dev, orb_dev, slab_rows):
        row, off = g // pair_dev, (g % pair_dev) * FIELDS
        base = place[1] * orb_dev
        self.left = table[row, off] - base
        self.right = table[row, off + 1] - base
        self.x, self.y, self.z = (table[row, off + 2 + d] for d in range(3))
        first_row = place[0] * slab_rows
        self.first_row = first_row
        self.rows = slab_rows
        self.meets = in_box(first_row, self.x) | in_box(first_row + slab_rows - 1, self.x)
        self.has_left = (self.left >= 0) & (self.left < orb_dev)
        self.has_right = (self.right >= 0) & (self.right < orb_dev)

    def row_mask(self):
        at = lax.broadcasted_iota(jnp.int32, (self.rows, LANES), 0)
        return in_box(at + self.first_row, self.x)


def pack_kernel(pair_dev, table, place, orbitals, out, held, sems):
    orb_dev, slab_rows, _ = orbitals.shape
    pairs = out.shape[0]

    def task_of(g):
        return Task(table, place, g, pair_dev, orb_dev, slab_rows)

    def copy_of(index, slot):
        return pltpu.make_async_copy(orbitals.at[index], held.at[slot], sems.at[slot])

    @pl.loop(0, pairs)
    def _(g):
        t = task_of(g)

        @pl.when(t.has_left & t.meets)
        def _():
            copy_of(t.left, 2 * g).start()

        @pl.when(t.has_right & t.meets)
        def _():
            copy_of(t.right, 2 * g + 1).start()

    @pl.loop(0, pairs)
    def _(g):
        t = task_of(g)

        def put(full):
            mask = t.row_mask()
            for q, piece in enumerate(fold(full, t.y, t.z)):
                out[g, :, q * LANES : (q + 1) * LANES] = jnp.where(mask, piece, 0.0)

        @pl.when(t.has_left & t.meets)
        def _():
            copy_of(t.left, 2 * g).wait()

        @pl.when(t.has_right & t.meets)
        def _():
            copy_of(t.right, 2 * g + 1).wait()

        @pl.when(t.meets & t.has_left & t.has_right)
        def _():
            put(held[2 * g] * held[2 * g + 1])

        @pl.when(t.meets & (t.has_left != t.has_right))
        def _():
            put(held[2 * g + jnp.where(t.has_left, 0, 1)])

        @pl.when(jnp.logical_not(t.meets))
        def _():
            out[g] = jnp.zeros(out.shape[1:], jnp.float32)


def dot3(a, b):
    def dot(left, right):
        return jnp.dot(left, right, preferred_element_type=jnp.float32)

    return dot(a[0], b[0]) + (dot(a[0], b[1]) + dot(a[1], b[0]))


def tile(full, row, col):
    return full[row * 8 : row * 8 + 8, col * LANES : (col + 1) * LANES]


def blocks(rows):
    return jnp.concatenate([jnp.concatenate(r, axis=1) for r in rows], axis=0)


def potential_of(density, x, xt, z, zt, y, yt, weights):
    pairs_x = MODES // 16
    u = dot3(x, split(density))
    u = blocks(
        [[tile(u, 2 * tp + par, q) for par in range(2)] for tp in range(pairs_x) for q in range(8)]
    )
    u = dot3(split(u), z)
    u = blocks(
        [[tile(u, tp * 8 + q, g) for tp in range(pairs_x)] for g in range(4) for q in range(8)]
    )
    u = dot3(y, split(u)) * weights
    u = dot3(yt, split(u))
    u = blocks(
        [[tile(u, g * 8 + q, tp) for g in range(4)] for tp in range(pairs_x) for q in range(8)]
    )
    u = dot3(split(u), zt)
    u = blocks(
        [[tile(u, tp * 8 + q, par) for q in range(8)] for tp in range(pairs_x) for par in range(2)]
    )
    return dot3(xt, split(u))


def solve_kernel(orb_dev, own, received, *refs):
    mats, weights, out, held, back, sems = refs[:12], *refs[12:]
    pair_dev = received.shape[2]
    n_slab, rows = held.shape[1], held.shape[2]
    for i in range(pair_dev):
        plane = [own[i, side] // orb_dev for side in range(2)]
        ins = [
            pltpu.make_async_copy(received.at[:, plane[side], i], held.at[side], sems.at[side])
            for side in range(2)
        ]
        for c in ins:
            c.start()
        for c in ins:
            c.wait()
        half = n_slab // 2
        sides = [
            (held[side, :half] + held[side, half:]).reshape(HALF, PACKED) for side in range(2)
        ]
        together = plane[0] == plane[1]
        density = jnp.where(together, sides[0], sides[0] * sides[1])
        m = [(mats[k][i], mats[k + 1][i]) for k in range(0, 12, 2)]
        potential = potential_of(density, *m, weights[...])
        for side in range(2):
            term = jnp.where(together, potential, potential * sides[1 - side])
            term = term.reshape(half, rows, PACKED)
            back[side, :half] = term
            back[side, half:] = term
        outs = [
            pltpu.make_async_copy(back.at[side], out.at[:, plane[side], i], sems.at[side])
            for side in range(2)
        ]
        outs[0].start()

        @pl.when(jnp.logical_not(together))
        def _():
            outs[1].start()
            outs[1].wait()

        outs[0].wait()


def place_kernel(pair_dev, table, place, orbitals, returned, zeros, out, held, acc, flags, sems):
    del zeros
    orb_dev, slab_rows, _ = orbitals.shape
    pairs = returned.shape[0]

    def task_of(g):
        return Task(table, place, g, pair_dev, orb_dev, slab_rows)

    def both(t):
        return t.meets & t.has_left & t.has_right

    def copy_of(index, slot):
        return pltpu.make_async_copy(orbitals.at[index], held.at[slot], sems.at[slot])

    def copy_out(k):
        return pltpu.make_async_copy(acc.at[k], out.at[k], sems.at[2 * pairs + k])

    @pl.loop(0, orb_dev)
    def _(k):
        flags[k] = 0

    @pl.loop(0, pairs)
    def _(g):
        t = task_of(g)

        @pl.when(both(t))
        def _():
            copy_of(t.left, 2 * g).start()
            copy_of(t.right, 2 * g + 1).start()

    @pl.loop(0, pairs)
    def _(g):
        t = task_of(g)

        def add(k, factor_slot):
            pieces = unfold(returned[g], t.y, t.z, t.row_mask())

            def cols(v):
                return slice(v * LANES, (v + 1) * LANES)

            if factor_slot is not None:
                pieces = [p * held[factor_slot, :, cols(v)] for v, p in enumerate(pieces)]

            @pl.when(flags[k] == 0)
            def _():
                for v, p in enumerate(pieces):
                    acc[k, :, cols(v)] = p

            @pl.when(flags[k] != 0)
            def _():
                for v, p in enumerate(pieces):
                    acc[k, :, cols(v)] += p

            flags[k] = 1

        @pl.when(both(t))
        def _():
            copy_of(t.left, 2 * g).wait()
            copy_of(t.right, 2 * g + 1).wait()
            add(t.left, 2 * g + 1)
            add(t.right, 2 * g)

        @pl.when(t.meets & (t.has_left != t.has_right))
        def _():
            add(jnp.where(t.has_left, t.left, t.right), None)

    @pl.loop(0, orb_dev)
    def _(k):
        @pl.when(flags[k] != 0)
        def _():
            copy_out(k).start()

    @pl.loop(0, orb_dev)
    def _(k):
        @pl.when(flags[k] != 0)
        def _():
            copy_out(k).wait()


def body(orbitals, pair_list, box_start):
    n_slab = lax.axis_size("slab")
    n_orb = lax.axis_size("orb")
    axes = ("slab", "orb")
    orb_dev, slab_rows, cells = orbitals.shape
    pair_dev = pair_list.shape[0]
    devices = n_slab * n_orb
    pairs = devices * pair_dev
    place = jnp.stack([lax.axis_index("slab"), lax.axis_index("orb")]).astype(jnp.int32)

    smem = pl.BlockSpec(memory_space=pltpu.SMEM)
    vmem = pl.BlockSpec(memory_space=pltpu.VMEM)
    hbm = pl.BlockSpec(memory_space=pl.ANY)
    params = pltpu.CompilerParams(vmem_limit_bytes=VMEM_LIMIT)
    slots = (pairs, slab_rows, PACKED)

    own = jnp.pad(jnp.concatenate([pair_list, box_start], axis=1), ((0, 0), (0, FIELDS - 5)))
    row = own.reshape(1, pair_dev * FIELDS)
    row = jnp.pad(row, ((0, 0), (0, -row.shape[1] % LANES)))
    table = lax.all_to_all(
        jnp.broadcast_to(row, (devices, row.shape[1])), axes, split_axis=0, concat_axis=0, tiled=True
    )

    outgoing = pl.pallas_call(
        functools.partial(pack_kernel, pair_dev),
        out_shape=jax.ShapeDtypeStruct(slots, jnp.float32),
        in_specs=[smem, smem, hbm],
        out_specs=vmem,
        scratch_shapes=[
            pltpu.VMEM((2 * pairs, slab_rows, cells), jnp.float32),
            pltpu.SemaphoreType.DMA((2 * pairs,)),
        ],
        compiler_params=params,
        name="pack",
    )(table, place, orbitals)
    received = lax.all_to_all(outgoing, axes, split_axis=0, concat_axis=0, tiled=True)

    mats = matrices(box_start)
    solved = pl.pallas_call(
        functools.partial(solve_kernel, orb_dev),
        out_shape=jax.ShapeDtypeStruct((n_slab, n_orb, pair_dev, slab_rows, PACKED), jnp.float32),
        in_specs=[smem, hbm] + [vmem] * 13,
        out_specs=hbm,
        scratch_shapes=[
            pltpu.VMEM((2, n_slab, slab_rows, PACKED), jnp.float32),
            pltpu.VMEM((2, n_slab, slab_rows, PACKED), jnp.float32),
            pltpu.SemaphoreType.DMA((2,)),
        ],
        compiler_params=params,
        name="solve",
    )(
        pair_list,
        received.reshape(n_slab, n_orb, pair_dev, slab_rows, PACKED),
        *mats,
        jnp.asarray(spectrum()),
    )
    returned = lax.all_to_all(solved.reshape(slots), axes, split_axis=0, concat_axis=0, tiled=True)

    return pl.pallas_call(
        functools.partial(place_kernel, pair_dev),
        out_shape=jax.ShapeDtypeStruct(orbitals.shape, jnp.float32),
        in_specs=[smem, smem, hbm, vmem, hbm],
        out_specs=hbm,
        scratch_shapes=[
            pltpu.VMEM((2 * pairs, slab_rows, cells), jnp.float32),
            pltpu.VMEM(orbitals.shape, jnp.float32),
            pltpu.SMEM((orb_dev,), jnp.int32),
            pltpu.SemaphoreType.DMA((2 * pairs + orb_dev,)),
        ],
        input_output_aliases={4: 0},
        compiler_params=params,
        name="place",
    )(table, place, orbitals, returned, jnp.zeros(orbitals.shape, jnp.float32))


def solution(mesh):
    return jax.shard_map(
        body,
        mesh=mesh,
        in_specs=(P("orb", "slab", None), P(("slab", "orb"), None), P(("slab", "orb"), None)),
        out_specs=P("orb", "slab", None),
        check_vma=False,
    )
```

time: 720 us -> 97.4 us (0.14)
  waiting for transfers between devices: 225 us -> 14.5 us
  local copies, waits for them, and re-layouts: 206 us -> 8.05 us
  blocking collectives: 146 us -> 29.5 us
  other arithmetic: 107 us -> 16.9 us
  Pallas kernels: 0 us -> 17.7 us
  between operations: 16.5 us -> 0.09 us
    all_to_all x1 -> x2, waiting for transfers between devices: 178 us -> 14.5 us  [the longest x1 10 us: body(): lax.all_to_all(outgoing, axes, split_axis=0, concat_axis=0, tiled=True)]
    all_gather x2 -> x0, blocking collectives: 133 us -> none  [the longest x1 69.5 us: body(): lax.all_gather(pair_list, ('slab', 'orb'), axis=0, tiled=True)]
    gather x6 -> x0, local copies, waits for them, and re-layouts: 64.7 us -> none  [the longest x3 37.1 us: roll_cells(): grid = jnp.roll(grid, shift_z, 2)]
    concatenate x4 -> x1, other arithmetic: 56.3 us -> 0.75 us  [body(): jnp.concatenate([pair_list, box_start], axis=1)]
    all_gather x1 -> x0, waiting for transfers between devices: 47 us -> none  [body(): collected = lax.all_gather(returned, 'orb', axis=0, tiled=True)]
    concatenate x2 -> x0, local copies, waits for them, and re-layouts: 40.9 us -> none  [roll_cells(): grid = jnp.roll(grid, shift_z, 2)]
    slice x132 -> x1, local copies, waits for them, and re-layouts: 29.2 us -> 1.43 us  [matrices(): bx, by, bz = (box_start[:, d][:, None, None] for d in range(3))]
    add x33 -> x4, other arithmetic: 29 us -> 1.26 us  [sine(): phase = (mode + 1) * (place + MARGIN + 1) % PERIOD]
  transfers between devices with their start and end apart: 2 -> 2, of which waited for: 2 -> 2; matrix products, arithmetic and copies ran while one was open for 0% -> 18% of each run, Pallas kernels for 0% -> 0%
where the time goes in v1:
time: 97.4 us; the launch traced here: 96.7 us
  blocking collectives  29.5 us (30%)
  Pallas kernels  17.7 us (18%)
  other arithmetic  16.9 us (17%)
  waiting for transfers between devices  14.5 us (15%)
  starting transfers between devices  9.96 us (10%)
  local copies, waits for them, and re-layouts  8.05 us (8%)
    all_to_all x1, blocking collectives, body(): lax.all_to_all(solved.reshape(slots), axes, split_axis=0, concat_axis=0,...  29.5 us
    convert_element_type x6, other arithmetic, halves(): return (high.astype(jnp.bfloat16), (full - high).astype(jnp.bfloat16))  14.2 us
    all_to_all x1, waiting for transfers between devices, body(): lax.all_to_all(outgoing, axes, split_axis=0, concat_axis=0, tiled=True)  10 us
    all_to_all x1, starting transfers between devices, body(): lax.all_to_all(jnp.broadcast_to(row, (devices, row.shape[1])), axes, spli...  7.3 us
    pallas_call x1, Pallas kernels, body(): pl.pallas_call(functools.partial(place_kernel, pair_dev), out_shape=jax.S...  6.6 us
    pallas_call x1, Pallas kernels, body(): pl.pallas_call(functools.partial(solve_kernel, orb_dev), out_shape=jax.Sh...  5.67 us
    pallas_call x1, Pallas kernels, body(): pl.pallas_call(functools.partial(pack_kernel, pair_dev), out_shape=jax.Sh...  5.39 us
    all_to_all x1, waiting for transfers between devices, body(): lax.all_to_all(jnp.broadcast_to(row, (devices, row.shape[1])), axes, spli...  4.43 us
  transfers between devices with their start and end apart: 2, of which 2 were waited for; matrix products, arithmetic and copies ran while one was open for 18% of the time, Pallas kernels for 0%

profile of v1, /device:TPU:0, one launch (start us, length us, event | category | flops | bytes accessed | tf_op | source)
XLA Modules:
  0.0 96.7 jit_solution(2401298501495313360)
XLA Ops:
  0.0 0.7 pad_add_fusion
  0.8 0.6 broadcast_in_dim.24
  1.4 7.3 %all-to-all-start = ((s32[32,1,128]{2,1,0:T(1,128)}), s32[32,1,128]{2,1,0:T(1,128)S(1)}, u32[]{:S(2)}, u32[]{:S(2)}) async-start(s32[32,1,128]{2,1,0:T(1,128)} %broadcast_in_dim.24), calls=%async_computation | async-start | bytes 32768 | tf_op jit(solution)/shard_map/all_to_all | solution.py:393
  8.7 1.4 %fusion.60 = (s32[1,1]{1,0:T(1,128)}, s32[1,1]{1,0:T(1,128)}, s32[1,1]{1,0:T(1,128)}) fusion(s32[1,3]{1,0:T(1,128)} %param.6), kind=kLoop, calls=%fused_computation.99 | loop fusion | bytes 24 | tf_op jit(solution)/shard_map/slice | solution.py:75
  10.1 0.6 and_add_fusion
  10.7 0.7 pad_add_fusion.1.place
  11.3 4.4 %all-to-all-done = s32[32,1,128]{2,1,0:T(1,128)S(1)} async-done(((s32[32,1,128]{2,1,0:T(1,128)}), s32[32,1,128]{2,1,0:T(1,128)S(1)}, u32[]{:S(2)}, u32[]{:S(2)}) %all-to-all-start) | async-done | bytes 16416 | tf_op jit(solution)/shard_map/all_to_all | solution.py:393
  15.8 0.0 copy-start.1
  15.8 0.6 copy-done.1
  16.4 5.4 %pack.1 = f32[32,8,1024]{2,1,0:T(8,128)} custom-call(s32[32,128]{1,0:T(8,128)} %bitcast.12, s32[2]{0:T(128)} %pad_add_fusion.1.place, f32[64,8,4096]{2,1,0:T(8,128)} %orbitals.3), custom_call_target="tpu_custom_call" | custom-call | tf_op jit(solution)/shard_map/pack/pallas_call | solution.py:397
  21.8 2.7 %all-to-all-start.1 = ((f32[32,8,1024]{2,1,0:T(8,128)}), f32[32,8,1024]{2,1,0:T(8,128)S(1)}, u32[]{:S(2)}, u32[]{:S(2)}) async-start(f32[32,8,1024]{2,1,0:T(8,128)} %pack.1), calls=%async_computation.1 | async-start | bytes 2097152 | tf_op jit(solution)/shard_map/all_to_all | solution.py:409
  24.5 0.7 fusion.56
  25.2 1.3 %fusion.39 = (bf16[1,32,48]{2,1,0:T(8,128)(2,1)}, bf16[1,32,48]{2,1,0:T(8,128)(2,1)}) fusion(s32[]{:T(128)} %bitcast.5, s32[48]{0:T(128)S(1)} %iota_add_fusion), kind=kLoop, calls=%fused_computation.62 | loop fusion | flops 24576 | bytes 6340 | tf_op jit(solution)/shard_map/convert_element_type | solution.py:62
  26.5 1.4 %fusion.32 = (bf16[1,48,32]{2,1,0:T(8,128)(2,1)}, bf16[1,48,32]{2,1,0:T(8,128)(2,1)}) fusion(s32[]{:T(128)} %bitcast.5, s32[48]{0:T(128)S(1)} %iota_add_fusion), kind=kLoop, calls=%fused_computation.51 | loop fusion | flops 24576 | bytes 6340 | tf_op jit(solution)/shard_map/convert_element_type | solution.py:62
  28.0 2.5 %fusion.16 = (bf16[1,384,256]{2,1,0:T(8,128)(2,1)}, bf16[1,384,256]{2,1,0:T(8,128)(2,1)}) fusion(s32[256]{0:T(256)S(1)} %get-tuple-element.26, s32[384]{0:T(512)S(1)} %get-tuple-element.24, s32[256]{0:T(256)S(1)} %get-tuple-element.27, s32[384]{0:T(512)S(1)} %get-tuple-element.25), kind=kLoop, calls=%fused_computation.30 | loop fusion | flops 1474560 | bytes 398336 | tf_op jit(solution)/shard_map/convert_element_type | solution.py:62
  30.5 2.5 %fusion.17 = (bf16[1,256,384]{2,1,0:T(8,128)(2,1)}, bf16[1,256,384]{2,1,0:T(8,128)(2,1)}) fusion(s32[256]{0:T(256)S(1)} %get-tuple-element.26, s32[384]{0:T(512)S(1)} %get-tuple-element.24, s32[384]{0:T(512)S(1)} %get-tuple-element.25, s32[256]{0:T(256)S(1)} %get-tuple-element.27), kind=kLoop, calls=%fused_computation.31 | loop fusion | flops 1474560 | bytes 398336 | tf_op jit(solution)/shard_map/convert_element_type | solution.py:62
  33.0 3.1 %fusion = (bf16[1,256,512]{2,1,0:T(8,128)(2,1)}, bf16[1,256,512]{2,1,0:T(8,128)(2,1)}) fusion(s32[256]{0:T(256)S(1)} %and_add_fusion, s32[512]{0:T(512)S(1)} %get-tuple-element.21, pred[512]{0:T(512)(128)(4,1)S(1)} %fusion.47, s32[512]{0:T(512)S(1)} %get-tuple-element.20, s32[256]{0:T(256)S(1)} %get-tuple-element.23, s32[512]{0:T(512)S(1)} %fusion.48, ...), kind=kLoop, calls=%fused_computation.12 | loop fusion | flops 2359296 | bytes 534016 | tf_op jit(solution)/shard_map/convert_element_type | solution.py:62
  36.1 3.3 %fusion.1 = (bf16[1,512,256]{2,1,0:T(8,128)(2,1)}, bf16[1,512,256]{2,1,0:T(8,128)(2,1)}) fusion(s32[256]{0:T(256)S(1)} %and_add_fusion, s32[512]{0:T(512)S(1)} %get-tuple-element.21, pred[512]{0:T(512)(128)(4,1)S(1)} %fusion.47, s32[512]{0:T(512)S(1)} %get-tuple-element.20, s32[256]{0:T(256)S(1)} %get-tuple-element.23, s32[512]{0:T(512)S(1)} %fusion.48, ...), kind=kLoop, calls=%fused_computation.13 | loop fusion | flops 2359296 | bytes 534016 | tf_op jit(solution)/shard_map/convert_element_type | solution.py:62
  39.4 10.0 %all-to-all-done.1 = f32[32,8,1024]{2,1,0:T(8,128)S(1)} async-done(((f32[32,8,1024]{2,1,0:T(8,128)}), f32[32,8,1024]{2,1,0:T(8,128)S(1)}, u32[]{:S(2)}, u32[]{:S(2)}) %all-to-all-start.1) | async-done | bytes 1048608 | tf_op jit(solution)/shard_map/all_to_all | solution.py:409
  49.5 0.0 copy-start
  49.5 1.0 %copy-done = f32[32,8,1024]{2,1,0:T(8,128)} copy-done((f32[32,8,1024]{2,1,0:T(8,128)}, f32[32,8,1024]{2,1,0:T(8,128)S(1)}, u32[]{:S(2)}) %copy-start) | copy-done | bytes 1048600
  50.4 5.7 %solve.1 = f32[8,4,1,8,1024]{4,3,2,1,0:T(8,128)} custom-call(s32[1,2]{1,0:T(1,128)} %own.1, f32[8,4,1,8,1024]{4,3,2,1,0:T(8,128)} %bitcast.10, bf16[1,48,32]{2,1,0:T(8,128)(2,1)} %get-tuple-element.19.refs_0_, bf16[1,48,32]{2,1,0:T(8,128)(2,1)} %get-tuple-element.18.refs_1_, bf16[1,32,48]{2,1,0:T(8,128)(2,1)} %get-tuple-element.17.refs_2_, ...), custom_call_target="tpu_custom_call" | custom-call | tf_op jit(solution)/shard_map/solve/pallas_call | solution.py:412
  56.1 29.5 %all_to_all.18.returned = f32[32,8,1024]{2,1,0:T(8,128)} all-to-all(f32[32,8,1024]{2,1,0:T(8,128)} %bitcast.11), channel_id=1, replica_groups=mesh['slab'=8,'orb'=4] {'slab','orb'}, dimensions={0} | all-to-all | bytes 2097152 | tf_op jit(solution)/shard_map/all_to_all | solution.py:430
  85.6 4.4 %broadcast_in_dim.29.zeros = f32[64,8,4096]{2,1,0:T(8,128)} broadcast(f32[]{:T(128)} %constant.46.clone.1), dimensions={} | broadcast | bytes 8388612 | tf_op jit(solution)/shard_map/broadcast_in_dim | solution.py:446
  90.1 6.6 %place.1 = f32[64,8,4096]{2,1,0:T(8,128)} custom-call(s32[32,128]{1,0:T(8,128)} %bitcast.13, s32[2]{0:T(128)} %pad_add_fusion.1.place, f32[64,8,4096]{2,1,0:T(8,128)} %orbitals.3, f32[32,8,1024]{2,1,0:T(8,128)} %all_to_all.18.returned, f32[64,8,4096]{2,1,0:T(8,128)} %broadcast_in_dim.29.zeros), custom_call_target="tpu_custom_call", output_to_operand_aliasing={{}: (4, {})} | custom-call | tf_op jit(solution)/shard_map/place/pallas_call | solution.py:432
  (7 shorter events, 0.0 us)
Async XLA Ops:
  1.4 14.4 %all-to-all-start = ((s32[32,1,128]{2,1,0:T(1,128)}), s32[32,1,128]{2,1,0:T(1,128)S(1)}, u32[]{:S(2)}, u32[]{:S(2)}) async-start(s32[32,1,128]{2,1,0:T(1,128)} %broadcast_in_dim.24), calls=%async_computation | async-start | bytes 32768 | tf_op jit(solution)/shard_map/all_to_all | solution.py:393
  15.8 0.6 copy-start.1
  21.8 27.7 %all-to-all-start.1 = ((f32[32,8,1024]{2,1,0:T(8,128)}), f32[32,8,1024]{2,1,0:T(8,128)S(1)}, u32[]{:S(2)}, u32[]{:S(2)}) async-start(f32[32,8,1024]{2,1,0:T(8,128)} %pack.1), calls=%async_computation.1 | async-start | bytes 2097152 | tf_op jit(solution)/shard_map/all_to_all | solution.py:409
  49.5 1.0 %copy-start = (f32[32,8,1024]{2,1,0:T(8,128)}, f32[32,8,1024]{2,1,0:T(8,128)S(1)}, u32[]{:S(2)}) copy-start(f32[32,8,1024]{2,1,0:T(8,128)S(1)} %all-to-all-done.1) | copy-start | bytes 3145732

commit v2 on v1

--- a/solution.py
+++ b/solution.py
@@ -19,7 +19,9 @@
 PERIOD = 2 * (MODES + 1)
 LANES = 128
 FIELDS = 8
-VMEM_LIMIT = 56 * 1024 * 1024
+CLEARS = 16
+MIB = 1024 * 1024
+COUNT, ORB, PAIR, SLOT, SECOND, START_X, START_Y, START_Z, BLANK = range(9)
 
 screening = 0.02
 center_eig = 6.0 + screening
@@ -151,67 +153,123 @@
         self.right = table[row, off + 1] - base
         self.x, self.y, self.z = (table[row, off + 2 + d] for d in range(3))
         first_row = place[0] * slab_rows
-        self.first_row = first_row
-        self.rows = slab_rows
         self.meets = in_box(first_row, self.x) | in_box(first_row + slab_rows - 1, self.x)
         self.has_left = (self.left >= 0) & (self.left < orb_dev)
         self.has_right = (self.right >= 0) & (self.right < orb_dev)
 
-    def row_mask(self):
-        at = lax.broadcasted_iota(jnp.int32, (self.rows, LANES), 0)
-        return in_box(at + self.first_row, self.x)
-
-
-def pack_kernel(pair_dev, table, place, orbitals, out, held, sems):
+
+def row_mask(place, rows, start_x):
+    at = lax.broadcasted_iota(jnp.int32, (rows, LANES), 0)
+    return in_box(at + place[0] * rows, start_x)
+
+
+def pack_kernel(pair_dev, table, place, orbitals, out, work, held, packed, slot_of, sems, out_sems):
     orb_dev, slab_rows, _ = orbitals.shape
     pairs = out.shape[0]
-
-    def task_of(g):
-        return Task(table, place, g, pair_dev, orb_dev, slab_rows)
+    packed[pairs] = jnp.zeros(packed.shape[1:], jnp.float32)
 
     def copy_of(index, slot):
         return pltpu.make_async_copy(orbitals.at[index], held.at[slot], sems.at[slot])
 
-    @pl.loop(0, pairs)
-    def _(g):
-        t = task_of(g)
-
-        @pl.when(t.has_left & t.meets)
-        def _():
-            copy_of(t.left, 2 * g).start()
-
-        @pl.when(t.has_right & t.meets)
-        def _():
-            copy_of(t.right, 2 * g + 1).start()
-
-    @pl.loop(0, pairs)
-    def _(g):
-        t = task_of(g)
+    def send(g, source):
+        return pltpu.make_async_copy(packed.at[source], out.at[g], out_sems.at[g])
+
+    @pl.loop(0, orb_dev)
+    def _(k):
+        slot_of[k] = -1
+
+    def entry(k, orbs):
+        seen = slot_of[k] >= 0
+        slot = jnp.where(seen, slot_of[k], orbs)
+
+        @pl.when(jnp.logical_not(seen))
+        def _():
+            slot_of[k] = orbs
+            work[ORB, orbs] = k
+            copy_of(k, orbs).start()
+
+        return slot, jnp.where(seen, orbs, orbs + 1)
+
+    def scan(g, carry):
+        terms, orbs, blanks = carry
+        t = Task(table, place, g, pair_dev, orb_dev, slab_rows)
+        any_here = t.has_left | t.has_right
+        live = t.meets & any_here
+
+        def listed(_):
+            both = t.has_left & t.has_right
+            a, orbs_a = entry(jnp.where(t.has_left, t.left, t.right), orbs)
+            work[PAIR, terms] = g
+            work[SLOT, terms] = a
+            work[SECOND, terms] = -1
+            work[START_X, terms] = t.x
+            work[START_Y, terms] = t.y
+            work[START_Z, terms] = t.z
+
+            def second(_):
+                b, orbs_b = entry(t.right, orbs_a)
+                work[SECOND, terms] = b
+                return orbs_b
+
+            return terms + 1, lax.cond(both, second, lambda _: orbs_a, 0)
+
+        terms, orbs = lax.cond(live, listed, lambda _: (terms, orbs), 0)
+        blank = any_here & jnp.logical_not(t.meets)
+
+        @pl.when(blank)
+        def _():
+            send(g, pairs).start()
+            work[BLANK, blanks] = g
+
+        return terms, orbs, jnp.where(blank, blanks + 1, blanks)
+
+    terms, orbs, blanks = lax.fori_loop(0, pairs, scan, (0, 0, 0))
+    work[COUNT, 0] = terms
+    work[COUNT, 1] = orbs
+
+    @pl.loop(0, orbs)
+    def _(e):
+        copy_of(work[ORB, e], e).wait()
+
+    @pl.loop(0, terms)
+    def _(i):
+        g, a, b = work[PAIR, i], work[SLOT, i], work[SECOND, i]
 
         def put(full):
-            mask = t.row_mask()
-            for q, piece in enumerate(fold(full, t.y, t.z)):
-                out[g, :, q * LANES : (q + 1) * LANES] = jnp.where(mask, piece, 0.0)
-
-        @pl.when(t.has_left & t.meets)
-        def _():
-            copy_of(t.left, 2 * g).wait()
-
-        @pl.when(t.has_right & t.meets)
-        def _():
-            copy_of(t.right, 2 * g + 1).wait()
-
-        @pl.when(t.meets & t.has_left & t.has_right)
-        def _():
-            put(held[2 * g] * held[2 * g + 1])
-
-        @pl.when(t.meets & (t.has_left != t.has_right))
-        def _():
-            put(held[2 * g + jnp.where(t.has_left, 0, 1)])
-
-        @pl.when(jnp.logical_not(t.meets))
-        def _():
-            out[g] = jnp.zeros(out.shape[1:], jnp.float32)
+            mask = row_mask(place, slab_rows, work[START_X, i])
+            for q, piece in enumerate(fold(full, work[START_Y, i], work[START_Z, i])):
+                packed[g, :, q * LANES : (q + 1) * LANES] = jnp.where(mask, piece, 0.0)
+            send(g, g).start()
+
+        @pl.when(b >= 0)
+        def _():
+            put(held[a] * held[b])
+
+        @pl.when(b < 0)
+        def _():
+            put(held[a])
+
+    @pl.loop(0, terms)
+    def _(i):
+        send(work[PAIR, i], work[PAIR, i]).wait()
+
+    @pl.loop(0, blanks)
+    def _(i):
+        send(work[BLANK, i], pairs).wait()
+
+
+def clear_kernel(work, out, done, blank, sems):
+    done[...] = jnp.full(done.shape, work[COUNT, 0], jnp.int32)
+    count = blank.shape[0]
+    blank[...] = jnp.zeros(blank.shape, jnp.float32)
+    copies = [
+        pltpu.make_async_copy(blank, out.at[c * count : (c + 1) * count], sems.at[c])
+        for c in range(CLEARS)
+    ]
+    for c in copies:
+        c.start()
+    for c in copies:
+        c.wait()
 
 
 def dot3(a, b):
@@ -251,7 +309,8 @@
     return dot3(xt, split(u))
 
 
-def solve_kernel(orb_dev, own, received, *refs):
+def solve_kernel(orb_dev, own, received, cleared, *refs):
+    del cleared
     mats, weights, out, held, back, sems = refs[:12], *refs[12:]
     pair_dev = received.shape[2]
     n_slab, rows = held.shape[1], held.shape[2]
@@ -292,83 +351,63 @@
         outs[0].wait()
 
 
-def place_kernel(pair_dev, table, place, orbitals, returned, zeros, out, held, acc, flags, sems):
+def place_kernel(work, place, orbitals, returned, zeros, out, held, arrived, acc, sems, in_sems):
     del zeros
-    orb_dev, slab_rows, _ = orbitals.shape
-    pairs = returned.shape[0]
-
-    def task_of(g):
-        return Task(table, place, g, pair_dev, orb_dev, slab_rows)
-
-    def both(t):
-        return t.meets & t.has_left & t.has_right
-
-    def copy_of(index, slot):
-        return pltpu.make_async_copy(orbitals.at[index], held.at[slot], sems.at[slot])
-
-    def copy_out(k):
-        return pltpu.make_async_copy(acc.at[k], out.at[k], sems.at[2 * pairs + k])
-
-    @pl.loop(0, orb_dev)
-    def _(k):
-        flags[k] = 0
-
-    @pl.loop(0, pairs)
-    def _(g):
-        t = task_of(g)
-
-        @pl.when(both(t))
-        def _():
-            copy_of(t.left, 2 * g).start()
-            copy_of(t.right, 2 * g + 1).start()
-
-    @pl.loop(0, pairs)
-    def _(g):
-        t = task_of(g)
-
-        def add(k, factor_slot):
-            pieces = unfold(returned[g], t.y, t.z, t.row_mask())
-
-            def cols(v):
-                return slice(v * LANES, (v + 1) * LANES)
-
-            if factor_slot is not None:
-                pieces = [p * held[factor_slot, :, cols(v)] for v, p in enumerate(pieces)]
-
-            @pl.when(flags[k] == 0)
-            def _():
-                for v, p in enumerate(pieces):
-                    acc[k, :, cols(v)] = p
-
-            @pl.when(flags[k] != 0)
-            def _():
-                for v, p in enumerate(pieces):
-                    acc[k, :, cols(v)] += p
-
-            flags[k] = 1
-
-        @pl.when(both(t))
-        def _():
-            copy_of(t.left, 2 * g).wait()
-            copy_of(t.right, 2 * g + 1).wait()
-            add(t.left, 2 * g + 1)
-            add(t.right, 2 * g)
-
-        @pl.when(t.meets & (t.has_left != t.has_right))
-        def _():
-            add(jnp.where(t.has_left, t.left, t.right), None)
-
-    @pl.loop(0, orb_dev)
-    def _(k):
-        @pl.when(flags[k] != 0)
-        def _():
-            copy_out(k).start()
-
-    @pl.loop(0, orb_dev)
-    def _(k):
-        @pl.when(flags[k] != 0)
-        def _():
-            copy_out(k).wait()
+    _, slab_rows, _ = orbitals.shape
+    terms, orbs = work[COUNT, 0], work[COUNT, 1]
+
+    def copy_of(e):
+        return pltpu.make_async_copy(orbitals.at[work[ORB, e]], held.at[e], sems.at[e])
+
+    def copy_out(e):
+        return pltpu.make_async_copy(acc.at[e], out.at[work[ORB, e]], sems.at[e])
+
+    def take(i):
+        g = work[PAIR, i]
+        return pltpu.make_async_copy(returned.at[g], arrived.at[i], in_sems.at[i])
+
+    @pl.loop(0, terms)
+    def _(i):
+        take(i).start()
+
+        @pl.when(work[SECOND, i] >= 0)
+        def _():
+            pair = copy_of(work[SLOT, i]), copy_of(work[SECOND, i])
+            for c in pair:
+                c.start()
+            for c in pair:
+                c.wait()
+
+    @pl.loop(0, orbs)
+    def _(e):
+        acc[e] = jnp.zeros(acc.shape[1:], jnp.float32)
+
+    @pl.loop(0, terms)
+    def _(i):
+        a, b = work[SLOT, i], work[SECOND, i]
+        take(i).wait()
+        mask = row_mask(place, slab_rows, work[START_X, i])
+        pieces = unfold(arrived[i], work[START_Y, i], work[START_Z, i], mask)
+
+        @pl.when(b >= 0)
+        def _():
+            for v, p in enumerate(pieces):
+                cols = slice(v * LANES, (v + 1) * LANES)
+                acc[a, :, cols] += p * held[b, :, cols]
+                acc[b, :, cols] += p * held[a, :, cols]
+
+        @pl.when(b < 0)
+        def _():
+            for v, p in enumerate(pieces):
+                acc[a, :, v * LANES : (v + 1) * LANES] += p
+
+    @pl.loop(0, orbs)
+    def _(e):
+        copy_out(e).start()
+
+    @pl.loop(0, orbs)
+    def _(e):
+        copy_out(e).wait()
 
 
 def body(orbitals, pair_list, box_start):
@@ -383,9 +422,14 @@
 
     smem = pl.BlockSpec(memory_space=pltpu.SMEM)
     vmem = pl.BlockSpec(memory_space=pltpu.VMEM)
-    hbm = pl.BlockSpec(memory_space=pl.ANY)
-    params = pltpu.CompilerParams(vmem_limit_bytes=VMEM_LIMIT)
+    free = pl.BlockSpec(memory_space=pl.ANY)
+    hbm = pl.BlockSpec(memory_space=pltpu.HBM)
     slots = (pairs, slab_rows, PACKED)
+    many = min(2 * pairs, orb_dev)
+    held = pltpu.VMEM((many, slab_rows, cells), jnp.float32)
+
+    def grant(mib):
+        return pltpu.CompilerParams(vmem_limit_bytes=mib * MIB)
 
     own = jnp.pad(jnp.concatenate([pair_list, box_start], axis=1), ((0, 0), (0, FIELDS - 5)))
     row = own.reshape(1, pair_dev * FIELDS)
@@ -394,56 +438,81 @@
         jnp.broadcast_to(row, (devices, row.shape[1])), axes, split_axis=0, concat_axis=0, tiled=True
     )
 
-    outgoing = pl.pallas_call(
+    outgoing, work = pl.pallas_call(
         functools.partial(pack_kernel, pair_dev),
-        out_shape=jax.ShapeDtypeStruct(slots, jnp.float32),
+        out_shape=[
+            jax.ShapeDtypeStruct(slots, jnp.float32),
+            jax.ShapeDtypeStruct((9, max(many, pairs)), jnp.int32),
+        ],
         in_specs=[smem, smem, hbm],
-        out_specs=vmem,
+        out_specs=[free, smem],
         scratch_shapes=[
-            pltpu.VMEM((2 * pairs, slab_rows, cells), jnp.float32),
-            pltpu.SemaphoreType.DMA((2 * pairs,)),
+            held,
+            pltpu.VMEM((pairs + 1, slab_rows, PACKED), jnp.float32),
+            pltpu.SMEM((orb_dev,), jnp.int32),
+            pltpu.SemaphoreType.DMA((many,)),
+            pltpu.SemaphoreType.DMA((pairs,)),
         ],
-        compiler_params=params,
+        compiler_params=grant(56),
         name="pack",
     )(table, place, orbitals)
     received = lax.all_to_all(outgoing, axes, split_axis=0, concat_axis=0, tiled=True)
 
-    mats = matrices(box_start)
+    zeros, cleared = pl.pallas_call(
+        clear_kernel,
+        out_shape=[
+            jax.ShapeDtypeStruct(orbitals.shape, jnp.float32),
+            jax.ShapeDtypeStruct((8, LANES), jnp.int32),
+        ],
+        in_specs=[smem],
+        out_specs=[hbm, vmem],
+        scratch_shapes=[
+            pltpu.VMEM((orb_dev // CLEARS, slab_rows, cells), jnp.float32),
+            pltpu.SemaphoreType.DMA((CLEARS,)),
+        ],
+        compiler_params=grant(16),
+        cost_estimate=pl.CostEstimate(
+            flops=0, bytes_accessed=orbitals.size * 4, transcendentals=0
+        ),
+        name="clear",
+    )(work)
     solved = pl.pallas_call(
         functools.partial(solve_kernel, orb_dev),
         out_shape=jax.ShapeDtypeStruct((n_slab, n_orb, pair_dev, slab_rows, PACKED), jnp.float32),
-        in_specs=[smem, hbm] + [vmem] * 13,
-        out_specs=hbm,
+        in_specs=[smem, free] + [vmem] * 14,
+        out_specs=free,
         scratch_shapes=[
             pltpu.VMEM((2, n_slab, slab_rows, PACKED), jnp.float32),
             pltpu.VMEM((2, n_slab, slab_rows, PACKED), jnp.float32),
             pltpu.SemaphoreType.DMA((2,)),
         ],
-        compiler_params=params,
+        compiler_params=grant(16),
         name="solve",
     )(
         pair_list,
         received.reshape(n_slab, n_orb, pair_dev, slab_rows, PACKED),
-        *mats,
+        cleared,
+        *matrices(box_start),
         jnp.asarray(spectrum()),
     )
     returned = lax.all_to_all(solved.reshape(slots), axes, split_axis=0, concat_axis=0, tiled=True)
 
     return pl.pallas_call(
-        functools.partial(place_kernel, pair_dev),
+        place_kernel,
         out_shape=jax.ShapeDtypeStruct(orbitals.shape, jnp.float32),
-        in_specs=[smem, smem, hbm, vmem, hbm],
+        in_specs=[smem, smem, hbm, free, hbm],
         out_specs=hbm,
         scratch_shapes=[
-            pltpu.VMEM((2 * pairs, slab_rows, cells), jnp.float32),
-            pltpu.VMEM(orbitals.shape, jnp.float32),
-            pltpu.SMEM((orb_dev,), jnp.int32),
-            pltpu.SemaphoreType.DMA((2 * pairs + orb_dev,)),
+            held,
+            pltpu.VMEM(slots, jnp.float32),
+            held,
+            pltpu.SemaphoreType.DMA((many,)),
+            pltpu.SemaphoreType.DMA((pairs,)),
         ],
         input_output_aliases={4: 0},
-        compiler_params=params,
+        compiler_params=grant(56),
         name="place",
-    )(table, place, orbitals, returned, jnp.zeros(orbitals.shape, jnp.float32))
+    )(work, place, orbitals, returned, zeros)
 
 
 def solution(mesh):

time: 97.4 us -> 91.3 us (0.937)
  the two profiles are of different devices: /device:TPU:0 before, /device:TPU:1 now
where the time goes in v2:
time: 91.3 us; the launch traced here: 89.6 us
  blocking collectives  29.4 us (32%)
  Pallas kernels  19 us (21%)
  waiting for transfers between devices  14.6 us (16%)
  other arithmetic  13 us (14%)
  starting transfers between devices  10.2 us (11%)
  local copies, waits for them, and re-layouts  3.28 us (4%)
    all_to_all x1, blocking collectives, body(): lax.all_to_all(solved.reshape(slots), axes, split_axis=0, concat_axis=0,...  29.4 us
    all_to_all x1, waiting for transfers between devices, body(): lax.all_to_all(outgoing, axes, split_axis=0, concat_axis=0, tiled=True)  10.5 us
    convert_element_type x6, other arithmetic, halves(): return (high.astype(jnp.bfloat16), (full - high).astype(jnp.bfloat16))  10.5 us
    all_to_all x1, starting transfers between devices, body(): lax.all_to_all(jnp.broadcast_to(row, (devices, row.shape[1])), axes, spli...  7.1 us
    pallas_call x1, Pallas kernels, body(): pl.pallas_call(functools.partial(pack_kernel, pair_dev), out_shape=[jax.S...  6.42 us
    pallas_call x1, Pallas kernels, body(): pl.pallas_call(place_kernel, out_shape=jax.ShapeDtypeStruct(orbitals.shap...  5.76 us
    pallas_call x1, Pallas kernels, body(): pl.pallas_call(clear_kernel, out_shape=[jax.ShapeDtypeStruct(orbitals.sha...  4.11 us
    all_to_all x1, waiting for transfers between devices, body(): lax.all_to_all(jnp.broadcast_to(row, (devices, row.shape[1])), axes, spli...  4.06 us
  transfers between devices with their start and end apart: 2, of which 2 were waited for; matrix products, arithmetic and copies ran while one was open for 15% of the time, Pallas kernels for 5%

profile of v2, /device:TPU:1, one launch (start us, length us, event | category | flops | bytes accessed | tf_op | source)
XLA Modules:
  0.0 89.6 jit_solution(6580805724557186080)
XLA Ops:
  0.0 0.0 copy-start
  0.0 0.0 copy-start.2
  0.0 0.8 pad_add_fusion
  0.8 0.6 broadcast_in_dim.21
  1.4 7.1 %all-to-all-start = ((s32[32,1,128]{2,1,0:T(1,128)}), s32[32,1,128]{2,1,0:T(1,128)S(1)}, u32[]{:S(2)}, u32[]{:S(2)}) async-start(s32[32,1,128]{2,1,0:T(1,128)} %broadcast_in_dim.21), calls=%async_computation | async-start | bytes 32768 | tf_op jit(solution)/shard_map/all_to_all | solution.py:437
  8.6 1.4 %fusion.60 = (s32[1,1]{1,0:T(1,128)}, s32[1,1]{1,0:T(1,128)}, s32[1,1]{1,0:T(1,128)}) fusion(s32[1,3]{1,0:T(1,128)} %param.6), kind=kLoop, calls=%fused_computation.99 | loop fusion | bytes 24 | tf_op jit(solution)/shard_map/slice | solution.py:77
  9.9 0.6 and_add_fusion
  10.5 0.6 pad_add_fusion.1.place
  11.1 4.1 %all-to-all-done = s32[32,1,128]{2,1,0:T(1,128)S(1)} async-done(((s32[32,1,128]{2,1,0:T(1,128)}), s32[32,1,128]{2,1,0:T(1,128)S(1)}, u32[]{:S(2)}, u32[]{:S(2)}) %all-to-all-start) | async-done | bytes 16416 | tf_op jit(solution)/shard_map/all_to_all | solution.py:437
  15.2 0.0 copy-start.3
  15.2 0.6 copy-done.3
  15.8 6.4 %pack.1 = (f32[32,8,1024]{2,1,0:T(8,128)}, s32[9,64]{1,0:T(8,128)}) custom-call(s32[32,128]{1,0:T(8,128)} %bitcast.12, s32[2]{0:T(128)} %pad_add_fusion.1.place, f32[64,8,4096]{2,1,0:T(8,128)} %orbitals.3), custom_call_target="tpu_custom_call" | custom-call | tf_op jit(solution)/shard_map/pack/pallas_call | solution.py:441
  22.2 3.1 %all-to-all-start.1 = ((f32[32,8,1024]{2,1,0:T(8,128)}), f32[32,8,1024]{2,1,0:T(8,128)S(1)}, u32[]{:S(2)}, u32[]{:S(2)}) async-start(f32[32,8,1024]{2,1,0:T(8,128)} %get-tuple-element.10), calls=%async_computation.1 | async-start | bytes 2097152 | tf_op jit(solution)/shard_map/all_to_all | solution.py:459
  25.3 0.6 fusion.56
  25.9 0.8 fusion.39
  26.6 0.9 fusion.32
  27.5 1.9 %fusion.16 = (bf16[1,384,256]{2,1,0:T(8,128)(2,1)S(1)}, bf16[1,384,256]{2,1,0:T(8,128)(2,1)S(1)}) fusion(s32[256]{0:T(256)S(1)} %get-tuple-element.34, s32[384]{0:T(512)S(1)} %get-tuple-element.32, s32[256]{0:T(256)S(1)} %get-tuple-element.35, s32[384]{0:T(512)S(1)} %get-tuple-element.33), kind=kLoop, calls=%fused_computation.30 | loop fusion | flops 1474560 | bytes 398336 | tf_op jit(solution)/shard_map/convert_element_type | solution.py:64
  29.4 1.8 %fusion.17 = (bf16[1,256,384]{2,1,0:T(8,128)(2,1)S(1)}, bf16[1,256,384]{2,1,0:T(8,128)(2,1)S(1)}) fusion(s32[256]{0:T(256)S(1)} %get-tuple-element.34, s32[384]{0:T(512)S(1)} %get-tuple-element.32, s32[384]{0:T(512)S(1)} %get-tuple-element.33, s32[256]{0:T(256)S(1)} %get-tuple-element.35), kind=kLoop, calls=%fused_computation.31 | loop fusion | flops 1474560 | bytes 398336 | tf_op jit(solution)/shard_map/convert_element_type | solution.py:64
  31.2 2.4 %fusion = (bf16[1,256,512]{2,1,0:T(8,128)(2,1)S(1)}, bf16[1,256,512]{2,1,0:T(8,128)(2,1)S(1)}) fusion(s32[256]{0:T(256)S(1)} %and_add_fusion, s32[512]{0:T(512)S(1)} %get-tuple-element.29, pred[512]{0:T(512)(128)(4,1)S(1)} %fusion.47, s32[512]{0:T(512)S(1)} %get-tuple-element.28, s32[256]{0:T(256)S(1)} %get-tuple-element.31, s32[512]{0:T(512)S(1)} %fusion.48, ...), kind=kLoop, calls=%fused_computation.12 | loop fusion | flops 2359296 | bytes 534016 | tf_op jit(solution)/shard_map/convert_element_type | solution.py:64
  33.7 2.7 %fusion.1 = (bf16[1,512,256]{2,1,0:T(8,128)(2,1)S(1)}, bf16[1,512,256]{2,1,0:T(8,128)(2,1)S(1)}) fusion(s32[256]{0:T(256)S(1)} %and_add_fusion, s32[512]{0:T(512)S(1)} %get-tuple-element.29, pred[512]{0:T(512)(128)(4,1)S(1)} %fusion.47, s32[512]{0:T(512)S(1)} %get-tuple-element.28, s32[256]{0:T(256)S(1)} %get-tuple-element.31, s32[512]{0:T(512)S(1)} %fusion.48, ...), kind=kLoop, calls=%fused_computation.13 | loop fusion | flops 2359296 | bytes 534016 | tf_op jit(solution)/shard_map/convert_element_type | solution.py:64
  36.4 0.0 copy-start.1
  36.4 0.7 copy-done.1
  37.1 4.1 %clear.1 = (f32[64,8,4096]{2,1,0:T(8,128)}, s32[8,128]{1,0:T(8,128)S(1)}) custom-call(s32[9,64]{1,0:T(8,128)S(1)} %copy-done.1), custom_call_target="tpu_custom_call" | custom-call | bytes 8388608 | tf_op jit(solution)/shard_map/clear/pallas_call | solution.py:461
  41.2 10.5 %all-to-all-done.1 = f32[32,8,1024]{2,1,0:T(8,128)S(1)} async-done(((f32[32,8,1024]{2,1,0:T(8,128)}), f32[32,8,1024]{2,1,0:T(8,128)S(1)}, u32[]{:S(2)}, u32[]{:S(2)}) %all-to-all-start.1) | async-done | bytes 1048608 | tf_op jit(solution)/shard_map/all_to_all | solution.py:459
  51.8 0.0 copy-done
  51.8 0.0 copy-done.2
  51.8 2.7 %solve.1 = f32[8,4,1,8,1024]{4,3,2,1,0:T(8,128)S(1)} custom-call(s32[1,2]{1,0:T(1,128)S(1)} %copy-done.2, f32[8,4,1,8,1024]{4,3,2,1,0:T(8,128)S(1)} %bitcast.10, s32[8,128]{1,0:T(8,128)S(1)} %get-tuple-element.11.cleared, bf16[1,48,32]{2,1,0:T(8,128)(2,1)S(1)} %get-tuple-element.27.refs_0_, bf16[1,48,32]{2,1,0:T(8,128)(2,1)S(1)} %get-tuple-element.26.refs_1_, ...), custom_call_target="tpu_custom_call" | custom-call | tf_op jit(solution)/shard_map/solve/pallas_call | solution.py:479
  54.5 29.4 %all_to_all.18.returned = f32[32,8,1024]{2,1,0:T(8,128)} all-to-all(f32[32,8,1024]{2,1,0:T(8,128)S(1)} %bitcast.11), channel_id=1, replica_groups=mesh['slab'=8,'orb'=4] {'slab','orb'}, dimensions={0} | all-to-all | bytes 2097152 | tf_op jit(solution)/shard_map/all_to_all | solution.py:498
  83.8 5.8 %place.1 = f32[64,8,4096]{2,1,0:T(8,128)} custom-call(s32[9,64]{1,0:T(8,128)} %get-tuple-element.9.work, s32[2]{0:T(128)} %pad_add_fusion.1.place, f32[64,8,4096]{2,1,0:T(8,128)} %orbitals.3, f32[32,8,1024]{2,1,0:T(8,128)} %all_to_all.18.returned, f32[64,8,4096]{2,1,0:T(8,128)} %get-tuple-element.12.zeros), custom_call_target="tpu_custom_call", output_to_operand_aliasing={{}: (4, {})} | custom-call | tf_op jit(solution)/shard_map/place/pallas_call | solution.py:500
  (7 shorter events, 0.0 us)
Async XLA Ops:
  0.0 51.8 %copy-start = (f32[384,384]{1,0:T(8,128)S(1)}, f32[384,384]{1,0:T(8,128)}, u32[]{:S(2)}) copy-start(f32[384,384]{1,0:T(8,128)} %constant.49.clone.refs_12_) | copy-start | bytes 1769476
  0.0 51.8 %copy-start.2 = (s32[1,2]{1,0:T(1,128)S(1)}, s32[1,2]{1,0:T(1,128)}, u32[]{:S(2)}) copy-start(s32[1,2]{1,0:T(1,128)} %own.1) | copy-start | bytes 28
  1.4 13.7 %all-to-all-start = ((s32[32,1,128]{2,1,0:T(1,128)}), s32[32,1,128]{2,1,0:T(1,128)S(1)}, u32[]{:S(2)}, u32[]{:S(2)}) async-start(s32[32,1,128]{2,1,0:T(1,128)} %broadcast_in_dim.21), calls=%async_computation | async-start | bytes 32768 | tf_op jit(solution)/shard_map/all_to_all | solution.py:437
  15.2 0.6 copy-start.3
  22.2 29.6 %all-to-all-start.1 = ((f32[32,8,1024]{2,1,0:T(8,128)}), f32[32,8,1024]{2,1,0:T(8,128)S(1)}, u32[]{:S(2)}, u32[]{:S(2)}) async-start(f32[32,8,1024]{2,1,0:T(8,128)} %get-tuple-element.10), calls=%async_computation.1 | async-start | bytes 2097152 | tf_op jit(solution)/shard_map/all_to_all | solution.py:459
  36.4 0.7 copy-start.1

commit v3 on v2

v3 whole, which is shorter than its diff:
```python
import functools

import jax
import jax.numpy as jnp
import numpy as np
from jax import lax
from jax.experimental import pallas as pl
from jax.experimental.pallas import tpu as pltpu
from jax.sharding import PartitionSpec as P

NY = 64
NZ = 64
ITERS = 16
HALF = 32
FULL = 64
PACKED = HALF * HALF
MODES = 48
MARGIN = (MODES - HALF) // 2
PERIOD = 2 * (MODES + 1)
LANES = 128
FIELDS = 8
CLEARS = 16
MIB = 1024 * 1024
COUNT, PAIR, SLOT, SECOND, FIRST_A, FIRST_B, LAST_A, LAST_B, START_X, START_Y, START_Z, BLANK = range(12)

screening = 0.02
center_eig = 6.0 + screening
half_width = 6.0
sigma_one = center_eig / half_width


def spectrum():
    cosine = np.cos(np.pi * (np.arange(MODES) + 1) / (MODES + 1))
    lam = center_eig - 2.0 * (
        cosine[:, None, None] + cosine[None, :, None] + cosine[None, None, :]
    )
    solution_now, residue, ratio = np.zeros_like(lam), np.ones_like(lam), 1.0 / sigma_one
    update = residue / center_eig
    for _ in range(ITERS):
        solution_now = solution_now + update
        residue = residue - lam * update
        ratio_next = 1.0 / (2.0 * sigma_one - ratio)
        update = ratio_next * ratio * update + 2.0 * ratio_next / half_width * residue
        ratio = ratio_next
    table = -solution_now * (2.0 / (MODES + 1)) ** 3
    table = np.pad(table, ((0, 0), (0, 0), (0, LANES // 2 - MODES)))
    table = table.reshape(MODES // 16, 2, 8, MODES, LANES // 2).transpose(3, 2, 0, 1, 4)
    return table.reshape(MODES * 8, MODES // 16 * LANES).astype(np.float32)


def sine(mode, cell, start):
    place = (cell - start) & (HALF - 1)
    phase = ((mode + 1) * (place + MARGIN + 1)) % PERIOD
    return jnp.sin(phase.astype(jnp.float32) * np.float32(np.pi / (MODES + 1)))


def split(full):
    high = full.astype(jnp.bfloat16)
    return high, (full - high.astype(jnp.float32)).astype(jnp.bfloat16)


def halves(full):
    high = lax.reduce_precision(full, 8, 7)
    return high.astype(jnp.bfloat16), (full - high).astype(jnp.bfloat16)


def iotas(shape):
    return [lax.broadcasted_iota(jnp.int32, shape, d) for d in range(len(shape))]


def cell_y(q, g):
    return 2 * q + (g >> 1) + HALF // 2 * (g & 1)


def matrices(box_start):
    count = box_start.shape[0]
    bx, by, bz = (box_start[:, d][:, None, None] for d in range(3))

    def x_of(k, r):
        return sine(k, r, bx)

    def y_of(row, col):
        g, q = col >> 6, (col >> 3) & 7
        return jnp.where((row & 7) == (col & 7), sine(row >> 3, cell_y(q, g), by), 0.0)

    def z_of(row, col):
        same = ((row >> 7) == ((col >> 6) & 1)) & (((row >> 5) & 3) == (col >> 7))
        kz = col & 63
        return jnp.where(same & (kz < MODES), sine(kz, row & 31, bz), 0.0)

    out = []
    for of, rows, cols in ((x_of, MODES, HALF), (z_of, 256, 512), (y_of, MODES * 8, 256)):
        _, row, col = iotas((count, rows, cols))
        out += halves(of(row, col))
        _, row, col = iotas((count, cols, rows))
        out += halves(of(col, row))
    return out


def lane(shape):
    return lax.broadcasted_iota(jnp.int32, shape, len(shape) - 1)


def in_box(cell, start):
    return ((cell - start) & (FULL - 1)) < HALF


def fold(full, start_y, start_z):
    rows = full.shape[0]
    at = lane((rows, LANES))
    upper = (at >> 6) & 1
    in_z = in_box(at & 31, start_z)
    first = (at & 63) < 32
    picked = []
    for v in range(HALF // 2):
        low = full[:, v * LANES : (v + 1) * LANES]
        high = full[:, (v + HALF // 2) * LANES : (v + HALF // 2 + 1) * LANES]
        picked.append(jnp.where(in_box(2 * v + upper, start_y), low, high))
    out = []
    for q in range(8):
        a, b = picked[q], picked[q + 8]
        a = jnp.where(in_z, a, pltpu.roll(a, 96, 1))
        b = jnp.where(in_z, pltpu.roll(b, 32, 1), b)
        out.append(jnp.where(first, a, b))
    return out


def unfold(packed, start_y, start_z, row_mask):
    rows = packed.shape[0]
    at = lane((rows, LANES))
    upper = (at >> 6) & 1
    inside = in_box(at & 63, start_z) & row_mask
    first = (at & 63) < 32
    out = [None] * 32
    for v in range(16):
        piece = packed[:, (v % 8) * LANES : (v % 8 + 1) * LANES]
        if v < 8:
            wide = jnp.where(first, piece, pltpu.roll(piece, 32, 1))
        else:
            wide = jnp.where(first, pltpu.roll(piece, 96, 1), piece)
        wide = jnp.where(inside, wide, 0.0)
        in_y = in_box(2 * v + upper, start_y)
        out[v] = jnp.where(in_y, wide, 0.0)
        out[v + 16] = jnp.where(in_y, 0.0, wide)
    return out


def row_mask(first_row, rows, start_x):
    at = lax.broadcasted_iota(jnp.int32, (rows, LANES), 0)
    return in_box(at + first_row, start_x)


def pack_kernel(pair_dev, table_in, orbitals, out, work, table, held, packed, seen, sems, out_sems, table_sem):
    orb_dev, slab_rows, _ = orbitals.shape
    pairs = out.shape[0]
    base, first_row = lax.axis_index("orb") * orb_dev, lax.axis_index("slab") * slab_rows
    table_copy = pltpu.make_async_copy(table_in, table, table_sem)
    table_copy.start()
    packed[pairs] = jnp.zeros(packed.shape[1:], jnp.float32)
    for k in range(orb_dev + 1):
        seen[k] = 0
    table_copy.wait()

    def copy_of(index, slot):
        return pltpu.make_async_copy(orbitals.at[index], held.at[slot], sems.at[slot])

    def send(g, source):
        return pltpu.make_async_copy(packed.at[source], out.at[g], out_sems.at[g])

    def scan(g, carry):
        terms, blanks = carry
        row, off = g // pair_dev, (g % pair_dev) * FIELDS
        left, right = table[row, off] - base, table[row, off + 1] - base
        x = table[row, off + 2]
        meets = in_box(first_row, x) | in_box(first_row + slab_rows - 1, x)
        has_left = (left >= 0) & (left < orb_dev)
        has_right = (right >= 0) & (right < orb_dev)
        here = has_left | has_right
        live = here & meets
        both = has_left & has_right
        a = jnp.where(has_left, left, right)
        b = jnp.where(both, right, -1)
        work[PAIR, terms] = g
        work[SLOT, terms] = a
        work[SECOND, terms] = b
        work[START_X, terms] = x
        work[START_Y, terms] = table[row, off + 3]
        work[START_Z, terms] = table[row, off + 4]
        work[BLANK, blanks] = g

        @pl.when(live)
        def _():
            copy_of(a, 2 * terms).start()

            @pl.when(both)
            def _():
                copy_of(b, 2 * terms + 1).start()

        for which, k, used in ((FIRST_A, a, live), (FIRST_B, b, live & both)):
            k = jnp.where(used, k, orb_dev)
            old = seen[k]
            work[which, terms] = old
            seen[k] = 1
        terms = terms + jnp.where(live, 1, 0)
        return terms, blanks + jnp.where(here & jnp.logical_not(meets), 1, 0)

    zero = jnp.int32(0)
    terms, blanks = lax.fori_loop(0, pairs, scan, (zero, zero), unroll=4)
    work[COUNT, 0] = terms
    work[COUNT, 1] = first_row

    @pl.loop(0, blanks)
    def _(i):
        send(work[BLANK, i], pairs).start()

    @pl.loop(0, terms)
    def _(n):
        i = terms - 1 - n
        for which, source in ((LAST_B, SECOND), (LAST_A, SLOT)):
            k = work[source, i]
            k = jnp.where(k < 0, orb_dev, k)
            work[which, i] = seen[k]
            seen[k] = 0

    @pl.loop(0, terms)
    def _(i):
        g = work[PAIR, i]

        def put(full):
            mask = row_mask(first_row, slab_rows, work[START_X, i])
            for q, piece in enumerate(fold(full, work[START_Y, i], work[START_Z, i])):
                packed[g, :, q * LANES : (q + 1) * LANES] = jnp.where(mask, piece, 0.0)
            send(g, g).start()

        copy_of(work[SLOT, i], 2 * i).wait()

        @pl.when(work[SECOND, i] >= 0)
        def _():
            copy_of(work[SECOND, i], 2 * i + 1).wait()
            put(held[2 * i] * held[2 * i + 1])

        @pl.when(work[SECOND, i] < 0)
        def _():
            put(held[2 * i])

    @pl.loop(0, terms)
    def _(i):
        send(work[PAIR, i], work[PAIR, i]).wait()

    @pl.loop(0, blanks)
    def _(i):
        send(work[BLANK, i], pairs).wait()


def clear_kernel(work, out, done, blank, sems):
    done[...] = jnp.full(done.shape, work[COUNT, 0], jnp.int32)
    count = blank.shape[0]
    blank[...] = jnp.zeros(blank.shape, jnp.float32)
    copies = [
        pltpu.make_async_copy(blank, out.at[c * count : (c + 1) * count], sems.at[c])
        for c in range(CLEARS)
    ]
    for c in copies:
        c.start()
    for c in copies:
        c.wait()


def dot3(a, b):
    def dot(left, right):
        return jnp.dot(left, right, preferred_element_type=jnp.float32)

    return dot(a[0], b[0]) + (dot(a[0], b[1]) + dot(a[1], b[0]))


def tile(full, row, col):
    return full[row * 8 : row * 8 + 8, col * LANES : (col + 1) * LANES]


def blocks(rows):
    return jnp.concatenate([jnp.concatenate(r, axis=1) for r in rows], axis=0)


def potential_of(density, x, xt, z, zt, y, yt, weights):
    pairs_x = MODES // 16
    u = dot3(x, split(density))
    u = blocks(
        [[tile(u, 2 * tp + par, q) for par in range(2)] for tp in range(pairs_x) for q in range(8)]
    )
    u = dot3(split(u), z)
    u = blocks(
        [[tile(u, tp * 8 + q, g) for tp in range(pairs_x)] for g in range(4) for q in range(8)]
    )
    u = dot3(y, split(u)) * weights
    u = dot3(yt, split(u))
    u = blocks(
        [[tile(u, g * 8 + q, tp) for g in range(4)] for tp in range(pairs_x) for q in range(8)]
    )
    u = dot3(split(u), zt)
    u = blocks(
        [[tile(u, tp * 8 + q, par) for q in range(8)] for tp in range(pairs_x) for par in range(2)]
    )
    return dot3(xt, split(u))


def solve_kernel(orb_dev, own, received, cleared, *refs):
    del cleared
    mats, weights, out = refs[:12], *refs[12:]
    n_slab, _, pair_dev, rows, _ = received.shape
    half = n_slab // 2
    for i in range(pair_dev):
        plane = [own[i, side] // orb_dev for side in range(2)]
        sides = [
            jnp.concatenate(
                [received[s, at, i] + received[s + half, at, i] for s in range(half)], axis=0
            )
            for at in plane
        ]
        together = plane[0] == plane[1]
        density = jnp.where(together, sides[0], sides[0] * sides[1])
        m = [(mats[k][i], mats[k + 1][i]) for k in range(0, 12, 2)]
        potential = potential_of(density, *m, weights[...])
        for side in range(2):
            term = jnp.where(together, potential, potential * sides[1 - side])
            for s in range(half):
                part = term[s * rows : (s + 1) * rows]
                out[s, plane[side], i] = part
                out[s + half, plane[side], i] = part


def place_kernel(work, orbitals, returned, zeros, out, held, acc, sems, out_sems):
    del zeros
    _, slab_rows, _ = orbitals.shape
    terms, first_row = work[COUNT, 0], work[COUNT, 1]

    def factors(i):
        return [
            pltpu.make_async_copy(
                orbitals.at[work[which, i]], held.at[2 * i + n], sems.at[2 * i + n]
            )
            for n, which in enumerate((SLOT, SECOND))
        ]

    def copy_out(k):
        return pltpu.make_async_copy(acc.at[k], out.at[k], out_sems.at[k])

    @pl.loop(0, terms)
    def _(i):
        @pl.when(work[SECOND, i] >= 0)
        def _():
            for c in factors(i):
                c.start()

    @pl.loop(0, terms)
    def _(i):
        a, b = work[SLOT, i], work[SECOND, i]
        mask = row_mask(first_row, slab_rows, work[START_X, i])
        pieces = unfold(returned[work[PAIR, i]], work[START_Y, i], work[START_Z, i], mask)

        def add(k, later, last, slot):
            def term(v):
                if slot is None:
                    return pieces[v]
                return pieces[v] * held[slot, :, v * LANES : (v + 1) * LANES]

            @pl.when(later == 0)
            def _():
                for v in range(len(pieces)):
                    acc[k, :, v * LANES : (v + 1) * LANES] = term(v)

            @pl.when(later != 0)
            def _():
                for v in range(len(pieces)):
                    acc[k, :, v * LANES : (v + 1) * LANES] += term(v)

            @pl.when(last != 0)
            def _():
                copy_out(k).start()

        @pl.when(b >= 0)
        def _():
            for c in factors(i):
                c.wait()
            add(a, work[FIRST_A, i], work[LAST_A, i], 2 * i + 1)
            add(b, work[FIRST_B, i], work[LAST_B, i], 2 * i)

        @pl.when(b < 0)
        def _():
            add(a, work[FIRST_A, i], work[LAST_A, i], None)

    @pl.loop(0, terms)
    def _(i):
        @pl.when(work[LAST_A, i] != 0)
        def _():
            copy_out(work[SLOT, i]).wait()

        @pl.when((work[SECOND, i] >= 0) & (work[LAST_B, i] != 0))
        def _():
            copy_out(work[SECOND, i]).wait()


def body(orbitals, pair_list, box_start):
    n_slab = lax.axis_size("slab")
    n_orb = lax.axis_size("orb")
    axes = ("slab", "orb")
    orb_dev, slab_rows, cells = orbitals.shape
    pair_dev = pair_list.shape[0]
    devices = n_slab * n_orb
    pairs = devices * pair_dev

    smem = pl.BlockSpec(memory_space=pltpu.SMEM)
    vmem = pl.BlockSpec(memory_space=pltpu.VMEM)
    free = pl.BlockSpec(memory_space=pl.ANY)
    hbm = pl.BlockSpec(memory_space=pltpu.HBM)
    slots = (pairs, slab_rows, PACKED)
    held = pltpu.VMEM((2 * pairs, slab_rows, cells), jnp.float32)

    def grant(mib):
        return pltpu.CompilerParams(vmem_limit_bytes=mib * MIB)

    width = -(-pair_dev * FIELDS // LANES) * LANES
    row = jnp.concatenate([pair_list, box_start], axis=1)
    row = jnp.pad(row, ((0, 0), (0, FIELDS - row.shape[1]))).reshape(1, pair_dev * FIELDS)
    row = jnp.pad(row, ((0, 0), (0, width - row.shape[1])))
    table = lax.all_to_all(
        jnp.broadcast_to(row, (devices, width)), axes, split_axis=0, concat_axis=0, tiled=True
    )

    outgoing, work = pl.pallas_call(
        functools.partial(pack_kernel, pair_dev),
        out_shape=[
            jax.ShapeDtypeStruct(slots, jnp.float32),
            jax.ShapeDtypeStruct((12, -(-(2 * pairs + 1) // LANES) * LANES), jnp.int32),
        ],
        in_specs=[free, hbm],
        out_specs=[hbm, smem],
        scratch_shapes=[
            pltpu.SMEM((devices, width), jnp.int32),
            held,
            pltpu.VMEM((pairs + 1, slab_rows, PACKED), jnp.float32),
            pltpu.SMEM((orb_dev + 1,), jnp.int32),
            pltpu.SemaphoreType.DMA((2 * pairs,)),
            pltpu.SemaphoreType.DMA((pairs,)),
            pltpu.SemaphoreType.DMA,
        ],
        compiler_params=grant(56),
        name="pack",
    )(table, orbitals)
    received = lax.all_to_all(outgoing, axes, split_axis=0, concat_axis=0, tiled=True)

    zeros, cleared = pl.pallas_call(
        clear_kernel,
        out_shape=[
            jax.ShapeDtypeStruct(orbitals.shape, jnp.float32),
            jax.ShapeDtypeStruct((8, LANES), jnp.int32),
        ],
        in_specs=[smem],
        out_specs=[hbm, vmem],
        scratch_shapes=[
            pltpu.VMEM((orb_dev // CLEARS, slab_rows, cells), jnp.float32),
            pltpu.SemaphoreType.DMA((CLEARS,)),
        ],
        compiler_params=grant(16),
        cost_estimate=pl.CostEstimate(
            flops=0, bytes_accessed=orbitals.size * 4, transcendentals=0
        ),
        name="clear",
    )(work)

    solved = pl.pallas_call(
        functools.partial(solve_kernel, orb_dev),
        out_shape=jax.ShapeDtypeStruct((n_slab, n_orb, pair_dev, slab_rows, PACKED), jnp.float32),
        in_specs=[smem] + [vmem] * 15,
        out_specs=vmem,
        compiler_params=grant(16),
        name="solve",
    )(
        pair_list,
        received.reshape(n_slab, n_orb, pair_dev, slab_rows, PACKED),
        cleared,
        *matrices(box_start),
        jnp.asarray(spectrum()),
    )
    returned = lax.all_to_all(solved.reshape(slots), axes, split_axis=0, concat_axis=0, tiled=True)

    return pl.pallas_call(
        place_kernel,
        out_shape=jax.ShapeDtypeStruct(orbitals.shape, jnp.float32),
        in_specs=[smem, hbm, vmem, hbm],
        out_specs=hbm,
        scratch_shapes=[
            held,
            pltpu.VMEM(orbitals.shape, jnp.float32),
            pltpu.SemaphoreType.DMA((2 * pairs,)),
            pltpu.SemaphoreType.DMA((orb_dev,)),
        ],
        input_output_aliases={3: 0},
        compiler_params=grant(52),
        name="place",
    )(work, orbitals, returned, zeros)


def solution(mesh):
    return jax.shard_map(
        body,
        mesh=mesh,
        in_specs=(P("orb", "slab", None), P(("slab", "orb"), None), P(("slab", "orb"), None)),
        out_specs=P("orb", "slab", None),
        check_vma=False,
    )
```

time: 91.3 us -> 86.3 us (0.945)
  the two profiles are of different devices: /device:TPU:1 before, /device:TPU:0 now
where the time goes in v3:
time: 86.3 us; the launch traced here: 85 us
  blocking collectives  29.3 us (34%)
  Pallas kernels  15.6 us (18%)
  waiting for transfers between devices  14.1 us (16%)
  other arithmetic  12.6 us (15%)
  starting transfers between devices  9.96 us (12%)
  local copies, waits for them, and re-layouts  3.34 us (4%)
    all_to_all x1, blocking collectives, body(): lax.all_to_all(solved.reshape(slots), axes, split_axis=0, concat_axis=0,...  29.3 us
    convert_element_type x6, other arithmetic, halves(): return (high.astype(jnp.bfloat16), (full - high).astype(jnp.bfloat16))  10.4 us
    all_to_all x1, waiting for transfers between devices, body(): lax.all_to_all(outgoing, axes, split_axis=0, concat_axis=0, tiled=True)  9.04 us
    all_to_all x1, starting transfers between devices, body(): lax.all_to_all(jnp.broadcast_to(row, (devices, width)), axes, split_axis=...  7.3 us
    all_to_all x1, waiting for transfers between devices, body(): lax.all_to_all(jnp.broadcast_to(row, (devices, width)), axes, split_axis=...  5.04 us
    pallas_call x1, Pallas kernels, body(): pl.pallas_call(functools.partial(pack_kernel, pair_dev), out_shape=[jax.S...  5.02 us
    pallas_call x1, Pallas kernels, body(): pl.pallas_call(clear_kernel, out_shape=[jax.ShapeDtypeStruct(orbitals.sha...  4.11 us
    pallas_call x1, Pallas kernels, body(): pl.pallas_call(place_kernel, out_shape=jax.ShapeDtypeStruct(orbitals.shap...  3.86 us
  transfers between devices with their start and end apart: 2, of which 2 were waited for; matrix products, arithmetic and copies ran while one was open for 15% of the time, Pallas kernels for 5%

profile of v3, /device:TPU:0, one launch (start us, length us, event | category | flops | bytes accessed | tf_op | source)
XLA Modules:
  0.0 85.0 jit_solution(18284457757611801653)
XLA Ops:
  0.0 0.0 copy-start
  0.0 0.0 copy-start.3
  0.0 0.8 pad_add_fusion
  0.8 0.6 broadcast_in_dim.21
  1.4 7.3 %all-to-all-start = ((s32[32,1,128]{2,1,0:T(1,128)}), s32[32,1,128]{2,1,0:T(1,128)S(1)}, u32[]{:S(2)}, u32[]{:S(2)}) async-start(s32[32,1,128]{2,1,0:T(1,128)} %broadcast_in_dim.21), calls=%async_computation | async-start | bytes 32768 | tf_op jit(solution)/shard_map/all_to_all | solution.py:425
  8.7 1.4 %fusion.60 = (s32[1,1]{1,0:T(1,128)}, s32[1,1]{1,0:T(1,128)}, s32[1,1]{1,0:T(1,128)}) fusion(s32[1,3]{1,0:T(1,128)} %param.6), kind=kLoop, calls=%fused_computation.98 | loop fusion | bytes 24 | tf_op jit(solution)/shard_map/slice | solution.py:77
  10.2 0.6 and_add_fusion
  10.8 5.0 %all-to-all-done = s32[32,1,128]{2,1,0:T(1,128)S(1)} async-done(((s32[32,1,128]{2,1,0:T(1,128)}), s32[32,1,128]{2,1,0:T(1,128)S(1)}, u32[]{:S(2)}, u32[]{:S(2)}) %all-to-all-start) | async-done | bytes 16416 | tf_op jit(solution)/shard_map/all_to_all | solution.py:425
  15.8 0.0 copy-start.4
  15.8 0.6 copy-done.4
  16.4 5.0 %pack.1 = (f32[32,8,1024]{2,1,0:T(8,128)}, s32[12,128]{1,0:T(8,128)}) custom-call(s32[32,128]{1,0:T(8,128)} %bitcast.10, f32[64,8,4096]{2,1,0:T(8,128)} %orbitals.3), custom_call_target="tpu_custom_call" | custom-call | tf_op jit(solution)/shard_map/pack/pallas_call | solution.py:429
  21.5 0.0 copy-start.2
  21.5 2.7 %all-to-all-start.1 = ((f32[32,8,1024]{2,1,0:T(8,128)}), f32[32,8,1024]{2,1,0:T(8,128)S(1)}, u32[]{:S(2)}, u32[]{:S(2)}) async-start(f32[32,8,1024]{2,1,0:T(8,128)} %get-tuple-element.10), calls=%async_computation.1 | async-start | bytes 2097152 | tf_op jit(solution)/shard_map/all_to_all | solution.py:449
  24.2 0.7 fusion.56
  24.9 0.7 fusion.39
  25.6 0.8 fusion.32
  26.4 1.9 %fusion.16 = (bf16[1,384,256]{2,1,0:T(8,128)(2,1)S(1)}, bf16[1,384,256]{2,1,0:T(8,128)(2,1)S(1)}) fusion(s32[256]{0:T(256)S(1)} %get-tuple-element.34, s32[384]{0:T(512)S(1)} %get-tuple-element.32, s32[256]{0:T(256)S(1)} %get-tuple-element.35, s32[384]{0:T(512)S(1)} %get-tuple-element.33), kind=kLoop, calls=%fused_computation.30 | loop fusion | flops 1474560 | bytes 398336 | tf_op jit(solution)/shard_map/convert_element_type | solution.py:64
  28.3 1.8 %fusion.17 = (bf16[1,256,384]{2,1,0:T(8,128)(2,1)S(1)}, bf16[1,256,384]{2,1,0:T(8,128)(2,1)S(1)}) fusion(s32[256]{0:T(256)S(1)} %get-tuple-element.34, s32[384]{0:T(512)S(1)} %get-tuple-element.32, s32[384]{0:T(512)S(1)} %get-tuple-element.33, s32[256]{0:T(256)S(1)} %get-tuple-element.35), kind=kLoop, calls=%fused_computation.31 | loop fusion | flops 1474560 | bytes 398336 | tf_op jit(solution)/shard_map/convert_element_type | solution.py:64
  30.2 2.4 %fusion = (bf16[1,256,512]{2,1,0:T(8,128)(2,1)S(1)}, bf16[1,256,512]{2,1,0:T(8,128)(2,1)S(1)}) fusion(s32[256]{0:T(256)S(1)} %and_add_fusion, s32[512]{0:T(512)S(1)} %get-tuple-element.29, pred[512]{0:T(512)(128)(4,1)S(1)} %fusion.47, s32[512]{0:T(512)S(1)} %get-tuple-element.28, s32[256]{0:T(256)S(1)} %get-tuple-element.31, s32[512]{0:T(512)S(1)} %fusion.48, ...), kind=kLoop, calls=%fused_computation.12 | loop fusion | flops 2359296 | bytes 534016 | tf_op jit(solution)/shard_map/convert_element_type | solution.py:64
  32.6 2.7 %fusion.1 = (bf16[1,512,256]{2,1,0:T(8,128)(2,1)S(1)}, bf16[1,512,256]{2,1,0:T(8,128)(2,1)S(1)}) fusion(s32[256]{0:T(256)S(1)} %and_add_fusion, s32[512]{0:T(512)S(1)} %get-tuple-element.29, pred[512]{0:T(512)(128)(4,1)S(1)} %fusion.47, s32[512]{0:T(512)S(1)} %get-tuple-element.28, s32[256]{0:T(256)S(1)} %get-tuple-element.31, s32[512]{0:T(512)S(1)} %fusion.48, ...), kind=kLoop, calls=%fused_computation.13 | loop fusion | flops 2359296 | bytes 534016 | tf_op jit(solution)/shard_map/convert_element_type | solution.py:64
  35.3 0.0 copy-start.1
  35.3 0.7 copy-done.1
  36.0 4.1 %clear.1 = (f32[64,8,4096]{2,1,0:T(8,128)}, s32[8,128]{1,0:T(8,128)S(1)}) custom-call(s32[12,128]{1,0:T(8,128)S(1)} %copy-done.1), custom_call_target="tpu_custom_call" | custom-call | bytes 8388608 | tf_op jit(solution)/shard_map/clear/pallas_call | solution.py:451
  40.2 9.0 %all-to-all-done.1 = f32[32,8,1024]{2,1,0:T(8,128)S(1)} async-done(((f32[32,8,1024]{2,1,0:T(8,128)}), f32[32,8,1024]{2,1,0:T(8,128)S(1)}, u32[]{:S(2)}, u32[]{:S(2)}) %all-to-all-start.1) | async-done | bytes 1048608 | tf_op jit(solution)/shard_map/all_to_all | solution.py:449
  49.2 0.0 copy-done
  49.2 0.0 copy-done.3
  49.2 2.6 %solve.1 = f32[8,4,1,8,1024]{4,3,2,1,0:T(8,128)S(1)} custom-call(s32[1,2]{1,0:T(1,128)S(1)} %copy-done.3, f32[8,4,1,8,1024]{4,3,2,1,0:T(8,128)S(1)} %bitcast.8, s32[8,128]{1,0:T(8,128)S(1)} %get-tuple-element.11.cleared, bf16[1,48,32]{2,1,0:T(8,128)(2,1)S(1)} %get-tuple-element.27.refs_0_, bf16[1,48,32]{2,1,0:T(8,128)(2,1)S(1)} %get-tuple-element.26.refs_1_, ...), custom_call_target="tpu_custom_call" | custom-call | tf_op jit(solution)/shard_map/solve/pallas_call | solution.py:470
  51.8 29.3 %all_to_all.18.returned = f32[32,8,1024]{2,1,0:T(8,128)S(1)} all-to-all(f32[32,8,1024]{2,1,0:T(8,128)S(1)} %bitcast.9), channel_id=1, replica_groups=mesh['slab'=8,'orb'=4] {'slab','orb'}, dimensions={0} | all-to-all | bytes 2097152 | tf_op jit(solution)/shard_map/all_to_all | solution.py:484
  81.1 0.0 copy-done.2
  81.1 3.9 %place.1 = f32[64,8,4096]{2,1,0:T(8,128)} custom-call(s32[12,128]{1,0:T(8,128)S(1)} %copy-done.2, f32[64,8,4096]{2,1,0:T(8,128)} %orbitals.3, f32[32,8,1024]{2,1,0:T(8,128)S(1)} %all_to_all.18.returned, f32[64,8,4096]{2,1,0:T(8,128)} %get-tuple-element.12.zeros), custom_call_target="tpu_custom_call", output_to_operand_aliasing={{}: (3, {})} | custom-call | tf_op jit(solution)/shard_map/place/pallas_call | solution.py:486
  (7 shorter events, 0.0 us)
Async XLA Ops:
  0.0 49.2 %copy-start = (f32[384,384]{1,0:T(8,128)S(1)}, f32[384,384]{1,0:T(8,128)}, u32[]{:S(2)}) copy-start(f32[384,384]{1,0:T(8,128)} %constant.43.clone.refs_12_) | copy-start | bytes 1769476
  0.0 49.2 %copy-start.3 = (s32[1,2]{1,0:T(1,128)S(1)}, s32[1,2]{1,0:T(1,128)}, u32[]{:S(2)}) copy-start(s32[1,2]{1,0:T(1,128)} %own.1) | copy-start | bytes 28
  1.4 14.4 %all-to-all-start = ((s32[32,1,128]{2,1,0:T(1,128)}), s32[32,1,128]{2,1,0:T(1,128)S(1)}, u32[]{:S(2)}, u32[]{:S(2)}) async-start(s32[32,1,128]{2,1,0:T(1,128)} %broadcast_in_dim.21), calls=%async_computation | async-start | bytes 32768 | tf_op jit(solution)/shard_map/all_to_all | solution.py:425
  15.8 0.6 copy-start.4
  21.5 59.6 %copy-start.2 = (s32[12,128]{1,0:T(8,128)S(1)}, s32[12,128]{1,0:T(8,128)}, u32[]{:S(2)}) copy-start(s32[12,128]{1,0:T(8,128)} %get-tuple-element.9.work) | copy-start | bytes 18436
  21.5 27.7 %all-to-all-start.1 = ((f32[32,8,1024]{2,1,0:T(8,128)}), f32[32,8,1024]{2,1,0:T(8,128)S(1)}, u32[]{:S(2)}, u32[]{:S(2)}) async-start(f32[32,8,1024]{2,1,0:T(8,128)} %get-tuple-element.10), calls=%async_computation.1 | async-start | bytes 2097152 | tf_op jit(solution)/shard_map/all_to_all | solution.py:449
  35.3 0.7 copy-start.1

commit v4 on v3

--- a/solution.py
+++ b/solution.py
@@ -22,6 +22,9 @@
 CLEARS = 16
 MIB = 1024 * 1024
 COUNT, PAIR, SLOT, SECOND, FIRST_A, FIRST_B, LAST_A, LAST_B, START_X, START_Y, START_Z, BLANK = range(12)
+OWN_A, OWN_B, OWN_MEETS, OWN_X, OWN_Y, OWN_Z = range(12, 18)
+FULL_ROWS = 24
+BIG = 1 << 20
 
 screening = 0.02
 center_eig = 6.0 + screening
@@ -148,6 +151,17 @@
 def row_mask(first_row, rows, start_x):
     at = lax.broadcasted_iota(jnp.int32, (rows, LANES), 0)
     return in_box(at + first_row, start_x)
+
+
+def mark_last(work, seen, terms, orb_dev):
+    @pl.loop(0, terms)
+    def _(n):
+        i = terms - 1 - n
+        for which, source in ((LAST_B, SECOND), (LAST_A, SLOT)):
+            k = work[source, i]
+            k = jnp.where(k < 0, orb_dev, k)
+            work[which, i] = seen[k]
+            seen[k] = 0
 
 
 def pack_kernel(pair_dev, table_in, orbitals, out, work, table, held, packed, seen, sems, out_sems, table_sem):
@@ -213,14 +227,7 @@
     def _(i):
         send(work[BLANK, i], pairs).start()
 
-    @pl.loop(0, terms)
-    def _(n):
-        i = terms - 1 - n
-        for which, source in ((LAST_B, SECOND), (LAST_A, SLOT)):
-            k = work[source, i]
-            k = jnp.where(k < 0, orb_dev, k)
-            work[which, i] = seen[k]
-            seen[k] = 0
+    mark_last(work, seen, terms, orb_dev)
 
     @pl.loop(0, terms)
     def _(i):
@@ -330,6 +337,10 @@
 
 def place_kernel(work, orbitals, returned, zeros, out, held, acc, sems, out_sems):
     del zeros
+    place_terms(work, orbitals, lambda at: returned[at], out, held, acc, sems, out_sems)
+
+
+def place_terms(work, orbitals, fetch, out, held, acc, sems, out_sems):
     _, slab_rows, _ = orbitals.shape
     terms, first_row = work[COUNT, 0], work[COUNT, 1]
 
@@ -355,7 +366,7 @@
     def _(i):
         a, b = work[SLOT, i], work[SECOND, i]
         mask = row_mask(first_row, slab_rows, work[START_X, i])
-        pieces = unfold(returned[work[PAIR, i]], work[START_Y, i], work[START_Z, i], mask)
+        pieces = unfold(fetch(work[PAIR, i]), work[START_Y, i], work[START_Z, i], mask)
 
         def add(k, later, last, slot):
             def term(v):
@@ -397,6 +408,268 @@
         @pl.when((work[SECOND, i] >= 0) & (work[LAST_B, i] != 0))
         def _():
             copy_out(work[SECOND, i]).wait()
+
+
+def quotient(value, by):
+    return value >> (by.bit_length() - 1) if by & (by - 1) == 0 else value // by
+
+
+def pick(parts, index, act):
+    begin = 0
+    for part in parts:
+        inside = (index >= begin) & (index < begin + part.shape[0])
+        pl.when(inside)(lambda part=part, begin=begin: act(part, index - begin))
+        begin += part.shape[0]
+
+
+def slab_fields(n_slab, slab_rows):
+    if n_slab > 8:
+        return np.ones((FULL,), np.int32), 0
+    bits = np.zeros((FULL,), np.int64)
+    for x in range(FULL):
+        for slab in range(n_slab):
+            ends = (slab * slab_rows, (slab + 1) * slab_rows - 1)
+            if any((e - x) % FULL < HALF for e in ends):
+                bits[x] += 1 << (4 * slab)
+    return bits.astype(np.uint32).view(np.int32), 4
+
+
+def crossing_slots(cap, n_orb):
+    return [max(cap * 3 // 4 if d == 1 else cap // 2, 1) for d in range(1, n_orb)]
+
+
+def route_kernel(
+    pair_dev, n_orb, width, table_in, fields, orbitals, *refs
+):
+    *sends, own, work, table, held, seen, load, pieces, crossing, chosen, sems, table_sem = refs
+    orb_dev, slab_rows, _ = orbitals.shape
+    pairs = table.shape[0] * pair_dev
+    cap = own.shape[0]
+    slots = crossing_slots(cap, n_orb)
+    me = lax.axis_index("orb")
+    slab = lax.axis_index("slab")
+    base, first_row = me * orb_dev, slab * slab_rows
+    table_copy = pltpu.make_async_copy(table_in, table, table_sem)
+    table_copy.start()
+    for k in range(orb_dev + 1):
+        seen[k] = 0
+    for k in range(n_orb):
+        load[k] = 0
+    for k in range(n_orb * n_orb):
+        pieces[k] = 0
+        crossing[k] = 0
+    table_copy.wait()
+
+    def copy_of(index, slot):
+        return pltpu.make_async_copy(orbitals.at[index], held.at[slot], sems.at[slot])
+
+    def scan(g, terms):
+        row, off = g // pair_dev, (g % pair_dev) * FIELDS
+        left, right = table[row, off], table[row, off + 1]
+        x, y, z = (table[row, off + 2 + d] for d in range(3))
+        a, b = quotient(left, orb_dev), quotient(right, orb_dev)
+        weight = jnp.where((a ^ b) == 1, 0, 2)
+        load_a, load_b = load[a], load[b]
+        cost_a = jnp.where(load_a < cap, load_a + weight * pieces[b * n_orb + a], BIG)
+        cost_b = jnp.where(load_b < cap, load_b + weight * pieces[a * n_orb + b], BIG)
+        chosen[0] = jnp.where(cost_a <= cost_b, a, b)
+
+        @pl.when((load_a >= cap) & (load_b >= cap))
+        def _():
+            least = jnp.int32(0)
+            for o in range(1, n_orb):
+                least = jnp.where(load[o] < load[least], o, least)
+            chosen[0] = least
+
+        k = chosen[0]
+        j = load[k]
+        load[k] = j + 1
+        here = fields[x]
+        meets = in_box(first_row, x) | in_box(first_row + slab_rows - 1, x)
+
+        def cross(o, used):
+            at = o * n_orb + k
+            taken = crossing[at]
+            crossing[at] = taken + jnp.where(used, here, 0)
+            pieces[at] = pieces[at] + jnp.where(used, 1, 0)
+            count = (taken >> (width * slab)) & 15 if width else taken
+            d = o ^ k
+            begin, room = jnp.int32(cap), jnp.int32(slots[0])
+            for n in range(1, len(slots)):
+                begin = jnp.where(d == n + 1, cap + sum(slots[:n]), begin)
+                room = jnp.where(d == n + 1, slots[n], room)
+            return begin + jnp.minimum(count, room - 1)
+
+        away_a = a != k
+        away_b = (b != k) & (a != b)
+        at_a = cross(a, away_a)
+        at_b = cross(b, away_b)
+        mine = k == me
+
+        @pl.when(mine)
+        def _():
+            both_away = away_a & away_b
+            work[OWN_A, j] = jnp.where(both_away | (away_a & (a == b)), at_a, j)
+            work[OWN_B, j] = jnp.where(away_b, at_b, jnp.where(away_a & (a != b), at_a, -1))
+            work[OWN_MEETS, j] = jnp.where(meets, 1, 0)
+            work[OWN_X, j] = x
+            work[OWN_Y, j] = y
+            work[OWN_Z, j] = z
+
+        has_left, has_right = a == me, b == me
+        live = (has_left | has_right) & meets
+        both = has_left & has_right
+        first = jnp.where(has_left, left, right) - base
+        second = jnp.where(both, right - base, -1)
+        work[PAIR, terms] = jnp.where(mine, j, jnp.where(has_left, at_a, at_b))
+        work[SLOT, terms] = first
+        work[SECOND, terms] = second
+        work[START_X, terms] = x
+        work[START_Y, terms] = y
+        work[START_Z, terms] = z
+
+        @pl.when(live)
+        def _():
+            copy_of(first, 2 * terms).start()
+
+            @pl.when(both)
+            def _():
+                copy_of(second, 2 * terms + 1).start()
+
+        for which, index, used in ((FIRST_A, first, live), (FIRST_B, second, live & both)):
+            index = jnp.where(used, index, orb_dev)
+            work[which, terms] = seen[index]
+            seen[index] = 1
+        return terms + jnp.where(live, 1, 0)
+
+    terms = lax.fori_loop(0, pairs, scan, jnp.int32(0), unroll=2)
+    over = jnp.int32(0)
+    for o in range(n_orb):
+        for k in range(n_orb):
+            if o != k:
+                room, count = slots[(o ^ k) - 1], crossing[o * n_orb + k]
+                for f in range(8 if width else 1):
+                    held_here = (count >> (width * f)) & 15 if width else count
+                    over = over | jnp.where(held_here > room, 1, 0)
+    work[COUNT, 0] = terms
+    work[COUNT, 1] = first_row
+    work[COUNT, 2] = over
+    mark_last(work, seen, terms, orb_dev)
+
+    @pl.loop(0, terms)
+    def _(i):
+        def put(full):
+            mask = row_mask(first_row, slab_rows, work[START_X, i])
+            folded = [
+                jnp.where(mask, piece, 0.0)
+                for piece in fold(full, work[START_Y, i], work[START_Z, i])
+            ]
+
+            def store(ref, n):
+                for q, piece in enumerate(folded):
+                    ref[n, :, q * LANES : (q + 1) * LANES] = piece
+
+            pick([own, *sends], work[PAIR, i], store)
+
+        copy_of(work[SLOT, i], 2 * i).wait()
+
+        @pl.when(work[SECOND, i] >= 0)
+        def _():
+            copy_of(work[SECOND, i], 2 * i + 1).wait()
+            put(held[2 * i] * held[2 * i + 1])
+
+        @pl.when(work[SECOND, i] < 0)
+        def _():
+            put(held[2 * i])
+
+
+def density_kernel(work, *refs):
+    *parts, out, side = refs
+
+    def load(ref, n):
+        side[...] = ref[n]
+
+    @pl.loop(0, out.shape[0])
+    def _(j):
+        a, b = work[OWN_A, j], work[OWN_B, j]
+        meets = work[OWN_MEETS, j] != 0
+
+        @pl.when(meets)
+        def _():
+            pick(parts, a, load)
+
+        def both(ref, n):
+            out[j] = side[...] * ref[n]
+
+        @pl.when(meets & (b >= 0))
+        def _():
+            pick(parts, b, both)
+
+        @pl.when(meets & (b < 0))
+        def _():
+            out[j] = side[...]
+
+        @pl.when(jnp.logical_not(meets))
+        def _():
+            out[j] = jnp.zeros(out.shape[1:], jnp.float32)
+
+
+def plane_solve_kernel(received, cleared, *refs):
+    del cleared
+    mats, weights, out = refs[:12], *refs[12:]
+    n_slab, pair_dev, rows, _ = received.shape
+    half = n_slab // 2
+    for i in range(pair_dev):
+        density = jnp.concatenate(
+            [received[s, i] + received[s + half, i] for s in range(half)], axis=0
+        )
+        m = [(mats[k][i], mats[k + 1][i]) for k in range(0, 12, 2)]
+        potential = potential_of(density, *m, weights[...])
+        for s in range(half):
+            part = potential[s * rows : (s + 1) * rows]
+            out[s, i] = part
+            out[s + half, i] = part
+
+
+def term_kernel(work, potential, *refs):
+    count = (len(refs) - 1) // 2
+    parts, outs, term = refs[:count], refs[count : 2 * count], refs[-1]
+
+    def store(ref, n):
+        ref[n] = term[...]
+
+    @pl.loop(0, potential.shape[0])
+    def _(j):
+        a, b = work[OWN_A, j], work[OWN_B, j]
+        meets = work[OWN_MEETS, j] != 0
+
+        def times(ref, n):
+            term[...] = potential[j] * ref[n]
+
+        @pl.when(meets & (b >= 0))
+        def _():
+            for source, target in ((a, b), (b, a)):
+                pick(parts, source, times)
+                pick(outs, target, store)
+
+        @pl.when(meets & (b < 0))
+        def _():
+            term[...] = potential[j]
+            pick(outs, a, store)
+
+
+def plane_place_kernel(work, orbitals, zeros, *refs):
+    del zeros
+    *parts, out, held, acc, term, sems, out_sems = refs
+
+    def load(ref, n):
+        term[...] = ref[n]
+
+    def fetch(at):
+        pick(parts, at, load)
+        return term[...]
+
+    place_terms(work, orbitals, fetch, out, held, acc, sems, out_sems)
 
 
 def body(orbitals, pair_list, box_start):
@@ -426,78 +699,186 @@
         jnp.broadcast_to(row, (devices, width)), axes, split_axis=0, concat_axis=0, tiled=True
     )
 
-    outgoing, work = pl.pallas_call(
-        functools.partial(pack_kernel, pair_dev),
-        out_shape=[
-            jax.ShapeDtypeStruct(slots, jnp.float32),
-            jax.ShapeDtypeStruct((12, -(-(2 * pairs + 1) // LANES) * LANES), jnp.int32),
-        ],
-        in_specs=[free, hbm],
-        out_specs=[hbm, smem],
+    cap = pairs // n_orb
+    crossings = crossing_slots(cap, n_orb)
+    fields, field_bits = slab_fields(n_slab, slab_rows)
+    lists = jax.ShapeDtypeStruct((FULL_ROWS, -(-(2 * pairs + 1) // LANES) * LANES), jnp.int32)
+    one_plane = jax.ShapeDtypeStruct((cap, slab_rows, PACKED), jnp.float32)
+    crossed = [jax.ShapeDtypeStruct((n, slab_rows, PACKED), jnp.float32) for n in crossings]
+    one_slot = pltpu.VMEM((slab_rows, PACKED), jnp.float32)
+
+    def cross(parts):
+        return [
+            lax.ppermute(part, "orb", [(o, o ^ (n + 1)) for o in range(n_orb)])
+            for n, part in reversed(list(enumerate(parts)))
+        ][::-1]
+
+    def clear(work):
+        return pl.pallas_call(
+            clear_kernel,
+            out_shape=[
+                jax.ShapeDtypeStruct(orbitals.shape, jnp.float32),
+                jax.ShapeDtypeStruct((8, LANES), jnp.int32),
+            ],
+            in_specs=[smem],
+            out_specs=[hbm, vmem],
+            scratch_shapes=[
+                pltpu.VMEM((orb_dev // CLEARS, slab_rows, cells), jnp.float32),
+                pltpu.SemaphoreType.DMA((CLEARS,)),
+            ],
+            compiler_params=grant(16),
+            cost_estimate=pl.CostEstimate(
+                flops=0, bytes_accessed=orbitals.size * 4, transcendentals=0
+            ),
+            name="clear",
+        )(work)
+
+    *sends, own_pieces, work = pl.pallas_call(
+        functools.partial(route_kernel, pair_dev, n_orb, field_bits),
+        out_shape=[*crossed, one_plane, lists],
+        in_specs=[free, smem, hbm],
+        out_specs=[vmem] * n_orb + [smem],
         scratch_shapes=[
             pltpu.SMEM((devices, width), jnp.int32),
             held,
-            pltpu.VMEM((pairs + 1, slab_rows, PACKED), jnp.float32),
             pltpu.SMEM((orb_dev + 1,), jnp.int32),
+            pltpu.SMEM((n_orb,), jnp.int32),
+            pltpu.SMEM((n_orb * n_orb,), jnp.int32),
+            pltpu.SMEM((n_orb * n_orb,), jnp.int32),
+            pltpu.SMEM((1,), jnp.int32),
             pltpu.SemaphoreType.DMA((2 * pairs,)),
-            pltpu.SemaphoreType.DMA((pairs,)),
             pltpu.SemaphoreType.DMA,
         ],
         compiler_params=grant(56),
-        name="pack",
-    )(table, orbitals)
-    received = lax.all_to_all(outgoing, axes, split_axis=0, concat_axis=0, tiled=True)
-
-    zeros, cleared = pl.pallas_call(
-        clear_kernel,
-        out_shape=[
-            jax.ShapeDtypeStruct(orbitals.shape, jnp.float32),
-            jax.ShapeDtypeStruct((8, LANES), jnp.int32),
-        ],
-        in_specs=[smem],
-        out_specs=[hbm, vmem],
-        scratch_shapes=[
-            pltpu.VMEM((orb_dev // CLEARS, slab_rows, cells), jnp.float32),
-            pltpu.SemaphoreType.DMA((CLEARS,)),
-        ],
-        compiler_params=grant(16),
-        cost_estimate=pl.CostEstimate(
-            flops=0, bytes_accessed=orbitals.size * 4, transcendentals=0
-        ),
-        name="clear",
-    )(work)
-
-    solved = pl.pallas_call(
-        functools.partial(solve_kernel, orb_dev),
-        out_shape=jax.ShapeDtypeStruct((n_slab, n_orb, pair_dev, slab_rows, PACKED), jnp.float32),
-        in_specs=[smem] + [vmem] * 15,
-        out_specs=vmem,
-        compiler_params=grant(16),
-        name="solve",
-    )(
-        pair_list,
-        received.reshape(n_slab, n_orb, pair_dev, slab_rows, PACKED),
-        cleared,
-        *matrices(box_start),
-        jnp.asarray(spectrum()),
+        name="route",
+    )(table, jnp.asarray(fields), orbitals)
+
+    def in_planes(table, orbitals, box_start, work, own_pieces, *sends):
+        del table, box_start
+        arrived = cross(sends)
+        zeros, cleared = clear(work)
+        starts = lax.dynamic_slice(
+            work, (OWN_X, lax.axis_index("slab") * pair_dev), (3, pair_dev)
+        ).T
+        mats = matrices(starts)
+        density = pl.pallas_call(
+            density_kernel,
+            out_shape=one_plane,
+            in_specs=[smem] + [vmem] * n_orb,
+            out_specs=vmem,
+            scratch_shapes=[one_slot],
+            compiler_params=grant(8),
+            name="density",
+        )(work, own_pieces, *arrived)
+        received = lax.all_to_all(density, "slab", split_axis=0, concat_axis=0, tiled=True)
+        by_slab = (n_slab, pair_dev, slab_rows, PACKED)
+        solved = pl.pallas_call(
+            plane_solve_kernel,
+            out_shape=jax.ShapeDtypeStruct(by_slab, jnp.float32),
+            in_specs=[vmem] * 15,
+            out_specs=vmem,
+            compiler_params=grant(16),
+            name="solve",
+        )(received.reshape(by_slab), cleared, *mats, jnp.asarray(spectrum()))
+        potential = lax.all_to_all(
+            solved.reshape(one_plane.shape), "slab", split_axis=0, concat_axis=0, tiled=True
+        )
+        own_terms, *sends = pl.pallas_call(
+            term_kernel,
+            out_shape=[one_plane, *crossed],
+            in_specs=[smem, vmem] + [vmem] * n_orb,
+            out_specs=[vmem] * n_orb,
+            scratch_shapes=[one_slot],
+            compiler_params=grant(8),
+            name="terms",
+        )(work, potential, own_pieces, *arrived)
+        arrived = cross(sends)
+        return pl.pallas_call(
+            plane_place_kernel,
+            out_shape=jax.ShapeDtypeStruct(orbitals.shape, jnp.float32),
+            in_specs=[smem, hbm, hbm] + [vmem] * n_orb,
+            out_specs=hbm,
+            scratch_shapes=[
+                held,
+                pltpu.VMEM(orbitals.shape, jnp.float32),
+                one_slot,
+                pltpu.SemaphoreType.DMA((2 * pairs,)),
+                pltpu.SemaphoreType.DMA((orb_dev,)),
+            ],
+            input_output_aliases={2: 0},
+            compiler_params=grant(52),
+            name="place",
+        )(work, orbitals, zeros, own_terms, *arrived)
+
+    def direct(table, orbitals, box_start, *unused):
+        del unused
+        outgoing, work = pl.pallas_call(
+            functools.partial(pack_kernel, pair_dev),
+            out_shape=[
+                jax.ShapeDtypeStruct(slots, jnp.float32),
+                lists,
+            ],
+            in_specs=[free, hbm],
+            out_specs=[hbm, smem],
+            scratch_shapes=[
+                pltpu.SMEM((devices, width), jnp.int32),
+                held,
+                pltpu.VMEM((pairs + 1, slab_rows, PACKED), jnp.float32),
+                pltpu.SMEM((orb_dev + 1,), jnp.int32),
+                pltpu.SemaphoreType.DMA((2 * pairs,)),
+                pltpu.SemaphoreType.DMA((pairs,)),
+                pltpu.SemaphoreType.DMA,
+            ],
+            compiler_params=grant(56),
+            name="pack",
+        )(table, orbitals)
+        received = lax.all_to_all(outgoing, axes, split_axis=0, concat_axis=0, tiled=True)
+
+        zeros, cleared = clear(work)
+
+        solved = pl.pallas_call(
+            functools.partial(solve_kernel, orb_dev),
+            out_shape=jax.ShapeDtypeStruct((n_slab, n_orb, pair_dev, slab_rows, PACKED), jnp.float32),
+            in_specs=[smem] + [vmem] * 15,
+            out_specs=vmem,
+            compiler_params=grant(16),
+            name="solve",
+        )(
+            pair_list,
+            received.reshape(n_slab, n_orb, pair_dev, slab_rows, PACKED),
+            cleared,
+            *matrices(box_start),
+            jnp.asarray(spectrum()),
+        )
+        returned = lax.all_to_all(solved.reshape(slots), axes, split_axis=0, concat_axis=0, tiled=True)
+
+        return pl.pallas_call(
+            place_kernel,
+            out_shape=jax.ShapeDtypeStruct(orbitals.shape, jnp.float32),
+            in_specs=[smem, hbm, vmem, hbm],
+            out_specs=hbm,
+            scratch_shapes=[
+                held,
+                pltpu.VMEM(orbitals.shape, jnp.float32),
+                pltpu.SemaphoreType.DMA((2 * pairs,)),
+                pltpu.SemaphoreType.DMA((orb_dev,)),
+            ],
+            input_output_aliases={3: 0},
+            compiler_params=grant(52),
+            name="place",
+        )(work, orbitals, returned, zeros)
+
+    return lax.cond(
+        work[COUNT, 2] > 0,
+        direct,
+        in_planes,
+        table,
+        orbitals,
+        box_start,
+        work,
+        own_pieces,
+        *sends,
     )
-    returned = lax.all_to_all(solved.reshape(slots), axes, split_axis=0, concat_axis=0, tiled=True)
-
-    return pl.pallas_call(
-        place_kernel,
-        out_shape=jax.ShapeDtypeStruct(orbitals.shape, jnp.float32),
-        in_specs=[smem, hbm, vmem, hbm],
-        out_specs=hbm,
-        scratch_shapes=[
-            held,
-            pltpu.VMEM(orbitals.shape, jnp.float32),
-            pltpu.SemaphoreType.DMA((2 * pairs,)),
-            pltpu.SemaphoreType.DMA((orb_dev,)),
-        ],
-        input_output_aliases={3: 0},
-        compiler_params=grant(52),
-        name="place",
-    )(work, orbitals, returned, zeros)
 
 
 def solution(mesh):

time: 86.3 us -> 81.3 us (0.942)
  blocking collectives: 29.3 us -> 24 us
  Pallas kernels: 15.6 us -> 19 us
  waiting for transfers between devices: 14.1 us -> 11 us
  local copies, waits for them, and re-layouts: 3.34 us -> 1.45 us
  starting transfers between devices: 9.96 us -> 11.4 us
    all_to_all x2 -> x1, waiting for transfers between devices: 14.1 us -> 1.13 us  [in_planes(): lax.all_to_all(density, 'slab', split_axis=0, concat_axis=0, tiled=True)]
    ppermute x0 -> x6, waiting for transfers between devices: none -> 9.84 us  [cross(): lax.ppermute(part, 'orb', [(o, o ^ n + 1) for o in range(n_orb)])]
    ppermute x0 -> x6, starting transfers between devices: none -> 8.01 us  [cross(): lax.ppermute(part, 'orb', [(o, o ^ n + 1) for o in range(n_orb)])]
    all_to_all x2 -> x1, starting transfers between devices: 9.96 us -> 3.41 us  [in_planes(): lax.all_to_all(density, 'slab', split_axis=0, concat_axis=0, tiled=True)]
    all_to_all x1 -> x2, blocking collectives: 29.3 us -> 24 us  [the longest x1 14.3 us: body(): lax.all_to_all(jnp.broadcast_to(row, (devices, width)), axes, split_axis=...]
    pallas_call x4 -> x6, Pallas kernels: 15.6 us -> 19 us  [the longest x1 6.2 us: body(): pl.pallas_call(functools.partial(route_kernel, pair_dev, n_orb, field_bit...]
    unnamed x10 -> x6, local copies, waits for them, and re-layouts: 1.31 us -> 0.01 us
  transfers between devices with their start and end apart: 2 -> 7, of which waited for: 2 -> 3; matrix products, arithmetic and copies ran while one was open for 15% -> 16% of each run, Pallas kernels for 5% -> 5%
where the time goes in v4:
time: 81.3 us; the launch traced here: 80.5 us
  blocking collectives  24 us (30%)
  Pallas kernels  19 us (23%)
  other arithmetic  12.5 us (15%)
  starting transfers between devices  11.4 us (14%)
  waiting for transfers between devices  11 us (14%)
  local copies, waits for them, and re-layouts  1.45 us (2%)
  between operations  0.87 us (1%)
    all_to_all x1, blocking collectives, body(): lax.all_to_all(jnp.broadcast_to(row, (devices, width)), axes, split_axis=...  14.3 us
    convert_element_type x6, other arithmetic, halves(): return (high.astype(jnp.bfloat16), (full - high).astype(jnp.bfloat16))  10.4 us
    ppermute x6, waiting for transfers between devices, cross(): lax.ppermute(part, 'orb', [(o, o ^ n + 1) for o in range(n_orb)])  9.84 us
    all_to_all x1, blocking collectives, in_planes(): lax.all_to_all(solved.reshape(one_plane.shape), 'slab', split_axis=0, con...  9.75 us
    ppermute x6, starting transfers between devices, cross(): lax.ppermute(part, 'orb', [(o, o ^ n + 1) for o in range(n_orb)])  8.01 us
    pallas_call x1, Pallas kernels, body(): pl.pallas_call(functools.partial(route_kernel, pair_dev, n_orb, field_bit...  6.2 us
    pallas_call x1, Pallas kernels, clear(): pl.pallas_call(clear_kernel, out_shape=[jax.ShapeDtypeStruct(orbitals.sha...  4.18 us
    pallas_call x1, Pallas kernels, in_planes(): pl.pallas_call(plane_place_kernel, out_shape=jax.ShapeDtypeStruct(orbital...  3.47 us
  transfers between devices with their start and end apart: 7, of which 3 were waited for; matrix products, arithmetic and copies ran while one was open for 16% of the time, Pallas kernels for 5%

profile of v4, /device:TPU:0, one launch (start us, length us, event | category | flops | bytes accessed | tf_op | source)
XLA Modules:
  0.0 80.5 jit_solution(3889976171408122042)
XLA Ops:
  0.0 0.0 copy-start.2
  0.0 0.0 copy-start.3
  0.0 0.0 copy-start.4
  0.0 0.8 %pad_add_fusion = s32[1,5]{1,0:T(1,128)S(1)} fusion(s32[1,3]{1,0:T(1,128)} %param.10, s32[1,2]{1,0:T(1,128)} %param.9), kind=kLoop, calls=%fused_computation.194 | loop fusion | flops 5 | bytes 40 | tf_op jit(solution)/shard_map/concatenate | solution.py:695
  0.8 14.3 %all_to_all.26 = s32[32,1,128]{2,1,0:T(1,128)S(1)} all-to-all(s32[32,1,128]{2,1,0:T(1,128)S(1)} %broadcast_in_dim.33), channel_id=1, replica_groups=mesh['slab'=8,'orb'=4] {'slab','orb'}, dimensions={0} | all-to-all | bytes 32768 | tf_op jit(solution)/shard_map/all_to_all | solution.py:698
  15.1 6.2 %route.1 = (f32[6,8,1024]{2,1,0:T(8,128)S(1)}, f32[4,8,1024]{2,1,0:T(8,128)}, f32[4,8,1024]{2,1,0:T(8,128)}, f32[8,8,1024]{2,1,0:T(8,128)S(1)}, s32[24,128]{1,0:T(8,128)S(1)}) custom-call(s32[32,128]{1,0:T(8,128)S(1)} %bitcast.19, s32[64]{0:T(128)} %constant.166.clone.fields, f32[64,8,4096]{2,1,0:T(8,128)} %orbitals.1), custom_call_target="tpu_custom_call" | custom-call | tf_op jit(solution)/shard_map/route/pallas_call | solution.py:736
  21.3 0.6 slice.21
  22.6 0.0 copy-done.2
  22.6 0.0 copy-done.3
  22.6 0.0 copy-done.4
  22.6 57.8 %conditional.1 = (f32[64,8,4096]{2,1,0:T(8,128)}) conditional(s32[]{:T(128)} %bitcast.12, (s32[24,128]{1,0:T(8,128)S(1)}, f32[6,8,1024]{2,1,0:T(8,128)S(1)}, f32[4,8,1024]{2,1,0:T(8,128)}, f32[4,8,1024]{2,1,0:T(8,128)}, f32[8,8,1024]{2,1,0:T(8,128)S(1)}, /*index=5*/f32[384,384]{1,0:T(8,128)S(1)}, f32[64,8,4096]{2,1,0:T(8,128)}) %tuple.41, ...), branch_computations={%region_0.1_spmd, %region_1.2_spmd} | conditional | flops 7726774 | bytes 15622344 | solution.py:871
  22.6 0.9 %collective-permute-start.1 = (f32[4,8,1024]{2,1,0:T(8,128)}, f32[4,8,1024]{2,1,0:T(8,128)S(1)}, u32[]{:S(2)}, u32[]{:S(2)}) collective-permute-start(f32[4,8,1024]{2,1,0:T(8,128)} %get-tuple-element.37), channel_id=1, source_target_pairs={{0,2},{1,3},{2,0},{3,1},{4,6},{5,7},{6,4},{7,5},{8,10},{9,11},{10,... | collective-permute-start | bytes 393224 | tf_op jit(solution)/shard_map/cond/branch_0_fun/ppermute | solution.py:712
  23.5 2.6 %collective-permute-start.2 = (f32[4,8,1024]{2,1,0:T(8,128)}, f32[4,8,1024]{2,1,0:T(8,128)S(1)}, u32[]{:S(2)}, u32[]{:S(2)}) collective-permute-start(f32[4,8,1024]{2,1,0:T(8,128)} %get-tuple-element.38), channel_id=1, source_target_pairs={{0,3},{1,2},{2,1},{3,0},{4,7},{5,6},{6,5},{7,4},{8,11},{9,10},{10,... | collective-permute-start | bytes 393224 | tf_op jit(solution)/shard_map/cond/branch_0_fun/ppermute | solution.py:712
  26.1 0.0 collective-permute-start
  26.2 0.2 dynamic-slice_reduce_fusion
  26.4 0.7 fusion.121
  27.0 0.6 and_add_fusion.1
  27.6 2.4 %fusion.60 = (bf16[1,256,512]{2,1,0:T(8,128)(2,1)S(1)}, bf16[1,256,512]{2,1,0:T(8,128)(2,1)S(1)}) fusion(s32[256]{0:T(256)S(1)} %and_add_fusion.1, s32[512]{0:T(512)S(1)} %get-tuple-element.104, pred[512]{0:T(512)(128)(4,1)S(1)} %fusion.107, s32[512]{0:T(512)S(1)} %get-tuple-element.103, s32[256]{0:T(256)S(1)} %get-tuple-element.106, s32[512]{0:T(512)S(1)} %fusion.108, ...), kind=kLoop, calls=%fused_computation.108 | loop fusion | flops 2359296 | bytes 534016 | tf_op jit(solution)/shard_map/cond/branch_0_fun/convert_element_type | solution.py:67
  30.1 2.7 %fusion.61 = (bf16[1,512,256]{2,1,0:T(8,128)(2,1)S(1)}, bf16[1,512,256]{2,1,0:T(8,128)(2,1)S(1)}) fusion(s32[256]{0:T(256)S(1)} %and_add_fusion.1, s32[512]{0:T(512)S(1)} %get-tuple-element.104, pred[512]{0:T(512)(128)(4,1)S(1)} %fusion.107, s32[512]{0:T(512)S(1)} %get-tuple-element.103, s32[256]{0:T(256)S(1)} %get-tuple-element.106, s32[512]{0:T(512)S(1)} %fusion.108, ...), kind=kLoop, calls=%fused_computation.109 | loop fusion | flops 2359296 | bytes 534016 | tf_op jit(solution)/shard_map/cond/branch_0_fun/convert_element_type | solution.py:67
  32.8 0.7 fusion.116
  33.4 1.9 %fusion.76 = (bf16[1,384,256]{2,1,0:T(8,128)(2,1)S(1)}, bf16[1,384,256]{2,1,0:T(8,128)(2,1)S(1)}) fusion(s32[256]{0:T(256)S(1)} %get-tuple-element.109, s32[384]{0:T(512)S(1)} %get-tuple-element.107, s32[256]{0:T(256)S(1)} %get-tuple-element.110, s32[384]{0:T(512)S(1)} %get-tuple-element.108), kind=kLoop, calls=%fused_computation.126 | loop fusion | flops 1474560 | bytes 398336 | tf_op jit(solution)/shard_map/cond/branch_0_fun/convert_element_type | solution.py:67
  35.3 1.8 %fusion.77 = (bf16[1,256,384]{2,1,0:T(8,128)(2,1)S(1)}, bf16[1,256,384]{2,1,0:T(8,128)(2,1)S(1)}) fusion(s32[256]{0:T(256)S(1)} %get-tuple-element.109, s32[384]{0:T(512)S(1)} %get-tuple-element.107, s32[384]{0:T(512)S(1)} %get-tuple-element.108, s32[256]{0:T(256)S(1)} %get-tuple-element.110), kind=kLoop, calls=%fused_computation.127 | loop fusion | flops 1474560 | bytes 398336 | tf_op jit(solution)/shard_map/cond/branch_0_fun/convert_element_type | solution.py:67
  37.2 0.0 collective-permute-done.1.refs_2_
  37.2 0.0 collective-permute-done.2.refs_3_
  37.2 0.2 collective-permute-done.refs_1_
  37.4 1.8 %density.1 = f32[8,8,1024]{2,1,0:T(8,128)} custom-call(s32[24,128]{1,0:T(8,128)S(1)} %get-tuple-element.32.work, f32[8,8,1024]{2,1,0:T(8,128)S(1)} %get-tuple-element.35.refs_0_, f32[6,8,1024]{2,1,0:T(8,128)S(1)} %collective-permute-done.refs_1_, f32[4,8,1024]{2,1,0:T(8,128)S(1)} %collective-permute-done.1.refs_2_, ...), custom_call_target="tpu_custom_call" | custom-call | tf_op jit(solution)/shard_map/cond/branch_0_fun/density/pallas_call | solution.py:764
  39.3 3.4 %all-to-all-start.2 = ((f32[8,8,1024]{2,1,0:T(8,128)}), f32[8,8,1024]{2,1,0:T(8,128)S(1)}, u32[]{:S(2)}, u32[]{:S(2)}) async-start(f32[8,8,1024]{2,1,0:T(8,128)} %density.1), calls=%async_computation.2 | async-start | bytes 524288 | tf_op jit(solution)/shard_map/cond/branch_0_fun/all_to_all | solution.py:773
  42.7 0.7 fusion.99
  43.4 4.2 %clear.2 = (f32[64,8,4096]{2,1,0:T(8,128)}, s32[8,128]{1,0:T(8,128)S(1)}) custom-call(s32[24,128]{1,0:T(8,128)S(1)} %get-tuple-element.32.work), custom_call_target="tpu_custom_call" | custom-call | bytes 8388608 | tf_op jit(solution)/shard_map/cond/branch_0_fun/clear/pallas_call | solution.py:717
  47.6 0.8 %fusion.92 = (bf16[1,48,32]{2,1,0:T(8,128)(2,1)S(1)}, bf16[1,48,32]{2,1,0:T(8,128)(2,1)S(1)}) fusion(s32[]{:T(128)} %bitcast.1, s32[48]{0:T(128)S(1)} %iota_add_fusion.1), kind=kLoop, calls=%fused_computation.147 | loop fusion | flops 24576 | bytes 6340 | tf_op jit(solution)/shard_map/cond/branch_0_fun/convert_element_type | solution.py:67
  48.4 1.1 %all-to-all-done.2 = f32[8,8,1024]{2,1,0:T(8,128)S(1)} async-done(((f32[8,8,1024]{2,1,0:T(8,128)}), f32[8,8,1024]{2,1,0:T(8,128)S(1)}, u32[]{:S(2)}, u32[]{:S(2)}) %all-to-all-start.2) | async-done | bytes 262176 | tf_op jit(solution)/shard_map/cond/branch_0_fun/all_to_all | solution.py:773
  49.5 2.1 %solve.2 = f32[8,1,8,1024]{3,2,1,0:T(8,128)S(1)} custom-call(f32[8,1,8,1024]{3,2,1,0:T(8,128)S(1)} %bitcast.17, s32[8,128]{1,0:T(8,128)S(1)} %get-tuple-element.39.cleared, bf16[1,48,32]{2,1,0:T(8,128)(2,1)S(1)} %get-tuple-element.102.refs_0_, bf16[1,48,32]{2,1,0:T(8,128)(2,1)S(1)} %get-tuple-element.101.refs_1_, ...), custom_call_target="tpu_custom_call" | custom-call | tf_op jit(solution)/shard_map/cond/branch_0_fun/solve/pallas_call | solution.py:775
  51.6 9.8 %all_to_all.24.potential = f32[8,8,1024]{2,1,0:T(8,128)S(1)} all-to-all(f32[8,8,1024]{2,1,0:T(8,128)S(1)} %bitcast.18), channel_id=1, replica_groups=mesh['slab'=8,'orb'=4] {'slab'}, dimensions={0} | all-to-all | bytes 524288 | tf_op jit(solution)/shard_map/cond/branch_0_fun/all_to_all | solution.py:783
  61.4 1.2 %terms.1 = (f32[8,8,1024]{2,1,0:T(8,128)S(1)}, f32[6,8,1024]{2,1,0:T(8,128)S(1)}, f32[4,8,1024]{2,1,0:T(8,128)S(1)}, f32[4,8,1024]{2,1,0:T(8,128)S(1)}) custom-call(s32[24,128]{1,0:T(8,128)S(1)} %get-tuple-element.32.work, f32[8,8,1024]{2,1,0:T(8,128)S(1)} %all_to_all.24.potential, f32[8,8,1024]{2,1,0:T(8,128)S(1)} %get-tuple-element.35.refs_0_, ...), custom_call_target="tpu_custom_call" | custom-call | tf_op jit(solution)/shard_map/cond/branch_0_fun/terms/pallas_call | solution.py:786
  62.6 1.8 %collective-permute-start.3 = (f32[6,8,1024]{2,1,0:T(8,128)S(1)}, f32[6,8,1024]{2,1,0:T(8,128)S(1)}, u32[]{:S(2)}, u32[]{:S(2)}) collective-permute-start(f32[6,8,1024]{2,1,0:T(8,128)S(1)} %get-tuple-element.42), channel_id=1, source_target_pairs={{0,1},{1,0},{2,3},{3,2},{4,5},{5,4},{6,7},{7,6},{8,9},{9,8},{10,11... | collective-permute-start | bytes 589832 | tf_op jit(solution)/shard_map/cond/branch_0_fun/ppermute | solution.py:712
  64.4 0.1 collective-permute-start.4
  64.5 2.5 %collective-permute-start.5 = (f32[4,8,1024]{2,1,0:T(8,128)S(1)}, f32[4,8,1024]{2,1,0:T(8,128)S(1)}, u32[]{:S(2)}, u32[]{:S(2)}) collective-permute-start(f32[4,8,1024]{2,1,0:T(8,128)S(1)} %get-tuple-element.44), channel_id=1, source_target_pairs={{0,3},{1,2},{2,1},{3,0},{4,7},{5,6},{6,5},{7,4},{8,11},{9,10},{10,... | collective-permute-start | bytes 393224 | tf_op jit(solution)/shard_map/cond/branch_0_fun/ppermute | solution.py:712
  67.1 9.6 %collective-permute-done.4.refs_2_ = f32[4,8,1024]{2,1,0:T(8,128)S(1)} collective-permute-done((f32[4,8,1024]{2,1,0:T(8,128)S(1)}, f32[4,8,1024]{2,1,0:T(8,128)S(1)}, u32[]{:S(2)}, u32[]{:S(2)}) %collective-permute-start.4) | collective-permute-done | bytes 131104 | tf_op jit(solution)/shard_map/cond/branch_0_fun/ppermute | solution.py:712
  76.7 0.0 collective-permute-done.5.refs_3_
  76.7 0.0 collective-permute-done.3.refs_1_
  76.7 3.5 %place.2 = f32[64,8,4096]{2,1,0:T(8,128)} custom-call(s32[24,128]{1,0:T(8,128)S(1)} %get-tuple-element.32.work, f32[64,8,4096]{2,1,0:T(8,128)} %get-tuple-element.33.orbitals, f32[64,8,4096]{2,1,0:T(8,128)} %get-tuple-element.34.zeros, f32[8,8,1024]{2,1,0:T(8,128)S(1)} %get-tuple-element.41.refs_0_, ...), custom_call_target="tpu_custom_call", output_to_operand_aliasing={{}: (2, {})} | custom-call | tf_op jit(solution)/shard_map/cond/branch_0_fun/place/pallas_call | solution.py:796
  (8 shorter events, 0.0 us)
Async XLA Ops:
  0.0 22.6 %copy-start.2 = (f32[384,384]{1,0:T(8,128)S(1)}, f32[384,384]{1,0:T(8,128)}, u32[]{:S(2)}) copy-start(f32[384,384]{1,0:T(8,128)} %constant.167.clone) | copy-start | bytes 1769476
  0.0 22.6 %copy-start.3 = (s32[1,3]{1,0:T(1,128)S(1)}, s32[1,3]{1,0:T(1,128)}, u32[]{:S(2)}) copy-start(s32[1,3]{1,0:T(1,128)} %param.10) | copy-start | bytes 40
  0.0 22.6 %copy-start.4 = (s32[1,2]{1,0:T(1,128)S(1)}, s32[1,2]{1,0:T(1,128)}, u32[]{:S(2)}) copy-start(s32[1,2]{1,0:T(1,128)} %param.9) | copy-start | bytes 28
  22.6 14.6 %collective-permute-start.1 = (f32[4,8,1024]{2,1,0:T(8,128)}, f32[4,8,1024]{2,1,0:T(8,128)S(1)}, u32[]{:S(2)}, u32[]{:S(2)}) collective-permute-start(f32[4,8,1024]{2,1,0:T(8,128)} %get-tuple-element.37), channel_id=1, source_target_pairs={{0,2},{1,3},{2,0},{3,1},{4,6},{5,7},{6,4},{7,5},{8,10},{9,11},{10,... | collective-permute-start | bytes 393224 | tf_op jit(solution)/shard_map/cond/branch_0_fun/ppermute | solution.py:712
  23.5 13.7 %collective-permute-start.2 = (f32[4,8,1024]{2,1,0:T(8,128)}, f32[4,8,1024]{2,1,0:T(8,128)S(1)}, u32[]{:S(2)}, u32[]{:S(2)}) collective-permute-start(f32[4,8,1024]{2,1,0:T(8,128)} %get-tuple-element.38), channel_id=1, source_target_pairs={{0,3},{1,2},{2,1},{3,0},{4,7},{5,6},{6,5},{7,4},{8,11},{9,10},{10,... | collective-permute-start | bytes 393224 | tf_op jit(solution)/shard_map/cond/branch_0_fun/ppermute | solution.py:712
  26.1 11.3 %collective-permute-start = (f32[6,8,1024]{2,1,0:T(8,128)S(1)}, f32[6,8,1024]{2,1,0:T(8,128)S(1)}, u32[]{:S(2)}, u32[]{:S(2)}) collective-permute-start(f32[6,8,1024]{2,1,0:T(8,128)S(1)} %get-tuple-element.36), channel_id=1, source_target_pairs={{0,1},{1,0},{2,3},{3,2},{4,5},{5,4},{6,7},{7,6},{8,9},{9,8},{10,11... | collective-permute-start | bytes 589832 | tf_op jit(solution)/shard_map/cond/branch_0_fun/ppermute | solution.py:712
  39.3 10.3 %all-to-all-start.2 = ((f32[8,8,1024]{2,1,0:T(8,128)}), f32[8,8,1024]{2,1,0:T(8,128)S(1)}, u32[]{:S(2)}, u32[]{:S(2)}) async-start(f32[8,8,1024]{2,1,0:T(8,128)} %density.1), calls=%async_computation.2 | async-start | bytes 524288 | tf_op jit(solution)/shard_map/cond/branch_0_fun/all_to_all | solution.py:773
  62.6 14.1 %collective-permute-start.3 = (f32[6,8,1024]{2,1,0:T(8,128)S(1)}, f32[6,8,1024]{2,1,0:T(8,128)S(1)}, u32[]{:S(2)}, u32[]{:S(2)}) collective-permute-start(f32[6,8,1024]{2,1,0:T(8,128)S(1)} %get-tuple-element.42), channel_id=1, source_target_pairs={{0,1},{1,0},{2,3},{3,2},{4,5},{5,4},{6,7},{7,6},{8,9},{9,8},{10,11... | collective-permute-start | bytes 589832 | tf_op jit(solution)/shard_map/cond/branch_0_fun/ppermute | solution.py:712
  64.4 12.2 %collective-permute-start.4 = (f32[4,8,1024]{2,1,0:T(8,128)S(1)}, f32[4,8,1024]{2,1,0:T(8,128)S(1)}, u32[]{:S(2)}, u32[]{:S(2)}) collective-permute-start(f32[4,8,1024]{2,1,0:T(8,128)S(1)} %get-tuple-element.43), channel_id=1, source_target_pairs={{0,2},{1,3},{2,0},{3,1},{4,6},{5,7},{6,4},{7,5},{8,10},{9,11},{10,... | collective-permute-start | bytes 393224 | tf_op jit(solution)/shard_map/cond/branch_0_fun/ppermute | solution.py:712
  64.5 12.2 %collective-permute-start.5 = (f32[4,8,1024]{2,1,0:T(8,128)S(1)}, f32[4,8,1024]{2,1,0:T(8,128)S(1)}, u32[]{:S(2)}, u32[]{:S(2)}) collective-permute-start(f32[4,8,1024]{2,1,0:T(8,128)S(1)} %get-tuple-element.44), channel_id=1, source_target_pairs={{0,3},{1,2},{2,1},{3,0},{4,7},{5,6},{6,5},{7,4},{8,11},{9,10},{10,... | collective-permute-start | bytes 393224 | tf_op jit(solution)/shard_map/cond/branch_0_fun/ppermute | solution.py:712

commit v5 on v4

--- a/solution.py
+++ b/solution.py
@@ -75,9 +75,9 @@
     return 2 * q + (g >> 1) + HALF // 2 * (g & 1)
 
 
-def matrices(box_start):
-    count = box_start.shape[0]
-    bx, by, bz = (box_start[:, d][:, None, None] for d in range(3))
+def matrices(*starts):
+    count = starts[0].shape[0]
+    bx, by, bz = (start[:, None, None] for start in starts)
 
     def x_of(k, r):
         return sine(k, r, bx)
@@ -259,8 +259,8 @@
         send(work[BLANK, i], pairs).wait()
 
 
-def clear_kernel(work, out, done, blank, sems):
-    done[...] = jnp.full(done.shape, work[COUNT, 0], jnp.int32)
+def clear_kernel(after, out, done, blank, sems):
+    done[...] = jnp.full(done.shape, after[0, 0], jnp.int32)
     count = blank.shape[0]
     blank[...] = jnp.zeros(blank.shape, jnp.float32)
     copies = [
@@ -414,12 +414,10 @@
     return value >> (by.bit_length() - 1) if by & (by - 1) == 0 else value // by
 
 
-def pick(parts, index, act):
-    begin = 0
-    for part in parts:
+def pick(begins, parts, index, act):
+    for begin, part in zip(begins, parts, strict=True):
         inside = (index >= begin) & (index < begin + part.shape[0])
         pl.when(inside)(lambda part=part, begin=begin: act(part, index - begin))
-        begin += part.shape[0]
 
 
 def slab_fields(n_slab, slab_rows):
@@ -435,7 +433,9 @@
 
 
 def crossing_slots(cap, n_orb):
-    return [max(cap * 3 // 4 if d == 1 else cap // 2, 1) for d in range(1, n_orb)]
+    near = max(cap * 3 // 4, 1)
+    far = max(cap * 3 // 8, 1)
+    return [(near, 0) if d == 1 else (far, max(cap // 2 - far, 1)) for d in range(1, n_orb)]
 
 
 def route_kernel(
@@ -445,7 +445,10 @@
     orb_dev, slab_rows, _ = orbitals.shape
     pairs = table.shape[0] * pair_dev
     cap = own.shape[0]
-    slots = crossing_slots(cap, n_orb)
+    spans = crossing_slots(cap, n_orb)
+    slots = [sum(span) for span in spans]
+    begins = [0] + [cap + sum(slots[:d]) for d in range(n_orb - 1)]
+    begins += [begins[d + 1] for d, span in enumerate(spans) if span[1]]
     me = lax.axis_index("orb")
     slab = lax.axis_index("slab")
     base, first_row = me * orb_dev, slab * slab_rows
@@ -543,17 +546,19 @@
         return terms + jnp.where(live, 1, 0)
 
     terms = lax.fori_loop(0, pairs, scan, jnp.int32(0), unroll=2)
-    over = jnp.int32(0)
+    level = jnp.int32(0)
     for o in range(n_orb):
         for k in range(n_orb):
             if o != k:
-                room, count = slots[(o ^ k) - 1], crossing[o * n_orb + k]
+                (base_room, more), count = spans[(o ^ k) - 1], crossing[o * n_orb + k]
                 for f in range(8 if width else 1):
                     held_here = (count >> (width * f)) & 15 if width else count
-                    over = over | jnp.where(held_here > room, 1, 0)
+                    if more:
+                        level = jnp.maximum(level, jnp.where(held_here > base_room, 1, 0))
+                    level = jnp.maximum(level, jnp.where(held_here > base_room + more, 2, 0))
     work[COUNT, 0] = terms
     work[COUNT, 1] = first_row
-    work[COUNT, 2] = over
+    work[COUNT, 2] = level
     mark_last(work, seen, terms, orb_dev)
 
     @pl.loop(0, terms)
@@ -569,7 +574,7 @@
                 for q, piece in enumerate(folded):
                     ref[n, :, q * LANES : (q + 1) * LANES] = piece
 
-            pick([own, *sends], work[PAIR, i], store)
+            pick(begins, [own, *sends], work[PAIR, i], store)
 
         copy_of(work[SLOT, i], 2 * i).wait()
 
@@ -583,8 +588,11 @@
             put(held[2 * i])
 
 
-def density_kernel(work, *refs):
-    *parts, out, side = refs
+def density_kernel(begins, work, *refs):
+    *parts, out, start_y, side = refs
+    pair_dev = start_y.shape[1]
+    for i in range(pair_dev):
+        start_y[0, i] = work[OWN_Y, lax.axis_index("slab") * pair_dev + i]
 
     def load(ref, n):
         side[...] = ref[n]
@@ -596,14 +604,14 @@
 
         @pl.when(meets)
         def _():
-            pick(parts, a, load)
+            pick(begins, parts, a, load)
 
         def both(ref, n):
             out[j] = side[...] * ref[n]
 
         @pl.when(meets & (b >= 0))
         def _():
-            pick(parts, b, both)
+            pick(begins, parts, b, both)
 
         @pl.when(meets & (b < 0))
         def _():
@@ -614,8 +622,7 @@
             out[j] = jnp.zeros(out.shape[1:], jnp.float32)
 
 
-def plane_solve_kernel(received, cleared, *refs):
-    del cleared
+def plane_solve_kernel(received, *refs):
     mats, weights, out = refs[:12], *refs[12:]
     n_slab, pair_dev, rows, _ = received.shape
     half = n_slab // 2
@@ -631,9 +638,11 @@
             out[s + half, i] = part
 
 
-def term_kernel(work, potential, *refs):
-    count = (len(refs) - 1) // 2
-    parts, outs, term = refs[:count], refs[count : 2 * count], refs[-1]
+def term_kernel(begins, work, potential, *refs):
+    count = (len(refs) - 2) // 2
+    parts, outs = refs[:count], refs[count : 2 * count]
+    after, term = refs[-2:]
+    after[0, 0] = work[COUNT, 0]
 
     def store(ref, n):
         ref[n] = term[...]
@@ -649,16 +658,16 @@
         @pl.when(meets & (b >= 0))
         def _():
             for source, target in ((a, b), (b, a)):
-                pick(parts, source, times)
-                pick(outs, target, store)
+                pick(begins, parts, source, times)
+                pick(begins, outs, target, store)
 
         @pl.when(meets & (b < 0))
         def _():
             term[...] = potential[j]
-            pick(outs, a, store)
-
-
-def plane_place_kernel(work, orbitals, zeros, *refs):
+            pick(begins, outs, a, store)
+
+
+def plane_place_kernel(begins, work, orbitals, zeros, *refs):
     del zeros
     *parts, out, held, acc, term, sems, out_sems = refs
 
@@ -666,7 +675,7 @@
         term[...] = ref[n]
 
     def fetch(at):
-        pick(parts, at, load)
+        pick(begins, parts, at, load)
         return term[...]
 
     place_terms(work, orbitals, fetch, out, held, acc, sems, out_sems)
@@ -700,18 +709,28 @@
     )
 
     cap = pairs // n_orb
-    crossings = crossing_slots(cap, n_orb)
+    spans = crossing_slots(cap, n_orb)
+    rooms = [sum(span) for span in spans]
+    begins = [0] + [cap + sum(rooms[:d]) for d in range(n_orb - 1)]
     fields, field_bits = slab_fields(n_slab, slab_rows)
     lists = jax.ShapeDtypeStruct((FULL_ROWS, -(-(2 * pairs + 1) // LANES) * LANES), jnp.int32)
     one_plane = jax.ShapeDtypeStruct((cap, slab_rows, PACKED), jnp.float32)
-    crossed = [jax.ShapeDtypeStruct((n, slab_rows, PACKED), jnp.float32) for n in crossings]
+
+    def crossed(level):
+        return [
+            jax.ShapeDtypeStruct((sum(span[: level + 1]), slab_rows, PACKED), jnp.float32)
+            for span in spans
+        ]
+
+    fewer = [d for d, span in enumerate(spans) if span[1]]
+    leaving = crossed(1) + [crossed(0)[d] for d in fewer]
     one_slot = pltpu.VMEM((slab_rows, PACKED), jnp.float32)
 
     def cross(parts):
         return [
             lax.ppermute(part, "orb", [(o, o ^ (n + 1)) for o in range(n_orb)])
-            for n, part in reversed(list(enumerate(parts)))
-        ][::-1]
+            for n, part in enumerate(parts)
+        ]
 
     def clear(work):
         return pl.pallas_call(
@@ -735,9 +754,9 @@
 
     *sends, own_pieces, work = pl.pallas_call(
         functools.partial(route_kernel, pair_dev, n_orb, field_bits),
-        out_shape=[*crossed, one_plane, lists],
+        out_shape=[*leaving, one_plane, lists],
         in_specs=[free, smem, hbm],
-        out_specs=[vmem] * n_orb + [smem],
+        out_specs=[vmem] * (len(leaving) + 1) + [smem],
         scratch_shapes=[
             pltpu.SMEM((devices, width), jnp.int32),
             held,
@@ -753,48 +772,52 @@
         name="route",
     )(table, jnp.asarray(fields), orbitals)
 
-    def in_planes(table, orbitals, box_start, work, own_pieces, *sends):
+    def in_planes(level, table, orbitals, box_start, work, own_pieces, *sends):
         del table, box_start
+        sends, short = list(sends[: n_orb - 1]), sends[n_orb - 1 :]
+        if level == 0:
+            for d, part in zip(fewer, short):
+                sends[d] = part
         arrived = cross(sends)
-        zeros, cleared = clear(work)
         starts = lax.dynamic_slice(
             work, (OWN_X, lax.axis_index("slab") * pair_dev), (3, pair_dev)
-        ).T
-        mats = matrices(starts)
-        density = pl.pallas_call(
-            density_kernel,
-            out_shape=one_plane,
+        )
+        density, start_y = pl.pallas_call(
+            functools.partial(density_kernel, begins),
+            out_shape=[one_plane, jax.ShapeDtypeStruct((1, pair_dev), jnp.int32)],
             in_specs=[smem] + [vmem] * n_orb,
-            out_specs=vmem,
+            out_specs=[vmem, smem],
             scratch_shapes=[one_slot],
             compiler_params=grant(8),
             name="density",
         )(work, own_pieces, *arrived)
+        mats = matrices(starts[0], start_y[0], starts[2])
         received = lax.all_to_all(density, "slab", split_axis=0, concat_axis=0, tiled=True)
         by_slab = (n_slab, pair_dev, slab_rows, PACKED)
         solved = pl.pallas_call(
             plane_solve_kernel,
             out_shape=jax.ShapeDtypeStruct(by_slab, jnp.float32),
-            in_specs=[vmem] * 15,
+            in_specs=[vmem] * 14,
             out_specs=vmem,
             compiler_params=grant(16),
             name="solve",
-        )(received.reshape(by_slab), cleared, *mats, jnp.asarray(spectrum()))
+        )(received.reshape(by_slab), *mats, jnp.asarray(spectrum()))
         potential = lax.all_to_all(
             solved.reshape(one_plane.shape), "slab", split_axis=0, concat_axis=0, tiled=True
         )
-        own_terms, *sends = pl.pallas_call(
-            term_kernel,
-            out_shape=[one_plane, *crossed],
+        own_terms, *sends, after = pl.pallas_call(
+            functools.partial(term_kernel, begins),
+            out_shape=[one_plane, *crossed(level), jax.ShapeDtypeStruct((1, 1), jnp.int32)],
             in_specs=[smem, vmem] + [vmem] * n_orb,
-            out_specs=[vmem] * n_orb,
+            out_specs=[vmem] * n_orb + [smem],
             scratch_shapes=[one_slot],
             compiler_params=grant(8),
             name="terms",
         )(work, potential, own_pieces, *arrived)
         arrived = cross(sends)
+        zeros, _ = clear(after)
         return pl.pallas_call(
-            plane_place_kernel,
+            functools.partial(plane_place_kernel, begins),
             out_shape=jax.ShapeDtypeStruct(orbitals.shape, jnp.float32),
             in_specs=[smem, hbm, hbm] + [vmem] * n_orb,
             out_specs=hbm,
@@ -847,7 +870,7 @@
             pair_list,
             received.reshape(n_slab, n_orb, pair_dev, slab_rows, PACKED),
             cleared,
-            *matrices(box_start),
+            *matrices(*box_start.T),
             jnp.asarray(spectrum()),
         )
         returned = lax.all_to_all(solved.reshape(slots), axes, split_axis=0, concat_axis=0, tiled=True)
@@ -868,10 +891,9 @@
             name="place",
         )(work, orbitals, returned, zeros)
 
-    return lax.cond(
-        work[COUNT, 2] > 0,
-        direct,
-        in_planes,
+    return lax.switch(
+        work[COUNT, 2],
+        [functools.partial(in_planes, 0), functools.partial(in_planes, 1), direct],
         table,
         orbitals,
         box_start,

time: 81.3 us -> 77.5 us (0.953); the launches traced: 80.5 us -> 77.8 us
  waiting for transfers between devices: 11 us -> 5.29 us
  Pallas kernels: 19 us -> 22.3 us
    ppermute x6, waiting for transfers between devices: 9.84 us -> 2.16 us  [cross(): lax.ppermute(part, 'orb', [(o, o ^ n + 1) for o in range(n_orb)])]
    all_to_all x1, waiting for transfers between devices: 1.13 us -> 3.13 us  [in_planes(): lax.all_to_all(density, 'slab', split_axis=0, concat_axis=0, tiled=True)]
    pallas_call x3, Pallas kernels: 6.54 us -> 8.5 us  [the longest x1 4.92 us: in_planes(): pl.pallas_call(functools.partial(plane_place_kernel, begins), out_shape=j...]
    pallas_call x1, Pallas kernels: 6.2 us -> 7.11 us  [body(): pl.pallas_call(functools.partial(route_kernel, pair_dev, n_orb, field_bit...]
  transfers between devices with their start and end apart: 7 -> 7, of which waited for: 3 -> 3; matrix products, arithmetic and copies ran while one was open for 16% -> 15% of each run, Pallas kernels for 5% -> 6%
where the time goes in v5:
time: 77.5 us; the launch traced here: 77.8 us
  blocking collectives  23.6 us (30%)
  Pallas kernels  22.3 us (29%)
  other arithmetic  12.5 us (16%)
  starting transfers between devices  11.4 us (15%)
  waiting for transfers between devices  5.29 us (7%)
  local copies, waits for them, and re-layouts  1.27 us (2%)
  between operations  0.88 us (1%)
    all_to_all x1, blocking collectives, body(): lax.all_to_all(jnp.broadcast_to(row, (devices, width)), axes, split_axis=...  14.3 us
    convert_element_type x6, other arithmetic, halves(): return (high.astype(jnp.bfloat16), (full - high).astype(jnp.bfloat16))  10.4 us
    all_to_all x1, blocking collectives, in_planes(): lax.all_to_all(solved.reshape(one_plane.shape), 'slab', split_axis=0, con...  9.35 us
    ppermute x6, starting transfers between devices, cross(): lax.ppermute(part, 'orb', [(o, o ^ n + 1) for o in range(n_orb)])  8 us
    pallas_call x1, Pallas kernels, body(): pl.pallas_call(functools.partial(route_kernel, pair_dev, n_orb, field_bit...  7.11 us
    pallas_call x1, Pallas kernels, in_planes(): pl.pallas_call(functools.partial(plane_place_kernel, begins), out_shape=j...  4.92 us
    pallas_call x1, Pallas kernels, clear(): pl.pallas_call(clear_kernel, out_shape=[jax.ShapeDtypeStruct(orbitals.sha...  4.67 us
    all_to_all x1, starting transfers between devices, in_planes(): lax.all_to_all(density, 'slab', split_axis=0, concat_axis=0, tiled=True)  3.42 us
  transfers between devices with their start and end apart: 7, of which 3 were waited for; matrix products, arithmetic and copies ran while one was open for 15% of the time, Pallas kernels for 6%

profile of v5, /device:TPU:0, one launch (start us, length us, event | category | flops | bytes accessed | tf_op | source)
XLA Modules:
  0.0 77.8 jit_solution(4995136173030371235)
XLA Ops:
  0.0 0.0 copy-start.2
  0.0 0.0 copy-start.3
  0.0 0.8 %pad_add_fusion = s32[1,5]{1,0:T(1,128)S(1)} fusion(s32[1,3]{1,0:T(1,128)} %param.12, s32[1,2]{1,0:T(1,128)} %param.11), kind=kLoop, calls=%fused_computation.291 | loop fusion | flops 5 | bytes 40 | tf_op jit(solution)/shard_map/concatenate | solution.py:704
  0.8 14.3 %all_to_all.35 = s32[32,1,128]{2,1,0:T(1,128)S(1)} all-to-all(s32[32,1,128]{2,1,0:T(1,128)S(1)} %broadcast_in_dim.45), channel_id=1, replica_groups=mesh['slab'=8,'orb'=4] {'slab','orb'}, dimensions={0} | all-to-all | bytes 32768 | tf_op jit(solution)/shard_map/all_to_all | solution.py:707
  15.1 7.1 %route.1 = (f32[6,8,1024]{2,1,0:T(8,128)}, f32[4,8,1024]{2,1,0:T(8,128)}, f32[4,8,1024]{2,1,0:T(8,128)}, f32[3,8,1024]{2,1,0:T(8,128)S(1)}, f32[3,8,1024]{2,1,0:...) custom-call(s32[32,128]{1,0:T(8,128)S(1)} %bitcast.25, s32[64]{0:T(128)} %constant.269.clone.fields, ...), custom_call_target="tpu_custom_call" | custom-call | tf_op jit(solution)/shard_map/route/pallas_call | solution.py:755
  22.2 0.6 slice.18
  23.5 0.0 copy-done.2
  23.5 0.0 copy-done.3
  23.5 54.1 %conditional.1 = (f32[64,8,4096]{2,1,0:T(8,128)}) conditional(s32[]{:T(128)} %bitcast.17, (f32[6,8,1024]{2,1,0:T(8,128)}, f32[3,8,1024]{2,1,0:T(8,128)S(1)}, f32[3,8,1024]{2,1,0:T(8,128)S(1)}, s32[24,128]{1,0:T(8,128)S(1)}, f32[8,8,1024]{2,1,0:T(8,128)S(1)}, /*index=5*/f32[384,384]{1,0:T(8,128)S(1)}, ...), branch_computations={%region_0.1_spmd, %region_1.2_spmd, %region_2.3_spmd} | conditional | flops 7726774 | bytes 15622404 | solution.py:894
  23.5 0.6 collective-permute-start.1
  24.1 1.5 %collective-permute-start.2 = (f32[3,8,1024]{2,1,0:T(8,128)S(1)}, f32[3,8,1024]{2,1,0:T(8,128)S(1)}, u32[]{:S(2)}, u32[]{:S(2)}) collective-permute-start(f32[3,8,1024]{2,1,0:T(8,128)S(1)} %get-tuple-element.52), channel_id=1, source_target_pairs={{0,3},{1,2},{2,1},{3,0},{4,7},{5,6},{6,5},{7,4},{8,11},{9,10},{10,... | collective-permute-start | bytes 294920 | tf_op jit(solution)/shard_map/cond/branch_0_fun/ppermute | solution.py:731
  25.6 1.5 %collective-permute-start = (f32[6,8,1024]{2,1,0:T(8,128)}, f32[6,8,1024]{2,1,0:T(8,128)S(1)}, u32[]{:S(2)}, u32[]{:S(2)}) collective-permute-start(f32[6,8,1024]{2,1,0:T(8,128)} %get-tuple-element.50), channel_id=1, source_target_pairs={{0,1},{1,0},{2,3},{3,2},{4,5},{5,4},{6,7},{7,6},{8,9},{9,8},{10,11... | collective-permute-start | bytes 589832 | tf_op jit(solution)/shard_map/cond/branch_0_fun/ppermute | solution.py:731
  27.1 0.1 constant_dynamic-slice_fusion
  27.2 0.6 fusion.180
  27.7 0.7 and_add_fusion
  28.4 2.5 %fusion = (bf16[1,256,512]{2,1,0:T(8,128)(2,1)S(1)}, bf16[1,256,512]{2,1,0:T(8,128)(2,1)S(1)}) fusion(s32[256]{0:T(256)S(1)} %and_add_fusion, s32[512]{0:T(512)S(1)} %get-tuple-element.116, pred[512]{0:T(512)(128)(4,1)S(1)} %fusion.47, s32[512]{0:T(512)S(1)} %get-tuple-element.115, s32[256]{0:T(256)S(1)} %get-tuple-element.118, s32[512]{0:T(512)S(1)} %fusion.48, ...), kind=kLoop, calls=%fused_computation.12 | loop fusion | flops 2359296 | bytes 534016 | tf_op jit(solution)/shard_map/cond/branch_0_fun/convert_element_type | solution.py:67
  30.9 2.7 %fusion.1 = (bf16[1,512,256]{2,1,0:T(8,128)(2,1)S(1)}, bf16[1,512,256]{2,1,0:T(8,128)(2,1)S(1)}) fusion(s32[256]{0:T(256)S(1)} %and_add_fusion, s32[512]{0:T(512)S(1)} %get-tuple-element.116, pred[512]{0:T(512)(128)(4,1)S(1)} %fusion.47, s32[512]{0:T(512)S(1)} %get-tuple-element.115, s32[256]{0:T(256)S(1)} %get-tuple-element.118, s32[512]{0:T(512)S(1)} %fusion.48, ...), kind=kLoop, calls=%fused_computation.13 | loop fusion | flops 2359296 | bytes 534016 | tf_op jit(solution)/shard_map/cond/branch_0_fun/convert_element_type | solution.py:67
  33.6 0.8 %fusion.32 = (bf16[1,48,32]{2,1,0:T(8,128)(2,1)S(1)}, bf16[1,48,32]{2,1,0:T(8,128)(2,1)S(1)}) fusion(s32[]{:T(128)} %bitcast.1, s32[48]{0:T(128)S(1)} %iota_add_fusion), kind=kLoop, calls=%fused_computation.51 | loop fusion | flops 24576 | bytes 6340 | tf_op jit(solution)/shard_map/cond/branch_0_fun/convert_element_type | solution.py:67
  34.4 0.7 fusion.39
  35.1 0.0 collective-permute-done.1.refs_2_
  35.1 0.0 collective-permute-done.2.refs_3_
  35.1 0.9 %collective-permute-done.refs_1_ = f32[6,8,1024]{2,1,0:T(8,128)S(1)} collective-permute-done((f32[6,8,1024]{2,1,0:T(8,128)}, f32[6,8,1024]{2,1,0:T(8,128)S(1)}, u32[]{:S(2)}, u32[]{:S(2)}) %collective-permute-start) | collective-permute-done | bytes 196640 | tf_op jit(solution)/shard_map/cond/branch_0_fun/ppermute | solution.py:731
  36.0 1.9 %density.2 = (f32[8,8,1024]{2,1,0:T(8,128)}, s32[1,1]{1,0:T(1,128)}) custom-call(s32[24,128]{1,0:T(8,128)S(1)} %get-tuple-element.46.work, f32[8,8,1024]{2,1,0:T(8,128)S(1)} %get-tuple-element.49.refs_0_, f32[6,8,1024]{2,1,0:T(8,128)S(1)} %collective-permute-done.refs_1_, f32[3,8,1024]{2,1,0:T(8,128)S(1)} %collective-permute-done.1.refs_2_, ...), custom_call_target="tpu_custom_call" | custom-call | tf_op jit(solution)/shard_map/cond/branch_0_fun/density/pallas_call | solution.py:785
  37.9 0.6 fusion.56
  38.6 3.4 %all-to-all-start = ((f32[8,8,1024]{2,1,0:T(8,128)}), f32[8,8,1024]{2,1,0:T(8,128)S(1)}, u32[]{:S(2)}, u32[]{:S(2)}) async-start(f32[8,8,1024]{2,1,0:T(8,128)} %get-tuple-element.53), calls=%async_computation | async-start | bytes 524288 | tf_op jit(solution)/shard_map/cond/branch_0_fun/all_to_all | solution.py:795
  42.0 1.9 %fusion.16 = (bf16[1,384,256]{2,1,0:T(8,128)(2,1)S(1)}, bf16[1,384,256]{2,1,0:T(8,128)(2,1)S(1)}) fusion(s32[256]{0:T(256)S(1)} %get-tuple-element.121, s32[384]{0:T(512)S(1)} %get-tuple-element.119, s32[256]{0:T(256)S(1)} %get-tuple-element.122, s32[384]{0:T(512)S(1)} %get-tuple-element.120), kind=kLoop, calls=%fused_computation.30 | loop fusion | flops 1474560 | bytes 398336 | tf_op jit(solution)/shard_map/cond/branch_0_fun/convert_element_type | solution.py:67
  43.9 1.8 %fusion.17 = (bf16[1,256,384]{2,1,0:T(8,128)(2,1)S(1)}, bf16[1,256,384]{2,1,0:T(8,128)(2,1)S(1)}) fusion(s32[256]{0:T(256)S(1)} %get-tuple-element.121, s32[384]{0:T(512)S(1)} %get-tuple-element.119, s32[384]{0:T(512)S(1)} %get-tuple-element.120, s32[256]{0:T(256)S(1)} %get-tuple-element.122), kind=kLoop, calls=%fused_computation.31 | loop fusion | flops 1474560 | bytes 398336 | tf_op jit(solution)/shard_map/cond/branch_0_fun/convert_element_type | solution.py:67
  45.7 3.1 %all-to-all-done = f32[8,8,1024]{2,1,0:T(8,128)S(1)} async-done(((f32[8,8,1024]{2,1,0:T(8,128)}), f32[8,8,1024]{2,1,0:T(8,128)S(1)}, u32[]{:S(2)}, u32[]{:S(2)}) %all-to-all-start) | async-done | bytes 262176 | tf_op jit(solution)/shard_map/cond/branch_0_fun/all_to_all | solution.py:795
  48.9 2.1 %solve.3 = f32[8,1,8,1024]{3,2,1,0:T(8,128)S(1)} custom-call(f32[8,1,8,1024]{3,2,1,0:T(8,128)S(1)} %bitcast.21, bf16[1,48,32]{2,1,0:T(8,128)(2,1)S(1)} %get-tuple-element.114.refs_0_, bf16[1,48,32]{2,1,0:T(8,128)(2,1)S(1)} %get-tuple-element.113.refs_1_, bf16[1,32,48]{2,1,0:T(8,128)(2,1)S(1)} %get-tuple-element.112.refs_2_, ...), custom_call_target="tpu_custom_call" | custom-call | tf_op jit(solution)/shard_map/cond/branch_0_fun/solve/pallas_call | solution.py:797
  50.9 9.3 %all_to_all.32.potential = f32[8,8,1024]{2,1,0:T(8,128)S(1)} all-to-all(f32[8,8,1024]{2,1,0:T(8,128)S(1)} %bitcast.23), channel_id=1, replica_groups=mesh['slab'=8,'orb'=4] {'slab'}, dimensions={0} | all-to-all | bytes 524288 | tf_op jit(solution)/shard_map/cond/branch_0_fun/all_to_all | solution.py:805
  60.3 1.7 %terms.2 = (f32[8,8,1024]{2,1,0:T(8,128)S(1)}, f32[6,8,1024]{2,1,0:T(8,128)S(1)}, f32[3,8,1024]{2,1,0:T(8,128)S(1)}, f32[3,8,1024]{2,1,0:T(8,128)S(1)}, s32[1,1]{1,0:T(1,128)}) custom-call(s32[24,128]{1,0:T(8,128)S(1)} %get-tuple-element.46.work, f32[8,8,1024]{2,1,0:T(8,128)S(1)} %all_to_all.32.potential, f32[8,8,1024]{2,1,0:T(8,128)S(1)} %get-tuple-element.49.refs_0_, ...), custom_call_target="tpu_custom_call" | custom-call | tf_op jit(solution)/shard_map/cond/branch_0_fun/terms/pallas_call | solution.py:808
  62.0 0.1 collective-permute-start.3
  62.1 1.5 %collective-permute-start.4 = (f32[3,8,1024]{2,1,0:T(8,128)S(1)}, f32[3,8,1024]{2,1,0:T(8,128)S(1)}, u32[]{:S(2)}, u32[]{:S(2)}) collective-permute-start(f32[3,8,1024]{2,1,0:T(8,128)S(1)} %get-tuple-element.60), channel_id=1, source_target_pairs={{0,2},{1,3},{2,0},{3,1},{4,6},{5,7},{6,4},{7,5},{8,10},{9,11},{10,... | collective-permute-start | bytes 294920 | tf_op jit(solution)/shard_map/cond/branch_0_fun/ppermute | solution.py:731
  63.6 2.8 %collective-permute-start.5 = (f32[3,8,1024]{2,1,0:T(8,128)S(1)}, f32[3,8,1024]{2,1,0:T(8,128)S(1)}, u32[]{:S(2)}, u32[]{:S(2)}) collective-permute-start(f32[3,8,1024]{2,1,0:T(8,128)S(1)} %get-tuple-element.61), channel_id=1, source_target_pairs={{0,3},{1,2},{2,1},{3,0},{4,7},{5,6},{6,5},{7,4},{8,11},{9,10},{10,... | collective-permute-start | bytes 294920 | tf_op jit(solution)/shard_map/cond/branch_0_fun/ppermute | solution.py:731
  66.4 4.7 %clear.3 = (f32[64,8,4096]{2,1,0:T(8,128)}, s32[8,128]{1,0:T(8,128)}) custom-call(s32[1,1]{1,0:T(1,128)} %get-tuple-element.56.after), custom_call_target="tpu_custom_call" | custom-call | bytes 8388608 | tf_op jit(solution)/shard_map/cond/branch_0_fun/clear/pallas_call | solution.py:736
  71.1 0.0 collective-permute-done.4.refs_2_
  71.1 1.3 %collective-permute-done.5.refs_3_ = f32[3,8,1024]{2,1,0:T(8,128)S(1)} collective-permute-done((f32[3,8,1024]{2,1,0:T(8,128)S(1)}, f32[3,8,1024]{2,1,0:T(8,128)S(1)}, u32[]{:S(2)}, u32[]{:S(2)}) %collective-permute-start.5) | collective-permute-done | bytes 98336 | tf_op jit(solution)/shard_map/cond/branch_0_fun/ppermute | solution.py:731
  72.4 0.0 collective-permute-done.3.refs_1_
  72.4 4.9 %place.3 = f32[64,8,4096]{2,1,0:T(8,128)} custom-call(s32[24,128]{1,0:T(8,128)S(1)} %get-tuple-element.46.work, f32[64,8,4096]{2,1,0:T(8,128)} %get-tuple-element.48.orbitals, f32[64,8,4096]{2,1,0:T(8,128)} %get-tuple-element.57.zeros, f32[8,8,1024]{2,1,0:T(8,128)S(1)} %get-tuple-element.58.refs_0_, ...), custom_call_target="tpu_custom_call", output_to_operand_aliasing={{}: (2, {})} | custom-call | tf_op jit(solution)/shard_map/cond/branch_0_fun/place/pallas_call | solution.py:819
  (8 shorter events, 0.0 us)
Async XLA Ops:
  0.0 23.5 %copy-start.2 = (f32[384,384]{1,0:T(8,128)S(1)}, f32[384,384]{1,0:T(8,128)}, u32[]{:S(2)}) copy-start(f32[384,384]{1,0:T(8,128)} %constant.270.clone) | copy-start | bytes 1769476
  0.0 23.5 %copy-start.3 = (s32[1,3]{1,0:T(1,128)S(1)}, s32[1,3]{1,0:T(1,128)}, u32[]{:S(2)}) copy-start(s32[1,3]{1,0:T(1,128)} %param.12) | copy-start | bytes 40
  23.5 11.6 %collective-permute-start.1 = (f32[3,8,1024]{2,1,0:T(8,128)S(1)}, f32[3,8,1024]{2,1,0:T(8,128)S(1)}, u32[]{:S(2)}, u32[]{:S(2)}) collective-permute-start(f32[3,8,1024]{2,1,0:T(8,128)S(1)} %get-tuple-element.51), channel_id=1, source_target_pairs={{0,2},{1,3},{2,0},{3,1},{4,6},{5,7},{6,4},{7,5},{8,10},{9,11},{10,... | collective-permute-start | bytes 294920 | tf_op jit(solution)/shard_map/cond/branch_0_fun/ppermute | solution.py:731
  24.1 11.0 %collective-permute-start.2 = (f32[3,8,1024]{2,1,0:T(8,128)S(1)}, f32[3,8,1024]{2,1,0:T(8,128)S(1)}, u32[]{:S(2)}, u32[]{:S(2)}) collective-permute-start(f32[3,8,1024]{2,1,0:T(8,128)S(1)} %get-tuple-element.52), channel_id=1, source_target_pairs={{0,3},{1,2},{2,1},{3,0},{4,7},{5,6},{6,5},{7,4},{8,11},{9,10},{10,... | collective-permute-start | bytes 294920 | tf_op jit(solution)/shard_map/cond/branch_0_fun/ppermute | solution.py:731
  25.6 10.5 %collective-permute-start = (f32[6,8,1024]{2,1,0:T(8,128)}, f32[6,8,1024]{2,1,0:T(8,128)S(1)}, u32[]{:S(2)}, u32[]{:S(2)}) collective-permute-start(f32[6,8,1024]{2,1,0:T(8,128)} %get-tuple-element.50), channel_id=1, source_target_pairs={{0,1},{1,0},{2,3},{3,2},{4,5},{5,4},{6,7},{7,6},{8,9},{9,8},{10,11... | collective-permute-start | bytes 589832 | tf_op jit(solution)/shard_map/cond/branch_0_fun/ppermute | solution.py:731
  38.6 10.3 %all-to-all-start = ((f32[8,8,1024]{2,1,0:T(8,128)}), f32[8,8,1024]{2,1,0:T(8,128)S(1)}, u32[]{:S(2)}, u32[]{:S(2)}) async-start(f32[8,8,1024]{2,1,0:T(8,128)} %get-tuple-element.53), calls=%async_computation | async-start | bytes 524288 | tf_op jit(solution)/shard_map/cond/branch_0_fun/all_to_all | solution.py:795
  62.0 10.4 %collective-permute-start.3 = (f32[6,8,1024]{2,1,0:T(8,128)S(1)}, f32[6,8,1024]{2,1,0:T(8,128)S(1)}, u32[]{:S(2)}, u32[]{:S(2)}) collective-permute-start(f32[6,8,1024]{2,1,0:T(8,128)S(1)} %get-tuple-element.59), channel_id=1, source_target_pairs={{0,1},{1,0},{2,3},{3,2},{4,5},{5,4},{6,7},{7,6},{8,9},{9,8},{10,11... | collective-permute-start | bytes 589832 | tf_op jit(solution)/shard_map/cond/branch_0_fun/ppermute | solution.py:731
  62.1 9.1 %collective-permute-start.4 = (f32[3,8,1024]{2,1,0:T(8,128)S(1)}, f32[3,8,1024]{2,1,0:T(8,128)S(1)}, u32[]{:S(2)}, u32[]{:S(2)}) collective-permute-start(f32[3,8,1024]{2,1,0:T(8,128)S(1)} %get-tuple-element.60), channel_id=1, source_target_pairs={{0,2},{1,3},{2,0},{3,1},{4,6},{5,7},{6,4},{7,5},{8,10},{9,11},{10,... | collective-permute-start | bytes 294920 | tf_op jit(solution)/shard_map/cond/branch_0_fun/ppermute | solution.py:731
  63.6 8.8 %collective-permute-start.5 = (f32[3,8,1024]{2,1,0:T(8,128)S(1)}, f32[3,8,1024]{2,1,0:T(8,128)S(1)}, u32[]{:S(2)}, u32[]{:S(2)}) collective-permute-start(f32[3,8,1024]{2,1,0:T(8,128)S(1)} %get-tuple-element.61), channel_id=1, source_target_pairs={{0,3},{1,2},{2,1},{3,0},{4,7},{5,6},{6,5},{7,4},{8,11},{9,10},{10,... | collective-permute-start | bytes 294920 | tf_op jit(solution)/shard_map/cond/branch_0_fun/ppermute | solution.py:731

commit v6 on v5

--- a/solution.py
+++ b/solution.py
@@ -435,7 +435,8 @@
 def crossing_slots(cap, n_orb):
     near = max(cap * 3 // 4, 1)
     far = max(cap * 3 // 8, 1)
-    return [(near, 0) if d == 1 else (far, max(cap // 2 - far, 1)) for d in range(1, n_orb)]
+    step = max(cap // 8, 1)
+    return [(near, 0, 0) if d == 1 else (far, step, step) for d in range(1, n_orb)]
 
 
 def route_kernel(
@@ -448,7 +449,8 @@
     spans = crossing_slots(cap, n_orb)
     slots = [sum(span) for span in spans]
     begins = [0] + [cap + sum(slots[:d]) for d in range(n_orb - 1)]
-    begins += [begins[d + 1] for d, span in enumerate(spans) if span[1]]
+    fewer = [d for d, span in enumerate(spans) if span[1]]
+    begins += [begins[d + 1] for d in fewer] * (len(spans[0]) - 1)
     me = lax.axis_index("orb")
     slab = lax.axis_index("slab")
     base, first_row = me * orb_dev, slab * slab_rows
@@ -550,12 +552,12 @@
     for o in range(n_orb):
         for k in range(n_orb):
             if o != k:
-                (base_room, more), count = spans[(o ^ k) - 1], crossing[o * n_orb + k]
+                span, count = spans[(o ^ k) - 1], crossing[o * n_orb + k]
                 for f in range(8 if width else 1):
                     held_here = (count >> (width * f)) & 15 if width else count
-                    if more:
-                        level = jnp.maximum(level, jnp.where(held_here > base_room, 1, 0))
-                    level = jnp.maximum(level, jnp.where(held_here > base_room + more, 2, 0))
+                    for at in range(len(span)):
+                        room = sum(span[: at + 1])
+                        level = jnp.maximum(level, jnp.where(held_here > room, at + 1, 0))
     work[COUNT, 0] = terms
     work[COUNT, 1] = first_row
     work[COUNT, 2] = level
@@ -723,7 +725,8 @@
         ]
 
     fewer = [d for d, span in enumerate(spans) if span[1]]
-    leaving = crossed(1) + [crossed(0)[d] for d in fewer]
+    top = len(spans[0]) - 1
+    leaving = crossed(top) + [crossed(level)[d] for level in range(top) for d in fewer]
     one_slot = pltpu.VMEM((slab_rows, PACKED), jnp.float32)
 
     def cross(parts):
@@ -775,8 +778,8 @@
     def in_planes(level, table, orbitals, box_start, work, own_pieces, *sends):
         del table, box_start
         sends, short = list(sends[: n_orb - 1]), sends[n_orb - 1 :]
-        if level == 0:
-            for d, part in zip(fewer, short):
+        if level < top:
+            for d, part in zip(fewer, short[level * len(fewer) :]):
                 sends[d] = part
         arrived = cross(sends)
         starts = lax.dynamic_slice(
@@ -893,7 +896,7 @@
 
     return lax.switch(
         work[COUNT, 2],
-        [functools.partial(in_planes, 0), functools.partial(in_planes, 1), direct],
+        [*(functools.partial(in_planes, level) for level in range(top + 1)), direct],
         table,
         orbitals,
         box_start,

time: 77.5 us -> 82.2 us (1.061)
  waiting for transfers between devices: 5.29 us -> 9.98 us
    ppermute x6, waiting for transfers between devices: 2.16 us -> 7.03 us  [cross(): lax.ppermute(part, 'orb', [(o, o ^ n + 1) for o in range(n_orb)])]
  transfers between devices with their start and end apart: 7 -> 7, of which waited for: 3 -> 4; matrix products, arithmetic and copies ran while one was open for 15% -> 14% of each run, Pallas kernels for 6% -> 6%
where the time goes in v6:
time: 82.2 us; the launch traced here: 82.6 us
  blocking collectives  23.6 us (29%)
  Pallas kernels  22.3 us (27%)
  other arithmetic  12.3 us (15%)
  starting transfers between devices  11.6 us (14%)
  waiting for transfers between devices  9.98 us (12%)
  local copies, waits for them, and re-layouts  1.21 us (1%)
  between operations  0.91 us (1%)
    all_to_all x1, blocking collectives, body(): lax.all_to_all(jnp.broadcast_to(row, (devices, width)), axes, split_axis=...  14.3 us
    convert_element_type x6, other arithmetic, halves(): return (high.astype(jnp.bfloat16), (full - high).astype(jnp.bfloat16))  10.2 us
    all_to_all x1, blocking collectives, in_planes(): lax.all_to_all(solved.reshape(one_plane.shape), 'slab', split_axis=0, con...  9.35 us
    ppermute x6, starting transfers between devices, cross(): lax.ppermute(part, 'orb', [(o, o ^ n + 1) for o in range(n_orb)])  8 us
    pallas_call x1, Pallas kernels, body(): pl.pallas_call(functools.partial(route_kernel, pair_dev, n_orb, field_bit...  7.3 us
    ppermute x6, waiting for transfers between devices, cross(): lax.ppermute(part, 'orb', [(o, o ^ n + 1) for o in range(n_orb)])  7.03 us
    pallas_call x1, Pallas kernels, clear(): pl.pallas_call(clear_kernel, out_shape=[jax.ShapeDtypeStruct(orbitals.sha...  4.58 us
    pallas_call x1, Pallas kernels, in_planes(): pl.pallas_call(functools.partial(plane_place_kernel, begins), out_shape=j...  4.57 us
  transfers between devices with their start and end apart: 7, of which 4 were waited for; matrix products, arithmetic and copies ran while one was open for 14% of the time, Pallas kernels for 6%

profile of v6, /device:TPU:0, one launch (start us, length us, event | category | flops | bytes accessed | tf_op | source)
XLA Modules:
  0.0 82.6 jit_solution(9499736005917918802)
XLA Ops:
  0.0 0.0 copy-start.2
  0.0 0.0 copy-start.3
  0.0 0.0 copy-start.4
  0.0 0.8 pad_add_fusion
  0.8 14.3 %all_to_all.44 = s32[32,1,128]{2,1,0:T(1,128)S(1)} all-to-all(s32[32,1,128]{2,1,0:T(1,128)S(1)} %broadcast_in_dim.57), channel_id=1, replica_groups=mesh['slab'=8,'orb'=4] {'slab','orb'}, dimensions={0} | all-to-all | bytes 32768 | tf_op jit(solution)/shard_map/all_to_all | solution.py:709
  15.1 7.3 %route.1 = (f32[6,8,1024]{2,1,0:T(8,128)}, f32[5,8,1024]{2,1,0:T(8,128)}, f32[5,8,1024]{2,1,0:T(8,128)}, f32[3,8,1024]{2,1,0:T(8,128)S(1)}, f32[3,8,1024]{2,1,0:...) custom-call(s32[32,128]{1,0:T(8,128)S(1)} %bitcast.32, ...), custom_call_target="tpu_custom_call" | custom-call | tf_op jit(solution)/shard_map/route/pallas_call | solution.py:758
  22.4 0.6 slice.24
  23.7 0.0 copy-done.2
  23.7 0.0 copy-done.3
  23.7 0.0 copy-done.4
  23.7 58.7 %conditional.1 = (f32[64,8,4096]{2,1,0:T(8,128)}) conditional(s32[]{:T(128)} %bitcast.22, (f32[6,8,1024]{2,1,0:T(8,128)}, f32[3,8,1024]{2,1,0:T(8,128)S(1)}, f32[3,8,1024]{2,1,0:T(8,128)S(1)}, s32[24,128]{1,0:T(8,128)S(1)}, f32[8,8,1024]{2,1,0:T(8,128)S(1)}, /*index=5*/f32[384,384]{1,0:T(8,128)S(1)}, ...), branch_computations={%region_0.1_spmd, %region_1.2_spmd, %region_2.3_spmd, %region_3.4_... | conditional | flops 7726774 | bytes 15786454 | solution.py:897
  23.7 0.1 collective-permute-start.7
  23.8 2.8 %collective-permute-start.8 = (f32[4,8,1024]{2,1,0:T(8,128)}, f32[4,8,1024]{2,1,0:T(8,128)S(1)}, u32[]{:S(2)}, u32[]{:S(2)}) collective-permute-start(f32[4,8,1024]{2,1,0:T(8,128)} %get-tuple-element.82), channel_id=1, source_target_pairs={{0,3},{1,2},{2,1},{3,0},{4,7},{5,6},{6,5},{7,4},{8,11},{9,10},{10,... | collective-permute-start | bytes 393224 | tf_op jit(solution)/shard_map/cond/branch_1_fun/ppermute | solution.py:734
  26.6 0.6 collective-permute-start.6
  27.3 0.1 constant_dynamic-slice_fusion.1
  27.4 0.5 fusion.241
  27.9 0.7 and_add_fusion.1
  28.6 2.5 %fusion.60 = (bf16[1,256,512]{2,1,0:T(8,128)(2,1)S(1)}, bf16[1,256,512]{2,1,0:T(8,128)(2,1)S(1)}) fusion(s32[256]{0:T(256)S(1)} %and_add_fusion.1, s32[512]{0:T(512)S(1)} %get-tuple-element.172, pred[512]{0:T(512)(128)(4,1)S(1)} %fusion.107, s32[512]{0:T(512)S(1)} %get-tuple-element.171, s32[256]{0:T(256)S(1)} %get-tuple-element.174, s32[512]{0:T(512)S(1)} %fusion.108, ...), kind=kLoop, calls=%fused_computation.109 | loop fusion | flops 2359296 | bytes 534016 | tf_op jit(solution)/shard_map/cond/branch_1_fun/convert_element_type | solution.py:67
  31.0 2.7 %fusion.61 = (bf16[1,512,256]{2,1,0:T(8,128)(2,1)S(1)}, bf16[1,512,256]{2,1,0:T(8,128)(2,1)S(1)}) fusion(s32[256]{0:T(256)S(1)} %and_add_fusion.1, s32[512]{0:T(512)S(1)} %get-tuple-element.172, pred[512]{0:T(512)(128)(4,1)S(1)} %fusion.107, s32[512]{0:T(512)S(1)} %get-tuple-element.171, s32[256]{0:T(256)S(1)} %get-tuple-element.174, s32[512]{0:T(512)S(1)} %fusion.108, ...), kind=kLoop, calls=%fused_computation.110 | loop fusion | flops 2359296 | bytes 534016 | tf_op jit(solution)/shard_map/cond/branch_1_fun/convert_element_type | solution.py:67
  33.7 0.7 fusion.92
  34.5 0.6 fusion.99
  35.1 1.1 %collective-permute-done.7.refs_2_ = f32[4,8,1024]{2,1,0:T(8,128)S(1)} collective-permute-done((f32[4,8,1024]{2,1,0:T(8,128)S(1)}, f32[4,8,1024]{2,1,0:T(8,128)S(1)}, u32[]{:S(2)}, u32[]{:S(2)}) %collective-permute-start.7) | collective-permute-done | bytes 131104 | tf_op jit(solution)/shard_map/cond/branch_1_fun/ppermute | solution.py:734
  36.2 0.0 collective-permute-done.8.refs_3_
  36.2 2.2 %collective-permute-done.6.refs_1_ = f32[6,8,1024]{2,1,0:T(8,128)S(1)} collective-permute-done((f32[6,8,1024]{2,1,0:T(8,128)}, f32[6,8,1024]{2,1,0:T(8,128)S(1)}, u32[]{:S(2)}, u32[]{:S(2)}) %collective-permute-start.6) | collective-permute-done | bytes 196640 | tf_op jit(solution)/shard_map/cond/branch_1_fun/ppermute | solution.py:734
  38.5 1.9 %density.4 = (f32[8,8,1024]{2,1,0:T(8,128)}, s32[1,1]{1,0:T(1,128)}) custom-call(s32[24,128]{1,0:T(8,128)S(1)} %get-tuple-element.77.work, f32[8,8,1024]{2,1,0:T(8,128)S(1)} %get-tuple-element.79.refs_0_, f32[6,8,1024]{2,1,0:T(8,128)S(1)} %collective-permute-done.6.refs_1_, f32[4,8,1024]{2,1,0:T(8,128)S(1)} %collective-permute-done.7.refs_2_, ...), custom_call_target="tpu_custom_call" | custom-call | tf_op jit(solution)/shard_map/cond/branch_1_fun/density/pallas_call | solution.py:788
  40.4 0.6 fusion.116
  41.0 3.6 %all-to-all-start.2 = ((f32[8,8,1024]{2,1,0:T(8,128)}), f32[8,8,1024]{2,1,0:T(8,128)S(1)}, u32[]{:S(2)}, u32[]{:S(2)}) async-start(f32[8,8,1024]{2,1,0:T(8,128)} %get-tuple-element.83), calls=%async_computation.2 | async-start | bytes 524288 | tf_op jit(solution)/shard_map/cond/branch_1_fun/all_to_all | solution.py:798
  44.6 1.9 %fusion.76 = (bf16[1,384,256]{2,1,0:T(8,128)(2,1)S(1)}, bf16[1,384,256]{2,1,0:T(8,128)(2,1)S(1)}) fusion(s32[256]{0:T(256)S(1)} %get-tuple-element.177, s32[384]{0:T(512)S(1)} %get-tuple-element.175, s32[256]{0:T(256)S(1)} %get-tuple-element.178, s32[384]{0:T(512)S(1)} %get-tuple-element.176), kind=kLoop, calls=%fused_computation.127 | loop fusion | flops 1474560 | bytes 398336 | tf_op jit(solution)/shard_map/cond/branch_1_fun/convert_element_type | solution.py:67
  46.5 1.8 %fusion.77 = (bf16[1,256,384]{2,1,0:T(8,128)(2,1)S(1)}, bf16[1,256,384]{2,1,0:T(8,128)(2,1)S(1)}) fusion(s32[256]{0:T(256)S(1)} %get-tuple-element.177, s32[384]{0:T(512)S(1)} %get-tuple-element.175, s32[384]{0:T(512)S(1)} %get-tuple-element.176, s32[256]{0:T(256)S(1)} %get-tuple-element.178), kind=kLoop, calls=%fused_computation.128 | loop fusion | flops 1474560 | bytes 398336 | tf_op jit(solution)/shard_map/cond/branch_1_fun/convert_element_type | solution.py:67
  48.3 2.9 %all-to-all-done.2 = f32[8,8,1024]{2,1,0:T(8,128)S(1)} async-done(((f32[8,8,1024]{2,1,0:T(8,128)}), f32[8,8,1024]{2,1,0:T(8,128)S(1)}, u32[]{:S(2)}, u32[]{:S(2)}) %all-to-all-start.2) | async-done | bytes 262176 | tf_op jit(solution)/shard_map/cond/branch_1_fun/all_to_all | solution.py:798
  51.3 2.1 %solve.5 = f32[8,1,8,1024]{3,2,1,0:T(8,128)S(1)} custom-call(f32[8,1,8,1024]{3,2,1,0:T(8,128)S(1)} %bitcast.27, bf16[1,48,32]{2,1,0:T(8,128)(2,1)S(1)} %get-tuple-element.170.refs_0_, bf16[1,48,32]{2,1,0:T(8,128)(2,1)S(1)} %get-tuple-element.169.refs_1_, bf16[1,32,48]{2,1,0:T(8,128)(2,1)S(1)} %get-tuple-element.168.refs_2_, ...), custom_call_target="tpu_custom_call" | custom-call | tf_op jit(solution)/shard_map/cond/branch_1_fun/solve/pallas_call | solution.py:800
  53.3 9.3 %all_to_all.41.potential = f32[8,8,1024]{2,1,0:T(8,128)S(1)} all-to-all(f32[8,8,1024]{2,1,0:T(8,128)S(1)} %bitcast.30), channel_id=1, replica_groups=mesh['slab'=8,'orb'=4] {'slab'}, dimensions={0} | all-to-all | bytes 524288 | tf_op jit(solution)/shard_map/cond/branch_1_fun/all_to_all | solution.py:808
  62.7 1.8 %terms.4 = (f32[8,8,1024]{2,1,0:T(8,128)S(1)}, f32[6,8,1024]{2,1,0:T(8,128)S(1)}, f32[4,8,1024]{2,1,0:T(8,128)S(1)}, f32[4,8,1024]{2,1,0:T(8,128)S(1)}, s32[1,1]{1,0:T(1,128)}) custom-call(s32[24,128]{1,0:T(8,128)S(1)} %get-tuple-element.77.work, f32[8,8,1024]{2,1,0:T(8,128)S(1)} %all_to_all.41.potential, f32[8,8,1024]{2,1,0:T(8,128)S(1)} %get-tuple-element.79.refs_0_, ...), custom_call_target="tpu_custom_call" | custom-call | tf_op jit(solution)/shard_map/cond/branch_1_fun/terms/pallas_call | solution.py:811
  64.5 0.4 collective-permute-start.9
  64.9 1.1 %collective-permute-start.10 = (f32[4,8,1024]{2,1,0:T(8,128)S(1)}, f32[4,8,1024]{2,1,0:T(8,128)S(1)}, u32[]{:S(2)}, u32[]{:S(2)}) collective-permute-start(f32[4,8,1024]{2,1,0:T(8,128)S(1)} %get-tuple-element.90), channel_id=1, source_target_pairs={{0,2},{1,3},{2,0},{3,1},{4,6},{5,7},{6,4},{7,5},{8,10},{9,11},{10,... | collective-permute-start | bytes 393224 | tf_op jit(solution)/shard_map/cond/branch_1_fun/ppermute | solution.py:734
  66.0 3.0 %collective-permute-start.11 = (f32[4,8,1024]{2,1,0:T(8,128)S(1)}, f32[4,8,1024]{2,1,0:T(8,128)S(1)}, u32[]{:S(2)}, u32[]{:S(2)}) collective-permute-start(f32[4,8,1024]{2,1,0:T(8,128)S(1)} %get-tuple-element.91), channel_id=1, source_target_pairs={{0,3},{1,2},{2,1},{3,0},{4,7},{5,6},{6,5},{7,4},{8,11},{9,10},{10,... | collective-permute-start | bytes 393224 | tf_op jit(solution)/shard_map/cond/branch_1_fun/ppermute | solution.py:734
  69.0 4.6 %clear.5 = (f32[64,8,4096]{2,1,0:T(8,128)}, s32[8,128]{1,0:T(8,128)}) custom-call(s32[1,1]{1,0:T(1,128)} %get-tuple-element.86.after), custom_call_target="tpu_custom_call" | custom-call | bytes 8388608 | tf_op jit(solution)/shard_map/cond/branch_1_fun/clear/pallas_call | solution.py:739
  73.6 3.7 %collective-permute-done.10.refs_2_ = f32[4,8,1024]{2,1,0:T(8,128)S(1)} collective-permute-done((f32[4,8,1024]{2,1,0:T(8,128)S(1)}, f32[4,8,1024]{2,1,0:T(8,128)S(1)}, u32[]{:S(2)}, u32[]{:S(2)}) %collective-permute-start.10) | collective-permute-done | bytes 131104 | tf_op jit(solution)/shard_map/cond/branch_1_fun/ppermute | solution.py:734
  77.2 0.0 collective-permute-done.11.refs_3_
  77.2 0.0 collective-permute-done.9.refs_1_
  77.3 4.6 %place.5 = f32[64,8,4096]{2,1,0:T(8,128)} custom-call(s32[24,128]{1,0:T(8,128)S(1)} %get-tuple-element.77.work, f32[64,8,4096]{2,1,0:T(8,128)} %get-tuple-element.78.orbitals, f32[64,8,4096]{2,1,0:T(8,128)} %get-tuple-element.87.zeros, f32[8,8,1024]{2,1,0:T(8,128)S(1)} %get-tuple-element.88.refs_0_, ...), custom_call_target="tpu_custom_call", output_to_operand_aliasing={{}: (2, {})} | custom-call | tf_op jit(solution)/shard_map/cond/branch_1_fun/place/pallas_call | solution.py:822
  (8 shorter events, 0.0 us)
Async XLA Ops:
  0.0 23.7 %copy-start.2 = (f32[384,384]{1,0:T(8,128)S(1)}, f32[384,384]{1,0:T(8,128)}, u32[]{:S(2)}) copy-start(f32[384,384]{1,0:T(8,128)} %constant.371.clone) | copy-start | bytes 1769476
  0.0 23.7 %copy-start.3 = (s32[1,3]{1,0:T(1,128)S(1)}, s32[1,3]{1,0:T(1,128)}, u32[]{:S(2)}) copy-start(s32[1,3]{1,0:T(1,128)} %param.14) | copy-start | bytes 40
  0.0 23.7 %copy-start.4 = (s32[1,2]{1,0:T(1,128)S(1)}, s32[1,2]{1,0:T(1,128)}, u32[]{:S(2)}) copy-start(s32[1,2]{1,0:T(1,128)} %param.13) | copy-start | bytes 28
  23.7 12.5 %collective-permute-start.7 = (f32[4,8,1024]{2,1,0:T(8,128)S(1)}, f32[4,8,1024]{2,1,0:T(8,128)S(1)}, u32[]{:S(2)}, u32[]{:S(2)}) collective-permute-start(f32[4,8,1024]{2,1,0:T(8,128)S(1)} %get-tuple-element.81), channel_id=1, source_target_pairs={{0,2},{1,3},{2,0},{3,1},{4,6},{5,7},{6,4},{7,5},{8,10},{9,11},{10,... | collective-permute-start | bytes 393224 | tf_op jit(solution)/shard_map/cond/branch_1_fun/ppermute | solution.py:734
  23.8 12.4 %collective-permute-start.8 = (f32[4,8,1024]{2,1,0:T(8,128)}, f32[4,8,1024]{2,1,0:T(8,128)S(1)}, u32[]{:S(2)}, u32[]{:S(2)}) collective-permute-start(f32[4,8,1024]{2,1,0:T(8,128)} %get-tuple-element.82), channel_id=1, source_target_pairs={{0,3},{1,2},{2,1},{3,0},{4,7},{5,6},{6,5},{7,4},{8,11},{9,10},{10,... | collective-permute-start | bytes 393224 | tf_op jit(solution)/shard_map/cond/branch_1_fun/ppermute | solution.py:734
  26.6 11.8 %collective-permute-start.6 = (f32[6,8,1024]{2,1,0:T(8,128)}, f32[6,8,1024]{2,1,0:T(8,128)S(1)}, u32[]{:S(2)}, u32[]{:S(2)}) collective-permute-start(f32[6,8,1024]{2,1,0:T(8,128)} %get-tuple-element.80), channel_id=1, source_target_pairs={{0,1},{1,0},{2,3},{3,2},{4,5},{5,4},{6,7},{7,6},{8,9},{9,8},{10,11... | collective-permute-start | bytes 589832 | tf_op jit(solution)/shard_map/cond/branch_1_fun/ppermute | solution.py:734
  41.0 10.3 %all-to-all-start.2 = ((f32[8,8,1024]{2,1,0:T(8,128)}), f32[8,8,1024]{2,1,0:T(8,128)S(1)}, u32[]{:S(2)}, u32[]{:S(2)}) async-start(f32[8,8,1024]{2,1,0:T(8,128)} %get-tuple-element.83), calls=%async_computation.2 | async-start | bytes 524288 | tf_op jit(solution)/shard_map/cond/branch_1_fun/all_to_all | solution.py:798
  64.5 12.7 %collective-permute-start.9 = (f32[6,8,1024]{2,1,0:T(8,128)S(1)}, f32[6,8,1024]{2,1,0:T(8,128)S(1)}, u32[]{:S(2)}, u32[]{:S(2)}) collective-permute-start(f32[6,8,1024]{2,1,0:T(8,128)S(1)} %get-tuple-element.89), channel_id=1, source_target_pairs={{0,1},{1,0},{2,3},{3,2},{4,5},{5,4},{6,7},{7,6},{8,9},{9,8},{10,11... | collective-permute-start | bytes 589832 | tf_op jit(solution)/shard_map/cond/branch_1_fun/ppermute | solution.py:734
  64.9 12.3 %collective-permute-start.10 = (f32[4,8,1024]{2,1,0:T(8,128)S(1)}, f32[4,8,1024]{2,1,0:T(8,128)S(1)}, u32[]{:S(2)}, u32[]{:S(2)}) collective-permute-start(f32[4,8,1024]{2,1,0:T(8,128)S(1)} %get-tuple-element.90), channel_id=1, source_target_pairs={{0,2},{1,3},{2,0},{3,1},{4,6},{5,7},{6,4},{7,5},{8,10},{9,11},{10,... | collective-permute-start | bytes 393224 | tf_op jit(solution)/shard_map/cond/branch_1_fun/ppermute | solution.py:734
  66.0 11.3 %collective-permute-start.11 = (f32[4,8,1024]{2,1,0:T(8,128)S(1)}, f32[4,8,1024]{2,1,0:T(8,128)S(1)}, u32[]{:S(2)}, u32[]{:S(2)}) collective-permute-start(f32[4,8,1024]{2,1,0:T(8,128)S(1)} %get-tuple-element.91), channel_id=1, source_target_pairs={{0,3},{1,2},{2,1},{3,0},{4,7},{5,6},{6,5},{7,4},{8,11},{9,10},{10,... | collective-permute-start | bytes 393224 | tf_op jit(solution)/shard_map/cond/branch_1_fun/ppermute | solution.py:734

commit v7 on v6

--- a/solution.py
+++ b/solution.py
@@ -599,7 +599,7 @@
     def load(ref, n):
         side[...] = ref[n]
 
-    @pl.loop(0, out.shape[0])
+    @pl.loop(0, out.shape[0], unroll=2)
     def _(j):
         a, b = work[OWN_A, j], work[OWN_B, j]
         meets = work[OWN_MEETS, j] != 0
@@ -649,7 +649,7 @@
     def store(ref, n):
         ref[n] = term[...]
 
-    @pl.loop(0, potential.shape[0])
+    @pl.loop(0, potential.shape[0], unroll=2)
     def _(j):
         a, b = work[OWN_A, j], work[OWN_B, j]
         meets = work[OWN_MEETS, j] != 0

time: 82.2 us -> 81.8 us (level)
  Pallas kernels: 22.3 us -> 21.2 us
where the time goes in v7:
time: 81.8 us; the launch traced here: 81.5 us
  blocking collectives  23.6 us (29%)
  Pallas kernels  21.2 us (26%)
  other arithmetic  12.3 us (15%)
  starting transfers between devices  11.6 us (14%)
  waiting for transfers between devices  9.94 us (12%)
  local copies, waits for them, and re-layouts  1.21 us (1%)
  between operations  0.91 us (1%)
    all_to_all x1, blocking collectives, body(): lax.all_to_all(jnp.broadcast_to(row, (devices, width)), axes, split_axis=...  14.3 us
    convert_element_type x6, other arithmetic, halves(): return (high.astype(jnp.bfloat16), (full - high).astype(jnp.bfloat16))  10.2 us
    all_to_all x1, blocking collectives, in_planes(): lax.all_to_all(solved.reshape(one_plane.shape), 'slab', split_axis=0, con...  9.35 us
    ppermute x6, starting transfers between devices, cross(): lax.ppermute(part, 'orb', [(o, o ^ n + 1) for o in range(n_orb)])  8.01 us
    ppermute x6, waiting for transfers between devices, cross(): lax.ppermute(part, 'orb', [(o, o ^ n + 1) for o in range(n_orb)])  7 us
    pallas_call x1, Pallas kernels, body(): pl.pallas_call(functools.partial(route_kernel, pair_dev, n_orb, field_bit...  6.77 us
    pallas_call x1, Pallas kernels, clear(): pl.pallas_call(clear_kernel, out_shape=[jax.ShapeDtypeStruct(orbitals.sha...  4.58 us
    pallas_call x1, Pallas kernels, in_planes(): pl.pallas_call(functools.partial(plane_place_kernel, begins), out_shape=j...  4.18 us
  transfers between devices with their start and end apart: 7, of which 4 were waited for; matrix products, arithmetic and copies ran while one was open for 14% of the time, Pallas kernels for 6%

profile of v7, /device:TPU:0, one launch (start us, length us, event | category | flops | bytes accessed | tf_op | source)
XLA Modules:
  0.0 81.5 jit_solution(10744048949121247053)
XLA Ops:
  0.0 0.0 copy-start.2
  0.0 0.0 copy-start.3
  0.0 0.0 copy-start.4
  0.0 0.8 pad_add_fusion
  0.8 14.3 %all_to_all.44 = s32[32,1,128]{2,1,0:T(1,128)S(1)} all-to-all(s32[32,1,128]{2,1,0:T(1,128)S(1)} %broadcast_in_dim.57), channel_id=1, replica_groups=mesh['slab'=8,'orb'=4] {'slab','orb'}, dimensions={0} | all-to-all | bytes 32768 | tf_op jit(solution)/shard_map/all_to_all | solution.py:709
  15.1 6.8 %route.1 = (f32[6,8,1024]{2,1,0:T(8,128)}, f32[5,8,1024]{2,1,0:T(8,128)}, f32[5,8,1024]{2,1,0:T(8,128)}, f32[3,8,1024]{2,1,0:T(8,128)S(1)}, f32[3,8,1024]{2,1,0:...) custom-call(s32[32,128]{1,0:T(8,128)S(1)} %bitcast.32, ...), custom_call_target="tpu_custom_call" | custom-call | tf_op jit(solution)/shard_map/route/pallas_call | solution.py:758
  21.9 0.6 slice.24
  23.1 0.0 copy-done.2
  23.1 0.0 copy-done.3
  23.1 0.0 copy-done.4
  23.2 58.1 %conditional.1 = (f32[64,8,4096]{2,1,0:T(8,128)}) conditional(s32[]{:T(128)} %bitcast.22, (f32[6,8,1024]{2,1,0:T(8,128)}, f32[3,8,1024]{2,1,0:T(8,128)S(1)}, f32[3,8,1024]{2,1,0:T(8,128)S(1)}, s32[24,128]{1,0:T(8,128)S(1)}, f32[8,8,1024]{2,1,0:T(8,128)S(1)}, /*index=5*/f32[384,384]{1,0:T(8,128)S(1)}, ...), branch_computations={%region_0.1_spmd, %region_1.2_spmd, %region_2.3_spmd, %region_3.4_... | conditional | flops 7726774 | bytes 15786454 | solution.py:897
  23.2 0.8 collective-permute-start.7
  24.0 2.1 %collective-permute-start.8 = (f32[4,8,1024]{2,1,0:T(8,128)}, f32[4,8,1024]{2,1,0:T(8,128)S(1)}, u32[]{:S(2)}, u32[]{:S(2)}) collective-permute-start(f32[4,8,1024]{2,1,0:T(8,128)} %get-tuple-element.82), channel_id=1, source_target_pairs={{0,3},{1,2},{2,1},{3,0},{4,7},{5,6},{6,5},{7,4},{8,11},{9,10},{10,... | collective-permute-start | bytes 393224 | tf_op jit(solution)/shard_map/cond/branch_1_fun/ppermute | solution.py:734
  26.1 0.6 collective-permute-start.6
  26.8 0.1 constant_dynamic-slice_fusion.1
  26.9 0.5 fusion.241
  27.4 0.7 and_add_fusion.1
  28.0 2.5 %fusion.60 = (bf16[1,256,512]{2,1,0:T(8,128)(2,1)S(1)}, bf16[1,256,512]{2,1,0:T(8,128)(2,1)S(1)}) fusion(s32[256]{0:T(256)S(1)} %and_add_fusion.1, s32[512]{0:T(512)S(1)} %get-tuple-element.172, pred[512]{0:T(512)(128)(4,1)S(1)} %fusion.107, s32[512]{0:T(512)S(1)} %get-tuple-element.171, s32[256]{0:T(256)S(1)} %get-tuple-element.174, s32[512]{0:T(512)S(1)} %fusion.108, ...), kind=kLoop, calls=%fused_computation.109 | loop fusion | flops 2359296 | bytes 534016 | tf_op jit(solution)/shard_map/cond/branch_1_fun/convert_element_type | solution.py:67
  30.5 2.7 %fusion.61 = (bf16[1,512,256]{2,1,0:T(8,128)(2,1)S(1)}, bf16[1,512,256]{2,1,0:T(8,128)(2,1)S(1)}) fusion(s32[256]{0:T(256)S(1)} %and_add_fusion.1, s32[512]{0:T(512)S(1)} %get-tuple-element.172, pred[512]{0:T(512)(128)(4,1)S(1)} %fusion.107, s32[512]{0:T(512)S(1)} %get-tuple-element.171, s32[256]{0:T(256)S(1)} %get-tuple-element.174, s32[512]{0:T(512)S(1)} %fusion.108, ...), kind=kLoop, calls=%fused_computation.110 | loop fusion | flops 2359296 | bytes 534016 | tf_op jit(solution)/shard_map/cond/branch_1_fun/convert_element_type | solution.py:67
  33.2 0.7 fusion.92
  33.9 0.6 fusion.99
  34.6 0.7 collective-permute-done.7.refs_2_
  35.3 0.0 collective-permute-done.8.refs_3_
  35.3 2.6 %collective-permute-done.6.refs_1_ = f32[6,8,1024]{2,1,0:T(8,128)S(1)} collective-permute-done((f32[6,8,1024]{2,1,0:T(8,128)}, f32[6,8,1024]{2,1,0:T(8,128)S(1)}, u32[]{:S(2)}, u32[]{:S(2)}) %collective-permute-start.6) | collective-permute-done | bytes 196640 | tf_op jit(solution)/shard_map/cond/branch_1_fun/ppermute | solution.py:734
  37.9 1.9 %density.4 = (f32[8,8,1024]{2,1,0:T(8,128)}, s32[1,1]{1,0:T(1,128)}) custom-call(s32[24,128]{1,0:T(8,128)S(1)} %get-tuple-element.77.work, f32[8,8,1024]{2,1,0:T(8,128)S(1)} %get-tuple-element.79.refs_0_, f32[6,8,1024]{2,1,0:T(8,128)S(1)} %collective-permute-done.6.refs_1_, f32[4,8,1024]{2,1,0:T(8,128)S(1)} %collective-permute-done.7.refs_2_, ...), custom_call_target="tpu_custom_call" | custom-call | tf_op jit(solution)/shard_map/cond/branch_1_fun/density/pallas_call | solution.py:788
  39.8 0.6 fusion.116
  40.4 3.6 %all-to-all-start.2 = ((f32[8,8,1024]{2,1,0:T(8,128)}), f32[8,8,1024]{2,1,0:T(8,128)S(1)}, u32[]{:S(2)}, u32[]{:S(2)}) async-start(f32[8,8,1024]{2,1,0:T(8,128)} %get-tuple-element.83), calls=%async_computation.2 | async-start | bytes 524288 | tf_op jit(solution)/shard_map/cond/branch_1_fun/all_to_all | solution.py:798
  44.0 1.9 %fusion.76 = (bf16[1,384,256]{2,1,0:T(8,128)(2,1)S(1)}, bf16[1,384,256]{2,1,0:T(8,128)(2,1)S(1)}) fusion(s32[256]{0:T(256)S(1)} %get-tuple-element.177, s32[384]{0:T(512)S(1)} %get-tuple-element.175, s32[256]{0:T(256)S(1)} %get-tuple-element.178, s32[384]{0:T(512)S(1)} %get-tuple-element.176), kind=kLoop, calls=%fused_computation.127 | loop fusion | flops 1474560 | bytes 398336 | tf_op jit(solution)/shard_map/cond/branch_1_fun/convert_element_type | solution.py:67
  45.9 1.8 %fusion.77 = (bf16[1,256,384]{2,1,0:T(8,128)(2,1)S(1)}, bf16[1,256,384]{2,1,0:T(8,128)(2,1)S(1)}) fusion(s32[256]{0:T(256)S(1)} %get-tuple-element.177, s32[384]{0:T(512)S(1)} %get-tuple-element.175, s32[384]{0:T(512)S(1)} %get-tuple-element.176, s32[256]{0:T(256)S(1)} %get-tuple-element.178), kind=kLoop, calls=%fused_computation.128 | loop fusion | flops 1474560 | bytes 398336 | tf_op jit(solution)/shard_map/cond/branch_1_fun/convert_element_type | solution.py:67
  47.7 2.9 %all-to-all-done.2 = f32[8,8,1024]{2,1,0:T(8,128)S(1)} async-done(((f32[8,8,1024]{2,1,0:T(8,128)}), f32[8,8,1024]{2,1,0:T(8,128)S(1)}, u32[]{:S(2)}, u32[]{:S(2)}) %all-to-all-start.2) | async-done | bytes 262176 | tf_op jit(solution)/shard_map/cond/branch_1_fun/all_to_all | solution.py:798
  50.7 2.1 %solve.5 = f32[8,1,8,1024]{3,2,1,0:T(8,128)S(1)} custom-call(f32[8,1,8,1024]{3,2,1,0:T(8,128)S(1)} %bitcast.27, bf16[1,48,32]{2,1,0:T(8,128)(2,1)S(1)} %get-tuple-element.170.refs_0_, bf16[1,48,32]{2,1,0:T(8,128)(2,1)S(1)} %get-tuple-element.169.refs_1_, bf16[1,32,48]{2,1,0:T(8,128)(2,1)S(1)} %get-tuple-element.168.refs_2_, ...), custom_call_target="tpu_custom_call" | custom-call | tf_op jit(solution)/shard_map/cond/branch_1_fun/solve/pallas_call | solution.py:800
  52.7 9.3 %all_to_all.41.potential = f32[8,8,1024]{2,1,0:T(8,128)S(1)} all-to-all(f32[8,8,1024]{2,1,0:T(8,128)S(1)} %bitcast.30), channel_id=1, replica_groups=mesh['slab'=8,'orb'=4] {'slab'}, dimensions={0} | all-to-all | bytes 524288 | tf_op jit(solution)/shard_map/cond/branch_1_fun/all_to_all | solution.py:808
  62.1 1.8 %terms.4 = (f32[8,8,1024]{2,1,0:T(8,128)S(1)}, f32[6,8,1024]{2,1,0:T(8,128)S(1)}, f32[4,8,1024]{2,1,0:T(8,128)S(1)}, f32[4,8,1024]{2,1,0:T(8,128)S(1)}, s32[1,1]{1,0:T(1,128)}) custom-call(s32[24,128]{1,0:T(8,128)S(1)} %get-tuple-element.77.work, f32[8,8,1024]{2,1,0:T(8,128)S(1)} %all_to_all.41.potential, f32[8,8,1024]{2,1,0:T(8,128)S(1)} %get-tuple-element.79.refs_0_, ...), custom_call_target="tpu_custom_call" | custom-call | tf_op jit(solution)/shard_map/cond/branch_1_fun/terms/pallas_call | solution.py:811
  63.9 0.2 collective-permute-start.9
  64.0 1.7 %collective-permute-start.10 = (f32[4,8,1024]{2,1,0:T(8,128)S(1)}, f32[4,8,1024]{2,1,0:T(8,128)S(1)}, u32[]{:S(2)}, u32[]{:S(2)}) collective-permute-start(f32[4,8,1024]{2,1,0:T(8,128)S(1)} %get-tuple-element.90), channel_id=1, source_target_pairs={{0,2},{1,3},{2,0},{3,1},{4,6},{5,7},{6,4},{7,5},{8,10},{9,11},{10,... | collective-permute-start | bytes 393224 | tf_op jit(solution)/shard_map/cond/branch_1_fun/ppermute | solution.py:734
  65.7 2.6 %collective-permute-start.11 = (f32[4,8,1024]{2,1,0:T(8,128)S(1)}, f32[4,8,1024]{2,1,0:T(8,128)S(1)}, u32[]{:S(2)}, u32[]{:S(2)}) collective-permute-start(f32[4,8,1024]{2,1,0:T(8,128)S(1)} %get-tuple-element.91), channel_id=1, source_target_pairs={{0,3},{1,2},{2,1},{3,0},{4,7},{5,6},{6,5},{7,4},{8,11},{9,10},{10,... | collective-permute-start | bytes 393224 | tf_op jit(solution)/shard_map/cond/branch_1_fun/ppermute | solution.py:734
  68.3 4.6 %clear.5 = (f32[64,8,4096]{2,1,0:T(8,128)}, s32[8,128]{1,0:T(8,128)}) custom-call(s32[1,1]{1,0:T(1,128)} %get-tuple-element.86.after), custom_call_target="tpu_custom_call" | custom-call | bytes 8388608 | tf_op jit(solution)/shard_map/cond/branch_1_fun/clear/pallas_call | solution.py:739
  72.9 3.7 %collective-permute-done.10.refs_2_ = f32[4,8,1024]{2,1,0:T(8,128)S(1)} collective-permute-done((f32[4,8,1024]{2,1,0:T(8,128)S(1)}, f32[4,8,1024]{2,1,0:T(8,128)S(1)}, u32[]{:S(2)}, u32[]{:S(2)}) %collective-permute-start.10) | collective-permute-done | bytes 131104 | tf_op jit(solution)/shard_map/cond/branch_1_fun/ppermute | solution.py:734
  76.6 0.0 collective-permute-done.11.refs_3_
  76.6 0.0 collective-permute-done.9.refs_1_
  76.6 4.2 %place.5 = f32[64,8,4096]{2,1,0:T(8,128)} custom-call(s32[24,128]{1,0:T(8,128)S(1)} %get-tuple-element.77.work, f32[64,8,4096]{2,1,0:T(8,128)} %get-tuple-element.78.orbitals, f32[64,8,4096]{2,1,0:T(8,128)} %get-tuple-element.87.zeros, f32[8,8,1024]{2,1,0:T(8,128)S(1)} %get-tuple-element.88.refs_0_, ...), custom_call_target="tpu_custom_call", output_to_operand_aliasing={{}: (2, {})} | custom-call | tf_op jit(solution)/shard_map/cond/branch_1_fun/place/pallas_call | solution.py:822
  (8 shorter events, 0.0 us)
Async XLA Ops:
  0.0 23.1 %copy-start.2 = (f32[384,384]{1,0:T(8,128)S(1)}, f32[384,384]{1,0:T(8,128)}, u32[]{:S(2)}) copy-start(f32[384,384]{1,0:T(8,128)} %constant.371.clone) | copy-start | bytes 1769476
  0.0 23.1 %copy-start.3 = (s32[1,3]{1,0:T(1,128)S(1)}, s32[1,3]{1,0:T(1,128)}, u32[]{:S(2)}) copy-start(s32[1,3]{1,0:T(1,128)} %param.14) | copy-start | bytes 40
  0.0 23.1 %copy-start.4 = (s32[1,2]{1,0:T(1,128)S(1)}, s32[1,2]{1,0:T(1,128)}, u32[]{:S(2)}) copy-start(s32[1,2]{1,0:T(1,128)} %param.13) | copy-start | bytes 28
  23.2 12.1 %collective-permute-start.7 = (f32[4,8,1024]{2,1,0:T(8,128)S(1)}, f32[4,8,1024]{2,1,0:T(8,128)S(1)}, u32[]{:S(2)}, u32[]{:S(2)}) collective-permute-start(f32[4,8,1024]{2,1,0:T(8,128)S(1)} %get-tuple-element.81), channel_id=1, source_target_pairs={{0,2},{1,3},{2,0},{3,1},{4,6},{5,7},{6,4},{7,5},{8,10},{9,11},{10,... | collective-permute-start | bytes 393224 | tf_op jit(solution)/shard_map/cond/branch_1_fun/ppermute | solution.py:734
  24.0 11.3 %collective-permute-start.8 = (f32[4,8,1024]{2,1,0:T(8,128)}, f32[4,8,1024]{2,1,0:T(8,128)S(1)}, u32[]{:S(2)}, u32[]{:S(2)}) collective-permute-start(f32[4,8,1024]{2,1,0:T(8,128)} %get-tuple-element.82), channel_id=1, source_target_pairs={{0,3},{1,2},{2,1},{3,0},{4,7},{5,6},{6,5},{7,4},{8,11},{9,10},{10,... | collective-permute-start | bytes 393224 | tf_op jit(solution)/shard_map/cond/branch_1_fun/ppermute | solution.py:734
  26.1 11.8 %collective-permute-start.6 = (f32[6,8,1024]{2,1,0:T(8,128)}, f32[6,8,1024]{2,1,0:T(8,128)S(1)}, u32[]{:S(2)}, u32[]{:S(2)}) collective-permute-start(f32[6,8,1024]{2,1,0:T(8,128)} %get-tuple-element.80), channel_id=1, source_target_pairs={{0,1},{1,0},{2,3},{3,2},{4,5},{5,4},{6,7},{7,6},{8,9},{9,8},{10,11... | collective-permute-start | bytes 589832 | tf_op jit(solution)/shard_map/cond/branch_1_fun/ppermute | solution.py:734
  40.4 10.3 %all-to-all-start.2 = ((f32[8,8,1024]{2,1,0:T(8,128)}), f32[8,8,1024]{2,1,0:T(8,128)S(1)}, u32[]{:S(2)}, u32[]{:S(2)}) async-start(f32[8,8,1024]{2,1,0:T(8,128)} %get-tuple-element.83), calls=%async_computation.2 | async-start | bytes 524288 | tf_op jit(solution)/shard_map/cond/branch_1_fun/all_to_all | solution.py:798
  63.9 12.7 %collective-permute-start.9 = (f32[6,8,1024]{2,1,0:T(8,128)S(1)}, f32[6,8,1024]{2,1,0:T(8,128)S(1)}, u32[]{:S(2)}, u32[]{:S(2)}) collective-permute-start(f32[6,8,1024]{2,1,0:T(8,128)S(1)} %get-tuple-element.89), channel_id=1, source_target_pairs={{0,1},{1,0},{2,3},{3,2},{4,5},{5,4},{6,7},{7,6},{8,9},{9,8},{10,11... | collective-permute-start | bytes 589832 | tf_op jit(solution)/shard_map/cond/branch_1_fun/ppermute | solution.py:734
  64.0 12.5 %collective-permute-start.10 = (f32[4,8,1024]{2,1,0:T(8,128)S(1)}, f32[4,8,1024]{2,1,0:T(8,128)S(1)}, u32[]{:S(2)}, u32[]{:S(2)}) collective-permute-start(f32[4,8,1024]{2,1,0:T(8,128)S(1)} %get-tuple-element.90), channel_id=1, source_target_pairs={{0,2},{1,3},{2,0},{3,1},{4,6},{5,7},{6,4},{7,5},{8,10},{9,11},{10,... | collective-permute-start | bytes 393224 | tf_op jit(solution)/shard_map/cond/branch_1_fun/ppermute | solution.py:734
  65.7 10.9 %collective-permute-start.11 = (f32[4,8,1024]{2,1,0:T(8,128)S(1)}, f32[4,8,1024]{2,1,0:T(8,128)S(1)}, u32[]{:S(2)}, u32[]{:S(2)}) collective-permute-start(f32[4,8,1024]{2,1,0:T(8,128)S(1)} %get-tuple-element.91), channel_id=1, source_target_pairs={{0,3},{1,2},{2,1},{3,0},{4,7},{5,6},{6,5},{7,4},{8,11},{9,10},{10,... | collective-permute-start | bytes 393224 | tf_op jit(solution)/shard_map/cond/branch_1_fun/ppermute | solution.py:734
